TPU v7x, 256 devices: a whole 4x4x8 slice. The times are simulated.
256 devices in a mesh: dp: 16 (over x, y_hi, core), tensor: 16 (over y_lo, z).
Axes of the slice: x: 4, y: 4 (y_hi: 2, y_lo: 2; y = y_hi * 2 + y_lo), z: 8, core: 2. Of those that a mesh axis runs over, the one named last changes fastest.
Arguments:
- tokens: bfloat16 [4096, 4096], P(('dp', 'tensor')), may hold values from -6 to 6
- weight_tiles: bfloat16 [16, 128, 2, 128, 128], P('tensor', 'dp'), may hold values from -0.125 to 0.125
- keep_mask: int32 [2, 32, 112], P(None, None, 'tensor'), may hold values from 0 to 1, as said below
- cotangent: bfloat16 [4096, 14336], P('dp', 'tensor'), may hold values from -6 to 6
Outputs:
- hidden: bfloat16 [4096, 14336], P('dp', 'tensor')
- grad_tokens: bfloat16 [4096, 4096], P(('dp', 'tensor'))
- tile_grads: float32 [16, 128, 2, 128, 128], P('tensor', 'dp')
Inputs may be any that keep to these rules, and one draw needn't show every extreme that they name: keep_mask[m, r, t * 7 + c] is 1 where tile (r, c) of tensor shard t's grid is kept in matrix m; each shard's grid of each matrix keeps 64 to 128 tiles, and some shard exactly 128.
All inputs are finite; a program needn't handle non-finite values.
Results may differ from a plain program's by a relative error of at most 0.0049.
Values may be sent and summed in bfloat16 or wider, within the bound.
No kernel may reach another device: no remote copies, remote signals or barrier semaphores. Data moves between devices by JAX's collectives and lax.ppermute only.
A program may use at most 128 MiB of HBM per device.

v0:
```python
import jax
import jax.numpy as jnp
from jax import lax
from jax.sharding import PartitionSpec as P


def slot_tables(keep_local, slot_total):
    matrix_count, rows_blocks, cols_blocks = keep_local.shape
    grid_size = rows_blocks * cols_blocks
    flat_keep = keep_local.reshape(matrix_count, grid_size)
    slot_order = jnp.cumsum(flat_keep, axis=1) - 1
    slot_ids = jnp.arange(slot_total, dtype=jnp.int32)
    matches = jnp.logical_and(
        slot_order[:, None, :] == slot_ids[None, :, None], flat_keep[:, None, :] == 1
    ).astype(jnp.int32)
    places = jnp.arange(grid_size, dtype=jnp.int32)
    row_index = jnp.sum(matches * (places // cols_blocks)[None, None, :], axis=2)
    col_index = jnp.sum(matches * (places % cols_blocks)[None, None, :], axis=2)
    live_slot = jnp.sum(matches, axis=2)
    return (row_index, col_index, live_slot)


def run_groups(group_step, running, weights, first_table, second_table, group_size):
    slot_span = weights.shape[0]

    def one_turn(turn_index, partial_sum):
        offset = turn_index * group_size
        return group_step(
            partial_sum,
            lax.dynamic_slice_in_dim(weights, offset, group_size, 0),
            lax.dynamic_slice_in_dim(first_table, offset, group_size, first_table.ndim - 1),
            lax.dynamic_slice_in_dim(second_table, offset, group_size, second_table.ndim - 1),
        )

    return lax.fori_loop(0, slot_span // group_size, one_turn, running)


def body(tokens, weight_tiles, keep_mask, cotangent):
    tile_size = weight_tiles.shape[3]
    slot_local = weight_tiles.shape[1]
    slot_total = slot_local * lax.axis_size("dp")
    rows_blocks = tokens.shape[1] // tile_size
    cols_blocks = keep_mask.shape[2]
    row_index, col_index, live_slot = slot_tables(keep_mask, slot_total)
    col_live = jnp.stack([col_index, live_slot], axis=1)
    row_live = jnp.stack([row_index, live_slot], axis=1)
    gathered = lax.all_gather(tokens, "tensor", axis=0, tiled=True)
    group_rows = gathered.shape[0]
    token_blocks = gathered.reshape(group_rows, rows_blocks, tile_size)

    def forward_group(running, tile_group, row_group, place_group):
        column_sums = []
        for matrix_id in range(2):
            picked = jnp.take(token_blocks, row_group[matrix_id], axis=1)
            product = jnp.einsum(
                "tgb,gbc->tgc", picked, tile_group[:, matrix_id], preferred_element_type=jnp.float32
            )
            product = product * place_group[matrix_id, 1].astype(jnp.float32)[None, :, None]
            column_sums.append(running[matrix_id].at[:, place_group[matrix_id, 0]].add(product))
        return jnp.stack(column_sums)

    initial = jnp.zeros((2, group_rows, cols_blocks, tile_size), jnp.float32)
    whole_tiles = lax.all_gather(weight_tiles, "dp", axis=1, tiled=True)
    rows_part = row_index
    place_part = col_live
    folded = run_groups(forward_group, initial, whole_tiles[0], rows_part, place_part, slot_local)
    gate_sum = folded[0].reshape(group_rows, cols_blocks * tile_size)
    upward = folded[1].reshape(group_rows, cols_blocks * tile_size)
    sigma = jax.nn.sigmoid(gate_sum)
    hidden = (gate_sum * sigma * upward).astype(jnp.bfloat16)
    grad_out = cotangent.astype(jnp.float32)
    grad_up = (grad_out * gate_sum * sigma).astype(jnp.bfloat16)
    grad_gate = (grad_out * upward * sigma * (1.0 + gate_sum * (1.0 - sigma))).astype(jnp.bfloat16)
    grad_blocks = jnp.stack([grad_gate, grad_up]).reshape(2, group_rows, cols_blocks, tile_size)

    def backward_group(running, tile_group, col_group, place_group):
        for matrix_id in range(2):
            picked = jnp.take(grad_blocks[matrix_id], col_group[matrix_id], axis=1)
            product = jnp.einsum(
                "tgc,gbc->tgb", picked, tile_group[:, matrix_id], preferred_element_type=jnp.float32
            )
            product = product * place_group[matrix_id, 1].astype(jnp.float32)[None, :, None]
            running = running.at[:, place_group[matrix_id, 0]].add(product)
        return running

    zero_rows = jnp.zeros((group_rows, rows_blocks, tile_size), jnp.float32)
    cols_part = col_index
    place_part = row_live
    partial_rows = run_groups(
        backward_group, zero_rows, whole_tiles[0], cols_part, place_part, slot_local
    )
    summed = lax.psum_scatter(
        partial_rows.reshape(group_rows, rows_blocks * tile_size),
        "tensor",
        scatter_dimension=0,
        tiled=True,
    )
    grad_tokens = summed.astype(jnp.bfloat16)
    rows_part = row_index
    cols_part = col_index
    live_part = live_slot.astype(jnp.float32)
    tile_terms = []
    for matrix_id in range(2):
        token_part = jnp.take(token_blocks, rows_part[matrix_id], axis=1)
        grad_part = jnp.take(grad_blocks[matrix_id], cols_part[matrix_id], axis=1)
        product = jnp.einsum(
            "tgb,tgc->gbc", token_part, grad_part, preferred_element_type=jnp.float32
        )
        tile_terms.append(product * live_part[matrix_id][:, None, None])
    summed = lax.psum_scatter(jnp.stack(tile_terms, axis=1), "dp", scatter_dimension=0, tiled=True)
    tile_grads = (summed * (1.0 / lax.axis_size("dp")))[None]
    return (hidden, grad_tokens, tile_grads)


def solution(mesh):
    in_specs = (
        P(("dp", "tensor"), None),
        P("tensor", "dp", None, None, None),
        P(None, None, "tensor"),
        P("dp", "tensor"),
    )
    out_specs = (P("dp", "tensor"), P(("dp", "tensor"), None), P("tensor", "dp", None, None, None))
    return jax.shard_map(body, mesh=mesh, in_specs=in_specs, out_specs=out_specs, check_vma=False)
```

profile of v0, /device:TPU:6, one launch (start us, length us, event | category | flops | bytes accessed | tf_op | source)
XLA Modules:
  0.0 1122.6 jit_solution(16056163825795791614)
XLA Ops:
  16.1 68.2 %all-gather.5.cloned.1.call-done = bf16[256,4096]{1,0:T(8,128)(2,1)} async-done(((bf16[16,4096]{1,0:T(8,128)(2,1)}), bf16[256,4096]{1,0:T(8,128)(2,1)}) %all-gather.5.cloned.1.call-update) | async-done | bytes 2097168 | tf_op jit(solution)/shard_map/all_gather | solution.py:47
  84.3 4.1 copy.99
  91.6 69.2 %all-gather.3.cloned.1.call-done = bf16[1,128,2,128,128]{4,3,1,2,0:T(8,128)(2,1)} async-done(((bf16[1,8,2,128,128]{4,3,1,2,0:T(8,128)(2,1)}), bf16[1,128,2,128,128]{4,3,1,2,0:T(8,128)(2,1)}) %all-gather.3.cloned.1.call-update) | async-done | bytes 8388624 | tf_op jit(solution)/shard_map/all_gather | solution.py:63
  162.3 401.0 %while.26 = (s32[]{:T(128)}, f32[2,256,7,128]{3,1,2,0:T(8,128)}, s32[2,2,128]{2,0,1:T(2,128)S(1)}, bf16[128,2,128,128]{3,2,0,1:T(8,128)(2,1)}, s32[2,128]{1,0:T(...) while((s32[]{:T(128)}, f32[2,256,7,128]{3,1,2,0:T(8,128)}, ...), condition=%wide.region_8.10_spmd, body=%wide.region_5.9_spmd.sunk | while | flops 136251552 | bytes 23603804 | solution.py:35
  172.9 3.7 scatter_fusion
  197.8 3.7 scatter_fusion
  222.8 3.7 scatter_fusion
  247.8 3.7 scatter_fusion
  272.7 3.7 scatter_fusion
  297.7 3.7 scatter_fusion
  322.7 3.8 scatter_fusion
  347.7 3.8 scatter_fusion
  372.7 3.8 scatter_fusion
  397.7 3.7 scatter_fusion
  422.6 4.0 scatter_fusion
  447.8 4.0 scatter_fusion
  473.0 4.0 scatter_fusion
  498.2 4.0 scatter_fusion
  523.4 4.0 scatter_fusion
  548.6 4.0 scatter_fusion
  574.7 301.2 %while.27 = (s32[]{:T(128)}, f32[256,32,128]{2,0,1:T(8,128)}, s32[2,2,128]{2,0,1:T(2,128)S(1)}, bf16[128,2,128,128]{3,2,0,1:T(8,128)(2,1)}, bf16[2,256,7,128]{3,...) while((s32[]{:T(128)}, f32[256,32,128]{2,0,1:T(8,128)}, ...), condition=%wide.region_12.15_spmd, body=%wide.region_9.14_spmd.sunk | while | flops 135792800 | bytes 18097136 | solution.py:35
  600.0 3.6 scatter_fusion.2
  618.9 3.6 scatter_fusion.2
  656.4 3.6 scatter_fusion.2
  702.8 3.6 scatter_fusion.3
  769.1 3.6 scatter_fusion.2
  777.9 3.6 scatter_fusion.3
  788.0 3.6 scatter_fusion.2
  796.8 3.6 scatter_fusion.3
  806.9 3.6 scatter_fusion.2
  815.7 3.6 scatter_fusion.3
  825.7 3.6 scatter_fusion.2
  834.5 3.6 scatter_fusion.3
  844.6 3.6 scatter_fusion.2
  853.4 3.6 scatter_fusion.3
  863.5 3.6 scatter_fusion.2
  872.3 3.6 scatter_fusion.3
  875.9 4.6 copy_bitcast_fusion.1
  881.6 6.6 gather_fusion.6
  888.2 6.6 gather_fusion.4
  895.3 6.6 gather_fusion.7
  901.9 6.6 gather_fusion.5
  908.4 12.6 %multiply_bitcast_fusion = f32[128,1,128,128]{3,2,0,1:T(8,128)} fusion(f32[128]{0:T(128)S(1)} %get-tuple-element.375, bf16[128,256,128]{2,1,0:T(8,128)(2,1)} %gather_fusion.7, pred[128]{0:T(512)(128)(4,1)S(1)} %get-tuple-element.372, bf16[128,256,128]{2,1,0:T(8,128)(2,1)} %gather_fusion.6, pred[128]{0:T(512)(128)(4,1)S(1)} %get-tuple-element.378), kind=kOutput, calls=%fused_computation.109 | convolution fusion | flops 1084227584 | bytes 25166592 | tf_op jit(solution)/shard_map/tgb,tgc->gbc/dot_general | solution.py:106
  921.0 12.6 %multiply_bitcast_fusion.1 = f32[128,1,128,128]{3,2,0,1:T(8,128)} fusion(f32[128]{0:T(128)S(1)} %get-tuple-element.374, bf16[128,256,128]{2,1,0:T(8,128)(2,1)} %gather_fusion.5, pred[128]{0:T(512)(128)(4,1)S(1)} %get-tuple-element.339, bf16[128,256,128]{2,1,0:T(8,128)(2,1)} %gather_fusion.4, pred[128]{0:T(512)(128)(4,1)S(1)} %get-tuple-element.380), kind=kOutput, calls=%fused_computation.110 | convolution fusion | flops 1084227584 | bytes 25166592 | tf_op jit(solution)/shard_map/tgb,tgc->gbc/dot_general | solution.py:106
  933.6 6.6 pad_maximum_fusion.1
  941.8 11.7 %copy.144 = f32[16,8,256,128]{3,1,2,0:T(8,128)} copy(f32[16,8,256,128]{3,2,1,0:T(8,128)S(1)} %bitcast.280) | data formatting | bytes 33554432
  955.6 4.3 reduce-scatter.6.cloned.1.call-done
  961.5 152.0 %reduce-scatter.8.cloned.1.call-done = f32[8,32768]{1,0:T(8,128)} async-done(((f32[128,32768]{1,0:T(8,128)}), f32[8,32768]{1,0:T(8,128)}) %reduce-scatter.8.cloned.1.call-update) | async-done | bytes 1048592
  (530 shorter events, 616.8 us)
Async XLA Ops:
  7.2 77.1 %all-gather.5.cloned.1.call-start = ((), (), s32[]{:S(2)}) async-start(), calls=%async_computation.3 | async-start | bytes 2228224 | tf_op jit(solution)/shard_map/all_gather | solution.py:47
  7.9 152.9 %all-gather.3.cloned.1.call-start = ((), (), s32[]{:S(2)}) async-start(), calls=%async_computation.2 | async-start | bytes 8912896 | tf_op jit(solution)/shard_map/all_gather | solution.py:63
  9.9 950.1 %reduce-scatter.6.cloned.1.call-start = ((), (), s32[]{:S(2)}) async-start(), calls=%async_computation.4 | async-start | bytes 4456448 | tf_op jit(solution)/shard_map/reduce_scatter | solution.py:92
  14.8 0.5 copy-start.5
  14.8 0.6 copy-start.8
  170.3 11.9 %copy-start.7 = (s32[8]{0:T(128)S(1)}, s32[8]{0:T(128)}, u32[]{:S(2)}) copy-start(s32[8]{0:T(128)} %get-tuple-element.482) | copy-start | bytes 100 | tf_op jit(solution)/shard_map/while
  195.2 11.9 %copy-start.7 = (s32[8]{0:T(128)S(1)}, s32[8]{0:T(128)}, u32[]{:S(2)}) copy-start(s32[8]{0:T(128)} %get-tuple-element.482) | copy-start | bytes 100 | tf_op jit(solution)/shard_map/while
  220.2 11.9 %copy-start.7 = (s32[8]{0:T(128)S(1)}, s32[8]{0:T(128)}, u32[]{:S(2)}) copy-start(s32[8]{0:T(128)} %get-tuple-element.482) | copy-start | bytes 100 | tf_op jit(solution)/shard_map/while
  245.2 11.9 %copy-start.7 = (s32[8]{0:T(128)S(1)}, s32[8]{0:T(128)}, u32[]{:S(2)}) copy-start(s32[8]{0:T(128)} %get-tuple-element.482) | copy-start | bytes 100 | tf_op jit(solution)/shard_map/while
  270.1 11.9 %copy-start.7 = (s32[8]{0:T(128)S(1)}, s32[8]{0:T(128)}, u32[]{:S(2)}) copy-start(s32[8]{0:T(128)} %get-tuple-element.482) | copy-start | bytes 100 | tf_op jit(solution)/shard_map/while
  295.1 11.9 %copy-start.7 = (s32[8]{0:T(128)S(1)}, s32[8]{0:T(128)}, u32[]{:S(2)}) copy-start(s32[8]{0:T(128)} %get-tuple-element.482) | copy-start | bytes 100 | tf_op jit(solution)/shard_map/while
  320.1 11.9 %copy-start.7 = (s32[8]{0:T(128)S(1)}, s32[8]{0:T(128)}, u32[]{:S(2)}) copy-start(s32[8]{0:T(128)} %get-tuple-element.482) | copy-start | bytes 100 | tf_op jit(solution)/shard_map/while
  345.1 11.9 %copy-start.7 = (s32[8]{0:T(128)S(1)}, s32[8]{0:T(128)}, u32[]{:S(2)}) copy-start(s32[8]{0:T(128)} %get-tuple-element.482) | copy-start | bytes 100 | tf_op jit(solution)/shard_map/while
  370.1 12.0 %copy-start.7 = (s32[8]{0:T(128)S(1)}, s32[8]{0:T(128)}, u32[]{:S(2)}) copy-start(s32[8]{0:T(128)} %get-tuple-element.482) | copy-start | bytes 100 | tf_op jit(solution)/shard_map/while
  395.1 11.9 %copy-start.7 = (s32[8]{0:T(128)S(1)}, s32[8]{0:T(128)}, u32[]{:S(2)}) copy-start(s32[8]{0:T(128)} %get-tuple-element.482) | copy-start | bytes 100 | tf_op jit(solution)/shard_map/while
  420.0 12.2 %copy-start.7 = (s32[8]{0:T(128)S(1)}, s32[8]{0:T(128)}, u32[]{:S(2)}) copy-start(s32[8]{0:T(128)} %get-tuple-element.482) | copy-start | bytes 100 | tf_op jit(solution)/shard_map/while
  445.2 12.2 %copy-start.7 = (s32[8]{0:T(128)S(1)}, s32[8]{0:T(128)}, u32[]{:S(2)}) copy-start(s32[8]{0:T(128)} %get-tuple-element.482) | copy-start | bytes 100 | tf_op jit(solution)/shard_map/while
  470.4 12.2 %copy-start.7 = (s32[8]{0:T(128)S(1)}, s32[8]{0:T(128)}, u32[]{:S(2)}) copy-start(s32[8]{0:T(128)} %get-tuple-element.482) | copy-start | bytes 100 | tf_op jit(solution)/shard_map/while
  495.6 12.2 %copy-start.7 = (s32[8]{0:T(128)S(1)}, s32[8]{0:T(128)}, u32[]{:S(2)}) copy-start(s32[8]{0:T(128)} %get-tuple-element.482) | copy-start | bytes 100 | tf_op jit(solution)/shard_map/while
  520.8 12.2 %copy-start.7 = (s32[8]{0:T(128)S(1)}, s32[8]{0:T(128)}, u32[]{:S(2)}) copy-start(s32[8]{0:T(128)} %get-tuple-element.482) | copy-start | bytes 100 | tf_op jit(solution)/shard_map/while
  546.0 12.2 %copy-start.7 = (s32[8]{0:T(128)S(1)}, s32[8]{0:T(128)}, u32[]{:S(2)}) copy-start(s32[8]{0:T(128)} %get-tuple-element.482) | copy-start | bytes 100 | tf_op jit(solution)/shard_map/while
  566.0 8.7 copy-start.6
  569.9 0.8 copy-start
  569.9 0.9 copy-start.2
  875.9 4.9 copy-start.9
  880.5 233.0 %reduce-scatter.8.cloned.1.call-start = ((), (), s32[]{:S(2)}) async-start(), calls=%async_computation.5 | async-start | bytes 17825792
  888.2 6.6 copy-start.3
  888.2 6.8 copy-start.1
  953.6 1.0 copy-start.4
Sparse Core Ops, SparseCore 0:
  9.8 74.4 all-gather.4
  87.6 73.1 all-gather.2
  880.6 79.2 reduce-scatter.5
  964.4 149.0 reduce-scatter.7
where the time goes:
time: 1130 us; the launch traced here: 1120 us
  local copies, waits for them, and re-layouts  365 us (32%)
  other arithmetic  301 us (27%)
  waiting for transfers between devices  294 us (26%)
  matrix products  147 us (13%)
  between operations  13.9 us (1%)
    unnamed x5, waiting for transfers between devices  153 us
    scatter-add x32, other arithmetic, backward_group(): running = running.at[:, place_group[matrix_id, 0]].add(product)  114 us
    scatter-add x32, other arithmetic, forward_group(): running[matrix_id].at[:, place_group[matrix_id, 0]].add(product)  101 us
    mul x32, local copies, waits for them, and re-layouts, forward_group(): product * place_group[matrix_id, 1].astype(jnp.float32)[None, :, None]  83.3 us
    dot_general x32, matrix products, forward_group(): jnp.einsum('tgb,gbc->tgc', picked, tile_group[:, matrix_id], preferred_el...  74 us
    all_gather x1, waiting for transfers between devices, body(): whole_tiles = lax.all_gather(weight_tiles, 'dp', axis=1, tiled=True)  69.2 us
    all_gather x1, waiting for transfers between devices, body(): gathered = lax.all_gather(tokens, 'tensor', axis=0, tiled=True)  68.2 us
    gather x32, local copies, waits for them, and re-layouts, backward_group(): picked = jnp.take(grad_blocks[matrix_id], col_group[matrix_id], axis=1)  61.3 us
  transfers between devices with their start and end apart: 4, of which 4 were waited for; matrix products, arithmetic and copies ran while one was open for 8% of the time, Pallas kernels for 0%

commit v1 on v0

v1 whole, which is shorter than its diff:
```python
import functools

import jax
import jax.numpy as jnp
from jax import lax
from jax.experimental import pallas as pl
from jax.experimental.pallas import tpu as pltpu
from jax.sharding import PartitionSpec as P

TILE = 128
ROWS = 32
COLS = 7
CAP = 128
PER = 8
GROUP = 256
WIDTH = ROWS * TILE
HIDE = COLS * TILE
DEAD = ROWS * COLS
XS, YS, CS = 4, 2, 2
ZS, YL = 8, 2


def dp_perm(move):
    def index(x, y, c):
        return (x * YS + y) * CS + c

    return [
        (index(x, y, c), index(*move(x, y, c)))
        for x in range(XS)
        for y in range(YS)
        for c in range(CS)
    ]


X_UP = dp_perm(lambda x, y, c: ((x + 1) % XS, y, c))
X_DOWN = dp_perm(lambda x, y, c: ((x - 1) % XS, y, c))
Y_SWAP = dp_perm(lambda x, y, c: (x, 1 - y, c))
C_SWAP = dp_perm(lambda x, y, c: (x, y, 1 - c))
L_SWAP = [(l * ZS + z, (1 - l) * ZS + z) for l in range(YL) for z in range(ZS)]
Z_RINGS = [[l * ZS + z for z in range(ZS)] for l in range(YL)]

BLOCKS = {(1, 1): 0, (3, 1): 1, (2, 1): 2, (0, 1): 3, (2, 0): 4, (1, 0): 5, (3, 0): 6, (0, 0): 7}


def kernel(
    place, target, ranks,
    piece_a, piece_b, piece_c, piece_d, piece_e, piece_f,
    gathered, cotangent,
    hidden, send_out, keep_out, rows_out,
    weight, tokens, turned, grads, tiles, sems,
):
    weight[...] = jnp.zeros_like(weight)
    tiles[...] = jnp.zeros_like(tiles)

    first = 0
    for piece in (piece_a, piece_b, piece_c, piece_d, piece_e, piece_f):
        count = piece.shape[0]

        def put(index, unused, piece=piece, first=first):
            slot = ranks[first + index // PER] * PER + index % PER
            for m in range(2):
                weight[place[m, slot], :, m * TILE:(m + 1) * TILE] = piece[index, m]
            return unused

        lax.fori_loop(0, count, put, 0, unroll=4)
        first += count // PER

    for z in range(ZS):
        for l in range(YL):
            tokens[l * 128 + z * 16:l * 128 + z * 16 + 16, :] = gathered[z, l]
    for r in range(0, WIDTH, 512):
        turned[r:r + 512, :] = tokens[:, r:r + 512].T

    def forward(c, unused):
        dense = weight[pl.ds(c * ROWS, ROWS)].reshape(WIDTH, 2 * TILE)
        total = jnp.dot(tokens[...], dense, preferred_element_type=jnp.float32)
        gate, up = total[:, :TILE], total[:, TILE:]
        lanes = pl.ds(pl.multiple_of(c * TILE, TILE), TILE)
        sigma = 1.0 / (1.0 + jnp.exp(-gate))
        swish = gate * sigma
        hidden[:, lanes] = (swish * up).astype(jnp.bfloat16)
        out_grad = cotangent[:, lanes].astype(jnp.float32)
        grads[c, :, TILE:] = (out_grad * swish).astype(jnp.bfloat16)
        grads[c, :, :TILE] = (
            out_grad * up * sigma * (1.0 + gate * (1.0 - sigma))
        ).astype(jnp.bfloat16)
        return unused

    lax.fori_loop(0, COLS, forward, 0)

    span = 512

    def tile_sums(step, unused):
        c = step // (WIDTH // span)
        part = step % (WIDTH // span)
        rows = pl.ds(pl.multiple_of(part * span, span), span)
        total = jnp.dot(turned[rows, :], grads[c], preferred_element_type=jnp.float32)
        total = total.astype(jnp.bfloat16)
        for i in range(span // TILE):
            for m in range(2):
                spot = target[m, (part * (span // TILE) + i) * COLS + c]
                tiles[spot, m] = total[i * TILE:(i + 1) * TILE, m * TILE:(m + 1) * TILE]
        return unused

    lax.fori_loop(0, COLS * (WIDTH // span), tile_sums, 0)
    half = CAP // 2
    first_copy = pltpu.make_async_copy(tiles.at[pl.ds(0, half)], send_out, sems.at[0])
    first_copy.start()
    second_copy = pltpu.make_async_copy(tiles.at[pl.ds(half, half)], keep_out, sems.at[1])
    second_copy.start()

    def row_sums(part, unused):
        total = jnp.zeros((GROUP, 2 * TILE), jnp.float32)
        for c in range(COLS):
            dense = weight[pl.ds(c * ROWS + part * 2, 2)].reshape(2 * TILE, 2 * TILE)
            total += lax.dot_general(
                grads[c], dense, (((1,), (1,)), ((), ())), preferred_element_type=jnp.float32
            )
        total = total.astype(jnp.bfloat16)
        lanes = pl.ds(pl.multiple_of(part * 256, 256), 256)
        for z in range(ZS):
            for l in range(YL):
                rows_out[z, l, :, lanes] = total[l * 128 + z * 16:l * 128 + z * 16 + 16]
        return unused

    lax.fori_loop(0, WIDTH // 256, row_sums, 0)
    first_copy.wait()
    second_copy.wait()


def local_work(place, target, ranks, pieces, gathered, cotangent):
    smem = pl.BlockSpec(memory_space=pltpu.SMEM)
    vmem = pl.BlockSpec(memory_space=pltpu.VMEM)
    hbm = pl.BlockSpec(memory_space=pl.ANY)
    bf16 = jnp.bfloat16
    return pl.pallas_call(
        kernel,
        out_shape=(
            jax.ShapeDtypeStruct((GROUP, HIDE), bf16),
            jax.ShapeDtypeStruct((CAP // 2, 2, TILE, TILE), bf16),
            jax.ShapeDtypeStruct((CAP // 2, 2, TILE, TILE), bf16),
            jax.ShapeDtypeStruct((ZS, YL, 16, WIDTH), bf16),
        ),
        in_specs=[smem] * 3 + [vmem] * 8,
        out_specs=(vmem, hbm, hbm, vmem),
        scratch_shapes=[
            pltpu.VMEM((DEAD + 1, TILE, 2 * TILE), bf16),
            pltpu.VMEM((GROUP, WIDTH), bf16),
            pltpu.VMEM((WIDTH, GROUP), bf16),
            pltpu.VMEM((COLS, GROUP, 2 * TILE), bf16),
            pltpu.VMEM((CAP + 1, 2, TILE, TILE), bf16),
            pltpu.SemaphoreType.DMA((2,)),
        ],
        compiler_params=pltpu.CompilerParams(vmem_limit_bytes=58 * 1024 * 1024),
        cost_estimate=pl.CostEstimate(
            flops=6 * GROUP * WIDTH * 2 * HIDE, bytes_accessed=24 << 20, transcendentals=GROUP * HIDE
        ),
        name="swiglu_local",
    )(place, target, ranks, *pieces, gathered, cotangent)


def tables(keep_local, x, y, c):
    keep = keep_local.reshape(2, ROWS * COLS)
    spots = jnp.arange(ROWS * COLS, dtype=jnp.int32)
    order = jnp.sum(jnp.where(spots[None, :] <= spots[:, None], keep[:, None, :], 0), axis=2) - 1
    dense_spot = (spots % COLS) * ROWS + spots // COLS
    slots = jnp.arange(CAP, dtype=jnp.int32)
    match = (order[:, None, :] == slots[None, :, None]) & (keep[:, None, :] == 1)
    place = DEAD + jnp.sum(jnp.where(match, dense_spot - DEAD, 0), axis=2)
    owner = order // PER
    dx = (owner // (YS * CS) - x) % XS
    dy = (owner // CS) % YS ^ y
    dc = owner % CS ^ c
    block = jnp.zeros_like(owner)
    for (a, b), at in BLOCKS.items():
        block = jnp.where((dx == a) & (dy == b), at, block)
    target = ((1 - dc) * len(BLOCKS) + block) * PER + order % PER
    target = jnp.where(keep == 1, target, CAP)
    return place.astype(jnp.int32), target.astype(jnp.int32)


def piece_ranks(x, y, c):
    spots = [(0, 0), (-1, 0), (1, 0), (0, 1), (2, 0), (-1, 1), (1, 1), (2, 1)]
    ranks = [
        (((x + dx) % XS) * YS + (y ^ dy)) * CS + (c ^ dc) for dc in range(2) for dx, dy in spots
    ]
    return jnp.stack(ranks).astype(jnp.int32)


def body(tokens, weight_tiles, keep_mask, cotangent):
    f32, bf16 = jnp.float32, jnp.bfloat16
    rank = lax.axis_index("dp")
    x, y, c = rank // (YS * CS), (rank // CS) % YS, rank % CS
    low = lax.axis_index("tensor") // ZS
    place, target = tables(keep_mask, x, y, c)
    ranks = piece_ranks(x, y, c)

    other = lax.ppermute(tokens, "tensor", L_SWAP)
    pair = jnp.where(low == 0, jnp.stack([tokens, other]), jnp.stack([other, tokens]))
    gathered = lax.all_gather(pair, "tensor", axis=0, axis_index_groups=Z_RINGS)

    own = weight_tiles[0]
    below = lax.ppermute(own, "dp", X_UP)
    above = lax.ppermute(own, "dp", X_DOWN)
    across = lax.ppermute(own, "dp", Y_SWAP)
    far_low = lax.ppermute(below[:PER // 2], "dp", X_UP)
    far_high = lax.ppermute(above[PER // 2:], "dp", X_DOWN)
    far = jnp.concatenate([far_low, far_high])
    below_across = lax.ppermute(across, "dp", X_UP)
    above_across = lax.ppermute(across, "dp", X_DOWN)
    far_across = lax.ppermute(far, "dp", Y_SWAP)
    piece_a = jnp.concatenate([own, below, above])
    piece_b = jnp.concatenate([across, far])
    piece_c = jnp.concatenate([below_across, above_across, far_across])
    pieces = [piece_a, piece_b, piece_c]
    pieces = pieces + [lax.ppermute(piece, "dp", C_SWAP) for piece in pieces]

    hidden, send, keep, rows = local_work(place, target, ranks, pieces, gathered, cotangent)

    summed = lax.psum_scatter(rows, "tensor", scatter_dimension=0, axis_index_groups=Z_RINGS)
    mine = jnp.where(low == 0, summed[0], summed[1])
    theirs = jnp.where(low == 0, summed[1], summed[0])
    back = lax.ppermute(theirs, "tensor", L_SWAP)
    grad_tokens = (mine.astype(f32) + back.astype(f32)).astype(bf16)

    came = lax.ppermute(send, "dp", C_SWAP)

    def block(dx, dy):
        at = BLOCKS[dx, dy] * PER
        return keep[at:at + PER].astype(f32) + came[at:at + PER].astype(f32)

    up_in = lax.ppermute(block(1, 1).astype(bf16), "dp", X_UP)
    down_in = lax.ppermute(block(3, 1).astype(bf16), "dp", X_DOWN)
    far_in = lax.ppermute(block(2, 1).astype(bf16), "dp", Y_SWAP)
    far_sum = (block(2, 0) + far_in.astype(f32)).astype(bf16)
    across_sum = (block(0, 1) + up_in.astype(f32) + down_in.astype(f32)).astype(bf16)
    half_up = lax.ppermute(far_sum[:PER // 2], "dp", X_UP)
    half_down = lax.ppermute(far_sum[PER // 2:], "dp", X_DOWN)
    across_in = lax.ppermute(across_sum, "dp", Y_SWAP)
    up_block, down_block = block(1, 0), block(3, 0)
    up_sum = jnp.concatenate([up_block[:PER // 2] + half_up.astype(f32), up_block[PER // 2:]])
    down_sum = jnp.concatenate([down_block[:PER // 2], down_block[PER // 2:] + half_down.astype(f32)])
    up_last = lax.ppermute(up_sum.astype(bf16), "dp", X_UP)
    down_last = lax.ppermute(down_sum.astype(bf16), "dp", X_DOWN)
    total = block(0, 0) + across_in.astype(f32) + up_last.astype(f32) + down_last.astype(f32)
    tile_grads = (total * (1.0 / (XS * YS * CS)))[None]
    return hidden, grad_tokens, tile_grads


def solution(mesh):
    in_specs = (
        P(("dp", "tensor"), None),
        P("tensor", "dp", None, None, None),
        P(None, None, "tensor"),
        P("dp", "tensor"),
    )
    out_specs = (P("dp", "tensor"), P(("dp", "tensor"), None), P("tensor", "dp", None, None, None))
    return jax.shard_map(body, mesh=mesh, in_specs=in_specs, out_specs=out_specs, check_vma=False)
```

time: 1130 us -> 177 us (0.16)
  local copies, waits for them, and re-layouts: 365 us -> 4.38 us
  other arithmetic: 301 us -> 14.6 us
  waiting for transfers between devices: 294 us -> 69.3 us
  matrix products: 147 us -> 0 us
  Pallas kernels: 0 us -> 36.2 us
  starting transfers between devices: 0.34 us -> 35 us
    scatter-add x64 -> x0, other arithmetic: 214 us -> none  [the longest x32 114 us: backward_group(): running = running.at[:, place_group[matrix_id, 0]].add(product)]
    unnamed x5 -> x2, waiting for transfers between devices: 153 us -> 0.03 us
    dot_general x66 -> x0, matrix products: 147 us -> none  [the longest x32 74 us: forward_group(): jnp.einsum('tgb,gbc->tgc', picked, tile_group[:, matrix_id], preferred_el...]
    all_gather x2 -> x1, waiting for transfers between devices: 137 us -> 2.85 us  [body(): gathered = lax.all_gather(pair, 'tensor', axis=0, axis_index_groups=Z_RINGS)]
    mul x65 -> x0, local copies, waits for them, and re-layouts: 125 us -> none  [the longest x32 83.3 us: forward_group(): product * place_group[matrix_id, 1].astype(jnp.float32)[None, :, None]]
    gather x68 -> x0, local copies, waits for them, and re-layouts: 108 us -> none  [the longest x32 61.3 us: backward_group(): picked = jnp.take(grad_blocks[matrix_id], col_group[matrix_id], axis=1)]
    squeeze x34 -> x0, local copies, waits for them, and re-layouts: 72.9 us -> none  [the longest x16 40.4 us: forward_group(): running[matrix_id].at[:, place_group[matrix_id, 0]].add(product)]
    ppermute x0 -> x22, waiting for transfers between devices: none -> 66.4 us  [the longest x1 11.9 us: body(): up_in = lax.ppermute(block(1, 1).astype(bf16), 'dp', X_UP)]
  transfers between devices with their start and end apart: 4 -> 24, of which waited for: 4 -> 15; matrix products, arithmetic and copies ran while one was open for 8% -> 8% of each run, Pallas kernels for 0% -> 0%
where the time goes in v1:
time: 177 us; the launch traced here: 174 us
  waiting for transfers between devices  69.3 us (39%)
  Pallas kernels  36.2 us (20%)
  starting transfers between devices  35 us (20%)
  other arithmetic  14.6 us (8%)
  between operations  14.3 us (8%)
  local copies, waits for them, and re-layouts  4.38 us (2%)
    pallas_call x1, Pallas kernels, local_work(): pl.pallas_call(kernel, out_shape=(jax.ShapeDtypeStruct((GROUP, HIDE), bf1...  36.2 us
    ppermute x1, waiting for transfers between devices, body(): up_in = lax.ppermute(block(1, 1).astype(bf16), 'dp', X_UP)  11.9 us
    ppermute x1, waiting for transfers between devices, body(): far_in = lax.ppermute(block(2, 1).astype(bf16), 'dp', Y_SWAP)  11.2 us
    ppermute x1, waiting for transfers between devices, body(): above = lax.ppermute(own, 'dp', X_DOWN)  7.78 us
    ppermute x1, waiting for transfers between devices, body(): came = lax.ppermute(send, 'dp', C_SWAP)  7.46 us
    ppermute x1, waiting for transfers between devices, body(): far_high = lax.ppermute(above[PER // 2:], 'dp', X_DOWN)  5.02 us
    ppermute x1, waiting for transfers between devices, body(): below_across = lax.ppermute(across, 'dp', X_UP)  4.05 us
    ppermute x1, waiting for transfers between devices, body(): other = lax.ppermute(tokens, 'tensor', L_SWAP)  3.87 us
  transfers between devices with their start and end apart: 24, of which 15 were waited for; matrix products, arithmetic and copies ran while one was open for 8% of the time, Pallas kernels for 0%

profile of v1, /device:TPU:6, one launch (start us, length us, event | category | flops | bytes accessed | tf_op | source)
XLA Modules:
  0.0 173.7 jit_solution(1648778659340588007)
XLA Ops:
  7.2 1.7 collective-permute-start.11
  8.9 3.9 %collective-permute-done.11 = bf16[16,4096]{1,0:T(8,128)(2,1)S(1)} collective-permute-done((bf16[16,4096]{1,0:T(8,128)(2,1)}, bf16[16,4096]{1,0:T(8,128)(2,1)S(1)}, u32[]{:S(2)}, u32[]{:S(2)}) %collective-permute-start.11) | collective-permute-done | bytes 131104 | tf_op jit(solution)/shard_map/ppermute | solution.py:198
  12.8 1.7 maximum_select_fusion
  14.5 0.9 collective-permute-start.1
  15.5 2.4 %collective-permute-start = (bf16[8,2,128,128]{3,2,1,0:T(8,128)(2,1)}, bf16[8,2,128,128]{3,2,1,0:T(8,128)(2,1)S(1)}, u32[]{:S(2)}, u32[]{:S(2)}) collective-permute-start(bf16[8,2,128,128]{3,2,1,0:T(8,128)(2,1)} %bitcast.27), channel_id=1, source_target_pairs={{0,64},{16,80},{32,96},{48,112},{64,128},{80,144},{96,160},{112,17... | collective-permute-start | bytes 1572872 | tf_op jit(solution)/shard_map/ppermute | solution.py:203
  17.9 3.2 %collective-permute-start.2 = (bf16[8,2,128,128]{3,2,1,0:T(8,128)(2,1)}, bf16[8,2,128,128]{3,2,1,0:T(8,128)(2,1)S(1)}, u32[]{:S(2)}, u32[]{:S(2)}) collective-permute-start(bf16[8,2,128,128]{3,2,1,0:T(8,128)(2,1)} %bitcast.28), channel_id=1, source_target_pairs={{0,32},{16,48},{32,0},{48,16},{64,96},{80,112},{96,64},{112,80},{1... | collective-permute-start | bytes 1572872 | tf_op jit(solution)/shard_map/ppermute | solution.py:205
  21.1 7.8 %collective-permute-done.1 = bf16[8,2,128,128]{3,2,1,0:T(8,128)(2,1)S(1)} collective-permute-done((bf16[8,2,128,128]{3,2,1,0:T(8,128)(2,1)}, bf16[8,2,128,128]{3,2,1,0:T(8,128)(2,1)S(1)}, u32[]{:S(2)}, u32[]{:S(2)}) %collective-permute-start.1) | collective-permute-done | bytes 524320 | tf_op jit(solution)/shard_map/ppermute | solution.py:204
  29.0 3.3 %collective-permute-start.3 = (bf16[4,2,128,128]{3,2,1,0:T(8,128)(2,1)S(1)}, bf16[4,2,128,128]{3,2,1,0:T(8,128)(2,1)S(1)}, u32[]{:S(2)}, u32[]{:S(2)}) collective-permute-start(bf16[4,2,128,128]{3,2,1,0:T(8,128)(2,1)S(1)} %slice.110), channel_id=1, source_target_pairs={{0,64},{16,80},{32,96},{48,112},{64,128},{80,144},{96,160},{112,17... | collective-permute-start | bytes 786440 | tf_op jit(solution)/shard_map/ppermute | solution.py:206
  32.4 1.9 %collective-permute-start.6 = (bf16[8,2,128,128]{3,2,1,0:T(8,128)(2,1)S(1)}, bf16[8,2,128,128]{3,2,1,0:T(8,128)(2,1)S(1)}, u32[]{:S(2)}, u32[]{:S(2)}) collective-permute-start(bf16[8,2,128,128]{3,2,1,0:T(8,128)(2,1)S(1)} %collective-permute-done.2), channel_id=1, source_target_pairs={{0,192},{16,208},{32,224},{48,240},{64,0},{80,16},{96,32},{112,48}... | collective-permute-start | bytes 1572872 | tf_op jit(solution)/shard_map/ppermute | solution.py:210
  34.3 5.0 %collective-permute-done.4 = bf16[4,2,128,128]{3,2,1,0:T(8,128)(2,1)S(1)} collective-permute-done((bf16[4,2,128,128]{3,2,1,0:T(8,128)(2,1)S(1)}, bf16[4,2,128,128]{3,2,1,0:T(8,128)(2,1)S(1)}, u32[]{:S(2)}, u32[]{:S(2)}) %collective-permute-start.4) | collective-permute-done | bytes 262176 | tf_op jit(solution)/shard_map/ppermute | solution.py:207
  39.4 3.3 %collective-permute-start.7 = (bf16[8,2,128,128]{3,2,1,0:T(8,128)(2,1)S(1)}, bf16[8,2,128,128]{3,2,1,0:T(8,128)(2,1)S(1)}, u32[]{:S(2)}, u32[]{:S(2)}) collective-permute-start(bf16[8,2,128,128]{3,2,1,0:T(8,128)(2,1)S(1)} %pad_maximum_fusion.1), channel_id=1, source_target_pairs={{0,32},{16,48},{32,0},{48,16},{64,96},{80,112},{96,64},{112,80},{1... | collective-permute-start | bytes 1572872 | tf_op jit(solution)/shard_map/ppermute | solution.py:211
  42.7 0.2 pad_maximum_fusion.piece_a
  43.0 4.1 %collective-permute-done.5 = bf16[8,2,128,128]{3,2,1,0:T(8,128)(2,1)S(1)} collective-permute-done((bf16[8,2,128,128]{3,2,1,0:T(8,128)(2,1)S(1)}, bf16[8,2,128,128]{3,2,1,0:T(8,128)(2,1)S(1)}, u32[]{:S(2)}, u32[]{:S(2)}) %collective-permute-start.5) | collective-permute-done | bytes 524320 | tf_op jit(solution)/shard_map/ppermute | solution.py:209
  47.0 0.8 constant_dynamic-update-slice_fusion.5
  47.8 0.8 constant_dynamic-update-slice_fusion.4
  48.7 1.5 collective-permute-done.7
  50.2 0.8 constant_dynamic-update-slice_fusion.3.piece_c
  51.1 0.8 collective-permute-start.9
  52.1 0.7 stack.81.ranks
  52.8 0.2 select_reduce_fusion
  53.0 0.6 fusion.9
  53.6 0.2 select_reduce_fusion.1
  53.9 0.6 broadcast_add_fusion.1.place
  54.5 1.6 collective-permute-done.9.piece_e
  56.0 2.9 %all-gather.2.cloned.1.call-done.gathered = bf16[8,2,16,4096]{3,2,1,0:T(8,128)(2,1)} async-done(((bf16[1,2,16,4096]{3,2,1,0:T(8,128)(2,1)}), bf16[8,2,16,4096]{3,2,1,0:T(8,128)(2,1)}) %all-gather.2.cloned.1.call-update) | async-done | bytes 2097168 | tf_op jit(solution)/shard_map/all_gather | solution.py:200
  58.9 36.2 %swiglu_local.1 = (bf16[256,896]{1,0:T(8,128)(2,1)}, bf16[64,2,128,128]{3,2,1,0:T(8,128)(2,1)}, bf16[64,2,128,128]{3,2,1,0:T(8,128)(2,1)}, bf16[8,2,16,4096]{3,2,1,0:T(8,128)(2,1)}) custom-call(s32[2,128]{1,0:T(2,128)} %broadcast_add_fusion.1.place, s32[2,224]{1,0:T(2,128)} %get-tuple-element.11.target, s32[16]{0:T(128)} %stack.81.ranks, ...), custom_call_target="tpu_custom_call" | custom-call | flops 11274289152 | bytes 25165824 | tf_op jit(solution)/shard_map/swiglu_local/pallas_call | solution.py:136
  95.2 7.5 %collective-permute-done.13 = bf16[64,2,128,128]{3,2,1,0:T(8,128)(2,1)} collective-permute-done((bf16[64,2,128,128]{3,2,1,0:T(8,128)(2,1)}, bf16[64,2,128,128]{3,2,1,0:T(8,128)(2,1)}, u32[]{:S(2)}, u32[]{:S(2)}) %collective-permute-start.13) | collective-permute-done | bytes 4194336 | tf_op jit(solution)/shard_map/ppermute | solution.py:226
  102.7 2.0 %add_convert_fusion.4 = (bf16[8,2,128,128]{3,2,1,0:T(8,128)(2,1)S(1)}, bf16[8,2,128,128]{3,2,1,0:T(8,128)(2,1)S(1)}) fusion(bf16[64,2,128,128]{3,2,1,0:T(8,128)(2,1)} %collective-permute-done.13, bf16[64,2,128,128]{3,2,1,0:T(8,128)(2,1)} %get-tuple-element.9), kind=kLoop, calls=%fused_computation.8 | loop fusion | flops 2097152 | bytes 3145728 | tf_op jit(solution)/shard_map/convert_element_type | solution.py:232
  104.7 0.7 collective-permute-start.14
  105.3 1.4 collective-permute-start.15
  106.8 11.9 %collective-permute-done.14 = bf16[8,2,128,128]{3,2,1,0:T(8,128)(2,1)S(1)} collective-permute-done((bf16[8,2,128,128]{3,2,1,0:T(8,128)(2,1)S(1)}, bf16[8,2,128,128]{3,2,1,0:T(8,128)(2,1)S(1)}, u32[]{:S(2)}, u32[]{:S(2)}) %collective-permute-start.14) | collective-permute-done | bytes 524320 | tf_op jit(solution)/shard_map/ppermute | solution.py:232
  118.7 1.5 collective-permute-done.15
  120.2 3.1 %add_convert_fusion.2 = (bf16[8,2,128,128]{3,2,1,0:T(8,128)(2,1)S(1)}, f32[8,2,128,128]{3,2,1,0:T(8,128)S(1)}, bf16[8,2,128,128]{3,2,1,0:T(8,128)(2,1)S(1)}, f32[8,2,128,128]{3,2,1,0:T(8,128)S(1)}) fusion(bf16[8,2,128,128]{3,2,1,0:T(8,128)(2,1)S(1)} %collective-permute-done.15, bf16[8,2,128,128]{3,2,1,0:T(8,128)(2,1)S(1)} %collective-permute-done.14, ...), kind=kLoop, calls=%fused_computation.6 | loop fusion | flops 4718592 | bytes 8388608 | tf_op jit(solution)/shard_map/convert_element_type | solution.py:236
  123.3 3.3 %collective-permute-start.17 = (bf16[8,2,128,128]{3,2,1,0:T(8,128)(2,1)S(1)}, bf16[8,2,128,128]{3,2,1,0:T(8,128)(2,1)S(1)}, u32[]{:S(2)}, u32[]{:S(2)}) collective-permute-start(bf16[8,2,128,128]{3,2,1,0:T(8,128)(2,1)S(1)} %get-tuple-element.15), channel_id=1, source_target_pairs={{0,32},{16,48},{32,0},{48,16},{64,96},{80,112},{96,64},{112,80},{1... | collective-permute-start | bytes 1572872 | tf_op jit(solution)/shard_map/ppermute | solution.py:234
  126.6 11.2 %collective-permute-done.17 = bf16[8,2,128,128]{3,2,1,0:T(8,128)(2,1)S(1)} collective-permute-done((bf16[8,2,128,128]{3,2,1,0:T(8,128)(2,1)S(1)}, bf16[8,2,128,128]{3,2,1,0:T(8,128)(2,1)S(1)}, u32[]{:S(2)}, u32[]{:S(2)}) %collective-permute-start.17) | collective-permute-done | bytes 524320 | tf_op jit(solution)/shard_map/ppermute | solution.py:234
  137.8 1.4 add_convert_fusion
  139.3 0.7 fusion.17
  140.2 1.0 select_bitcast_fusion
  141.2 1.6 collective-permute-start.12
  142.8 2.9 %collective-permute-start.16 = (bf16[8,2,128,128]{3,2,1,0:T(8,128)(2,1)S(1)}, bf16[8,2,128,128]{3,2,1,0:T(8,128)(2,1)S(1)}, u32[]{:S(2)}, u32[]{:S(2)}) collective-permute-start(bf16[8,2,128,128]{3,2,1,0:T(8,128)(2,1)S(1)} %get-tuple-element.13), channel_id=1, source_target_pairs={{0,32},{16,48},{32,0},{48,16},{64,96},{80,112},{96,64},{112,80},{1... | collective-permute-start | bytes 1572872 | tf_op jit(solution)/shard_map/ppermute | solution.py:239
  145.7 3.2 %collective-permute-start.18 = (bf16[4,2,128,128]{3,2,1,0:T(8,128)(2,1)S(1)}, bf16[4,2,128,128]{3,2,1,0:T(8,128)(2,1)S(1)}, u32[]{:S(2)}, u32[]{:S(2)}) collective-permute-start(bf16[4,2,128,128]{3,2,1,0:T(8,128)(2,1)S(1)} %get-tuple-element.19), channel_id=1, source_target_pairs={{0,64},{16,80},{32,96},{48,112},{64,128},{80,144},{96,160},{112,17... | collective-permute-start | bytes 786440 | tf_op jit(solution)/shard_map/ppermute | solution.py:237
  149.2 3.7 %collective-permute-done.18 = bf16[4,2,128,128]{3,2,1,0:T(8,128)(2,1)S(1)} collective-permute-done((bf16[4,2,128,128]{3,2,1,0:T(8,128)(2,1)S(1)}, bf16[4,2,128,128]{3,2,1,0:T(8,128)(2,1)S(1)}, u32[]{:S(2)}, u32[]{:S(2)}) %collective-permute-start.18) | collective-permute-done | bytes 262176 | tf_op jit(solution)/shard_map/ppermute | solution.py:237
  153.0 3.8 %collective-permute-start.19 = (bf16[8,2,128,128]{3,2,1,0:T(8,128)(2,1)S(1)}, bf16[8,2,128,128]{3,2,1,0:T(8,128)(2,1)S(1)}, u32[]{:S(2)}, u32[]{:S(2)}) collective-permute-start(bf16[8,2,128,128]{3,2,1,0:T(8,128)(2,1)S(1)} %pad_maximum_fusion.2), channel_id=1, source_target_pairs={{0,64},{16,80},{32,96},{48,112},{64,128},{80,144},{96,160},{112,17... | collective-permute-start | bytes 1572872 | tf_op jit(solution)/shard_map/ppermute | solution.py:243
  156.8 0.7 fusion.2
  157.5 0.9 collective-permute-done.16
  158.4 2.9 %collective-permute-done.21 = bf16[8,2,128,128]{3,2,1,0:T(8,128)(2,1)S(1)} collective-permute-done((bf16[8,2,128,128]{3,2,1,0:T(8,128)(2,1)S(1)}, bf16[8,2,128,128]{3,2,1,0:T(8,128)(2,1)S(1)}, u32[]{:S(2)}, u32[]{:S(2)}) %collective-permute-start.21) | collective-permute-done | bytes 524320 | tf_op jit(solution)/shard_map/ppermute | solution.py:244
  161.3 3.0 %collective-permute-done.19 = bf16[8,2,128,128]{3,2,1,0:T(8,128)(2,1)S(1)} collective-permute-done((bf16[8,2,128,128]{3,2,1,0:T(8,128)(2,1)S(1)}, bf16[8,2,128,128]{3,2,1,0:T(8,128)(2,1)S(1)}, u32[]{:S(2)}, u32[]{:S(2)}) %collective-permute-start.19) | collective-permute-done | bytes 524320 | tf_op jit(solution)/shard_map/ppermute | solution.py:243
  164.3 2.6 %multiply_bitcast_fusion = f32[1,8,2,128,128]{4,3,2,1,0:T(8,128)} fusion(bf16[8,2,128,128]{3,2,1,0:T(8,128)(2,1)S(1)} %collective-permute-done.21, bf16[8,2,128,128]{3,2,1,0:T(8,128)(2,1)S(1)} %collective-permute-done.19, bf16[8,2,128,128]{3,2,1,0:T(8,128)(2,1)S(1)} %collective-permute-done.16, bf16[64,2,128,128]{3,2,1,0:T(8,128)(2,1)} %collective-permute-done.13, ...), kind=kLoop, calls=%fused_computation.1 | loop fusion | flops 2621440 | bytes 3670016 | tf_op jit(solution)/shard_map/broadcast_in_dim | solution.py:246
  (46 shorter events, 1.5 us)
Async XLA Ops:
  7.2 35.5 %copy-start.2 = (bf16[1,8,2,128,128]{4,3,2,1,0:T(8,128)(2,1)S(1)}, bf16[1,8,2,128,128]{4,3,2,1,0:T(8,128)(2,1)}, u32[]{:S(2)}) copy-start(bf16[1,8,2,128,128]{4,3,2,1,0:T(8,128)(2,1)} %param.5) | copy-start | bytes 1572868
  7.2 51.7 %all-gather.2.cloned.1.call-start = ((), (), s32[]{:S(2)}) async-start(), calls=%async_computation.1 | async-start | bytes 2359296 | tf_op jit(solution)/shard_map/all_gather | solution.py:200
  7.2 5.5 %collective-permute-start.11 = (bf16[16,4096]{1,0:T(8,128)(2,1)}, bf16[16,4096]{1,0:T(8,128)(2,1)S(1)}, u32[]{:S(2)}, u32[]{:S(2)}) collective-permute-start(bf16[16,4096]{1,0:T(8,128)(2,1)} %param.4), channel_id=1, source_target_pairs={{0,8},{1,9},{2,10},{3,11},{4,12},{5,13},{6,14},{7,15},{8,0},{9,1},... | collective-permute-start | bytes 393224 | tf_op jit(solution)/shard_map/ppermute | solution.py:198
  14.5 125.7 %reduce-scatter.2.cloned.1.call-start = ((), (), s32[]{:S(2)}) async-start(), calls=%async_computation.2 | async-start | bytes 2359296 | tf_op jit(solution)/shard_map/reduce_scatter | solution.py:220
  14.5 14.3 %collective-permute-start.1 = (bf16[8,2,128,128]{3,2,1,0:T(8,128)(2,1)}, bf16[8,2,128,128]{3,2,1,0:T(8,128)(2,1)S(1)}, u32[]{:S(2)}, u32[]{:S(2)}) collective-permute-start(bf16[8,2,128,128]{3,2,1,0:T(8,128)(2,1)} %bitcast.26), channel_id=1, source_target_pairs={{0,192},{16,208},{32,224},{48,240},{64,0},{80,16},{96,32},{112,48}... | collective-permute-start | bytes 1572872 | tf_op jit(solution)/shard_map/ppermute | solution.py:204
  15.5 13.5 %collective-permute-start = (bf16[8,2,128,128]{3,2,1,0:T(8,128)(2,1)}, bf16[8,2,128,128]{3,2,1,0:T(8,128)(2,1)S(1)}, u32[]{:S(2)}, u32[]{:S(2)}) collective-permute-start(bf16[8,2,128,128]{3,2,1,0:T(8,128)(2,1)} %bitcast.27), channel_id=1, source_target_pairs={{0,64},{16,80},{32,96},{48,112},{64,128},{80,144},{96,160},{112,17... | collective-permute-start | bytes 1572872 | tf_op jit(solution)/shard_map/ppermute | solution.py:203
  17.9 14.4 %collective-permute-start.2 = (bf16[8,2,128,128]{3,2,1,0:T(8,128)(2,1)}, bf16[8,2,128,128]{3,2,1,0:T(8,128)(2,1)S(1)}, u32[]{:S(2)}, u32[]{:S(2)}) collective-permute-start(bf16[8,2,128,128]{3,2,1,0:T(8,128)(2,1)} %bitcast.28), channel_id=1, source_target_pairs={{0,32},{16,48},{32,0},{48,16},{64,96},{80,112},{96,64},{112,80},{1... | collective-permute-start | bytes 1572872 | tf_op jit(solution)/shard_map/ppermute | solution.py:205
  28.9 10.5 %collective-permute-start.4 = (bf16[4,2,128,128]{3,2,1,0:T(8,128)(2,1)S(1)}, bf16[4,2,128,128]{3,2,1,0:T(8,128)(2,1)S(1)}, u32[]{:S(2)}, u32[]{:S(2)}) collective-permute-start(bf16[4,2,128,128]{3,2,1,0:T(8,128)(2,1)S(1)} %slice.111), channel_id=1, source_target_pairs={{0,192},{16,208},{32,224},{48,240},{64,0},{80,16},{96,32},{112,48}... | collective-permute-start | bytes 786440 | tf_op jit(solution)/shard_map/ppermute | solution.py:207
  29.0 10.3 %collective-permute-start.3 = (bf16[4,2,128,128]{3,2,1,0:T(8,128)(2,1)S(1)}, bf16[4,2,128,128]{3,2,1,0:T(8,128)(2,1)S(1)}, u32[]{:S(2)}, u32[]{:S(2)}) collective-permute-start(bf16[4,2,128,128]{3,2,1,0:T(8,128)(2,1)S(1)} %slice.110), channel_id=1, source_target_pairs={{0,64},{16,80},{32,96},{48,112},{64,128},{80,144},{96,160},{112,17... | collective-permute-start | bytes 786440 | tf_op jit(solution)/shard_map/ppermute | solution.py:206
  32.3 14.7 %collective-permute-start.5 = (bf16[8,2,128,128]{3,2,1,0:T(8,128)(2,1)S(1)}, bf16[8,2,128,128]{3,2,1,0:T(8,128)(2,1)S(1)}, u32[]{:S(2)}, u32[]{:S(2)}) collective-permute-start(bf16[8,2,128,128]{3,2,1,0:T(8,128)(2,1)S(1)} %collective-permute-done.2), channel_id=1, source_target_pairs={{0,64},{16,80},{32,96},{48,112},{64,128},{80,144},{96,160},{112,17... | collective-permute-start | bytes 1572872 | tf_op jit(solution)/shard_map/ppermute | solution.py:209
  32.4 15.4 %collective-permute-start.6 = (bf16[8,2,128,128]{3,2,1,0:T(8,128)(2,1)S(1)}, bf16[8,2,128,128]{3,2,1,0:T(8,128)(2,1)S(1)}, u32[]{:S(2)}, u32[]{:S(2)}) collective-permute-start(bf16[8,2,128,128]{3,2,1,0:T(8,128)(2,1)S(1)} %collective-permute-done.2), channel_id=1, source_target_pairs={{0,192},{16,208},{32,224},{48,240},{64,0},{80,16},{96,32},{112,48}... | collective-permute-start | bytes 1572872 | tf_op jit(solution)/shard_map/ppermute | solution.py:210
  39.4 10.8 %collective-permute-start.7 = (bf16[8,2,128,128]{3,2,1,0:T(8,128)(2,1)S(1)}, bf16[8,2,128,128]{3,2,1,0:T(8,128)(2,1)S(1)}, u32[]{:S(2)}, u32[]{:S(2)}) collective-permute-start(bf16[8,2,128,128]{3,2,1,0:T(8,128)(2,1)S(1)} %pad_maximum_fusion.1), channel_id=1, source_target_pairs={{0,32},{16,48},{32,0},{48,16},{64,96},{80,112},{96,64},{112,80},{1... | collective-permute-start | bytes 1572872 | tf_op jit(solution)/shard_map/ppermute | solution.py:211
  42.8 8.2 %copy-start = (bf16[24,2,128,128]{3,2,1,0:T(8,128)(2,1)}, bf16[24,2,128,128]{3,2,1,0:T(8,128)(2,1)S(1)}, u32[]{:S(2)}) copy-start(bf16[24,2,128,128]{3,2,1,0:T(8,128)(2,1)S(1)} %pad_maximum_fusion.piece_a) | copy-start | bytes 4718596
  42.8 13.2 %collective-permute-start.8 = (bf16[24,2,128,128]{3,2,1,0:T(8,128)(2,1)S(1)}, bf16[24,2,128,128]{3,2,1,0:T(8,128)(2,1)}, u32[]{:S(2)}, u32[]{:S(2)}) collective-permute-start(bf16[24,2,128,128]{3,2,1,0:T(8,128)(2,1)S(1)} %pad_maximum_fusion.piece_a), channel_id=1, source_target_pairs={{0,16},{16,0},{32,48},{48,32},{64,80},{80,64},{96,112},{112,96},{1... | collective-permute-start | bytes 4718600 | tf_op jit(solution)/shard_map/ppermute | solution.py:216
  48.7 3.2 %copy-start.4 = (s32[2,32,7]{1,0,2:T(2,128)S(1)}, s32[2,32,7]{1,0,2:T(2,128)}, u32[]{:S(2)}) copy-start(s32[2,32,7]{1,0,2:T(2,128)} %param.6) | copy-start | bytes 5380
  51.0 5.0 %collective-permute-start.10 = (bf16[24,2,128,128]{3,2,1,0:T(8,128)(2,1)}, bf16[24,2,128,128]{3,2,1,0:T(8,128)(2,1)}, u32[]{:S(2)}, u32[]{:S(2)}) collective-permute-start(bf16[24,2,128,128]{3,2,1,0:T(8,128)(2,1)} %constant_dynamic-update-slice_fusion.3.piece_c), channel_id=1, source_target_pairs={{0,16},{16,0},{32,48},{48,32},{64,80},{80,64},{96,112},{112,96},{1... | collective-permute-start | bytes 4718600 | tf_op jit(solution)/shard_map/ppermute | solution.py:216
  51.1 7.8 %copy-start.3 = (bf16[16,2,128,128]{3,2,1,0:T(8,128)(2,1)}, bf16[16,2,128,128]{3,2,1,0:T(8,128)(2,1)S(1)}, u32[]{:S(2)}) copy-start(bf16[16,2,128,128]{3,2,1,0:T(8,128)(2,1)S(1)} %constant_dynamic-update-slice_fusion.piece_b) | copy-start | bytes 3145732
  51.1 4.9 %collective-permute-start.9 = (bf16[16,2,128,128]{3,2,1,0:T(8,128)(2,1)S(1)}, bf16[16,2,128,128]{3,2,1,0:T(8,128)(2,1)}, u32[]{:S(2)}, u32[]{:S(2)}) collective-permute-start(bf16[16,2,128,128]{3,2,1,0:T(8,128)(2,1)S(1)} %constant_dynamic-update-slice_fusion.piece_b), channel_id=1, source_target_pairs={{0,16},{16,0},{32,48},{48,32},{64,80},{80,64},{96,112},{112,96},{1... | collective-permute-start | bytes 3145736 | tf_op jit(solution)/shard_map/ppermute | solution.py:216
  95.1 7.6 %collective-permute-start.13 = (bf16[64,2,128,128]{3,2,1,0:T(8,128)(2,1)}, bf16[64,2,128,128]{3,2,1,0:T(8,128)(2,1)}, u32[]{:S(2)}, u32[]{:S(2)}) collective-permute-start(bf16[64,2,128,128]{3,2,1,0:T(8,128)(2,1)} %get-tuple-element.10), channel_id=1, source_target_pairs={{0,16},{16,0},{32,48},{48,32},{64,80},{80,64},{96,112},{112,96},{1... | collective-permute-start | bytes 12582920 | tf_op jit(solution)/shard_map/ppermute | solution.py:226
  104.7 14.0 %collective-permute-start.14 = (bf16[8,2,128,128]{3,2,1,0:T(8,128)(2,1)S(1)}, bf16[8,2,128,128]{3,2,1,0:T(8,128)(2,1)S(1)}, u32[]{:S(2)}, u32[]{:S(2)}) collective-permute-start(bf16[8,2,128,128]{3,2,1,0:T(8,128)(2,1)S(1)} %get-tuple-element.17), channel_id=1, source_target_pairs={{0,64},{16,80},{32,96},{48,112},{64,128},{80,144},{96,160},{112,17... | collective-permute-start | bytes 1572872 | tf_op jit(solution)/shard_map/ppermute | solution.py:232
  105.3 14.9 %collective-permute-start.15 = (bf16[8,2,128,128]{3,2,1,0:T(8,128)(2,1)S(1)}, bf16[8,2,128,128]{3,2,1,0:T(8,128)(2,1)S(1)}, u32[]{:S(2)}, u32[]{:S(2)}) collective-permute-start(bf16[8,2,128,128]{3,2,1,0:T(8,128)(2,1)S(1)} %get-tuple-element.18), channel_id=1, source_target_pairs={{0,192},{16,208},{32,224},{48,240},{64,0},{80,16},{96,32},{112,48}... | collective-permute-start | bytes 1572872 | tf_op jit(solution)/shard_map/ppermute | solution.py:233
  123.3 14.5 %collective-permute-start.17 = (bf16[8,2,128,128]{3,2,1,0:T(8,128)(2,1)S(1)}, bf16[8,2,128,128]{3,2,1,0:T(8,128)(2,1)S(1)}, u32[]{:S(2)}, u32[]{:S(2)}) collective-permute-start(bf16[8,2,128,128]{3,2,1,0:T(8,128)(2,1)S(1)} %get-tuple-element.15), channel_id=1, source_target_pairs={{0,32},{16,48},{32,0},{48,16},{64,96},{80,112},{96,64},{112,80},{1... | collective-permute-start | bytes 1572872 | tf_op jit(solution)/shard_map/ppermute | solution.py:234
  140.0 9.0 %collective-permute-start.20 = (bf16[4,2,128,128]{3,2,1,0:T(8,128)(2,1)}, bf16[4,2,128,128]{3,2,1,0:T(8,128)(2,1)S(1)}, u32[]{:S(2)}, u32[]{:S(2)}) collective-permute-start(bf16[4,2,128,128]{3,2,1,0:T(8,128)(2,1)} %get-tuple-element.20), channel_id=1, source_target_pairs={{0,192},{16,208},{32,224},{48,240},{64,0},{80,16},{96,32},{112,48}... | collective-permute-start | bytes 786440 | tf_op jit(solution)/shard_map/ppermute | solution.py:238
  141.2 15.6 %collective-permute-start.12 = (bf16[16,4096]{1,0:T(8,128)(2,1)S(1)}, bf16[16,4096]{1,0:T(8,128)(2,1)S(1)}, u32[]{:S(2)}, u32[]{:S(2)}) collective-permute-start(bf16[16,4096]{1,0:T(8,128)(2,1)S(1)} %select_bitcast_fusion), channel_id=1, source_target_pairs={{0,8},{1,9},{2,10},{3,11},{4,12},{5,13},{6,14},{7,15},{8,0},{9,1},... | collective-permute-start | bytes 393224 | tf_op jit(solution)/shard_map/ppermute | solution.py:223
  142.8 15.5 %collective-permute-start.16 = (bf16[8,2,128,128]{3,2,1,0:T(8,128)(2,1)S(1)}, bf16[8,2,128,128]{3,2,1,0:T(8,128)(2,1)S(1)}, u32[]{:S(2)}, u32[]{:S(2)}) collective-permute-start(bf16[8,2,128,128]{3,2,1,0:T(8,128)(2,1)S(1)} %get-tuple-element.13), channel_id=1, source_target_pairs={{0,32},{16,48},{32,0},{48,16},{64,96},{80,112},{96,64},{112,80},{1... | collective-permute-start | bytes 1572872 | tf_op jit(solution)/shard_map/ppermute | solution.py:239
  145.7 7.1 %collective-permute-start.18 = (bf16[4,2,128,128]{3,2,1,0:T(8,128)(2,1)S(1)}, bf16[4,2,128,128]{3,2,1,0:T(8,128)(2,1)S(1)}, u32[]{:S(2)}, u32[]{:S(2)}) collective-permute-start(bf16[4,2,128,128]{3,2,1,0:T(8,128)(2,1)S(1)} %get-tuple-element.19), channel_id=1, source_target_pairs={{0,64},{16,80},{32,96},{48,112},{64,128},{80,144},{96,160},{112,17... | collective-permute-start | bytes 786440 | tf_op jit(solution)/shard_map/ppermute | solution.py:237
  149.0 7.7 %copy-start.1 = (bf16[1,2,16,4096]{3,2,1,0:T(8,128)(2,1)S(1)}, bf16[1,2,16,4096]{3,2,1,0:T(8,128)(2,1)}, u32[]{:S(2)}) copy-start(bf16[1,2,16,4096]{3,2,1,0:T(8,128)(2,1)} %reduce-scatter.2.cloned.1.call-done) | copy-start | bytes 786436
  149.1 12.2 %collective-permute-start.21 = (bf16[8,2,128,128]{3,2,1,0:T(8,128)(2,1)S(1)}, bf16[8,2,128,128]{3,2,1,0:T(8,128)(2,1)S(1)}, u32[]{:S(2)}, u32[]{:S(2)}) collective-permute-start(bf16[8,2,128,128]{3,2,1,0:T(8,128)(2,1)S(1)} %pad_maximum_fusion.3), channel_id=1, source_target_pairs={{0,192},{16,208},{32,224},{48,240},{64,0},{80,16},{96,32},{112,48}... | collective-permute-start | bytes 1572872 | tf_op jit(solution)/shard_map/ppermute | solution.py:244
  153.0 11.3 %collective-permute-start.19 = (bf16[8,2,128,128]{3,2,1,0:T(8,128)(2,1)S(1)}, bf16[8,2,128,128]{3,2,1,0:T(8,128)(2,1)S(1)}, u32[]{:S(2)}, u32[]{:S(2)}) collective-permute-start(bf16[8,2,128,128]{3,2,1,0:T(8,128)(2,1)S(1)} %pad_maximum_fusion.2), channel_id=1, source_target_pairs={{0,64},{16,80},{32,96},{48,112},{64,128},{80,144},{96,160},{112,17... | collective-permute-start | bytes 1572872 | tf_op jit(solution)/shard_map/ppermute | solution.py:243
Sparse Core Ops, SparseCore 0:
  14.6 44.2 all-gather.1
  95.4 42.6 reduce-scatter.1

commit v2 on v1

v2 whole, which is shorter than its diff:
```python
import jax
import jax.numpy as jnp
from jax import lax
from jax.experimental import pallas as pl
from jax.experimental.pallas import tpu as pltpu
from jax.sharding import PartitionSpec as P

TILE = 128
ROWS = 32
COLS = 7
CAP = 128
PER = 8
GROUP = 256
WIDTH = ROWS * TILE
HIDE = COLS * TILE
DEAD = ROWS * COLS
XS, YS, CS = 4, 2, 2
ZS, YL = 8, 2


def dp_perm(move):
    def index(x, y, c):
        return (x * YS + y) * CS + c

    return [
        (index(x, y, c), index(*move(x, y, c)))
        for x in range(XS)
        for y in range(YS)
        for c in range(CS)
    ]


X_UP = dp_perm(lambda x, y, c: ((x + 1) % XS, y, c))
X_DOWN = dp_perm(lambda x, y, c: ((x - 1) % XS, y, c))
Y_SWAP = dp_perm(lambda x, y, c: (x, 1 - y, c))
C_SWAP = dp_perm(lambda x, y, c: (x, y, 1 - c))
L_SWAP = [(l * ZS + z, (1 - l) * ZS + z) for l in range(YL) for z in range(ZS)]
Z_RINGS = [[l * ZS + z for z in range(ZS)] for l in range(YL)]

BLOCKS = {(1, 1): 0, (3, 1): 1, (2, 1): 2, (0, 1): 3, (2, 0): 4, (1, 0): 5, (3, 0): 6, (0, 0): 7}
EARLY = 3 * PER
HALF = len(BLOCKS) * PER
PIECES = 2 * len(BLOCKS)
VMEM_LIMIT = 58 * 1024 * 1024


def start_rows(low, gathered, tokens, sems):
    copies = []
    for z in range(ZS):
        for l in range(YL):
            first = pl.multiple_of((low[0] ^ l) * (GROUP // YL) + z * 16, 16)
            copies.append(
                pltpu.make_async_copy(
                    gathered.at[z, l], tokens.at[pl.ds(first, 16)], sems.at[z * YL + l]
                )
            )
            copies[-1].start()
    return copies


def dense_kernel(*refs):
    place, ranks, low = refs[:3]
    pieces = refs[3:3 + PIECES]
    gathered, cotangent, hidden, grads, rows_out = refs[3 + PIECES:8 + PIECES]
    weight, stored, tokens, rows, piece_sems, row_sems, out_sems = refs[8 + PIECES:]
    copies = []
    for p in range(PIECES):
        copies.append(
            pltpu.make_async_copy(pieces[p], stored.at[pl.ds(p * PER, PER)], piece_sems.at[p])
        )
        copies[-1].start()
    row_copies = start_rows(low, gathered, tokens, row_sems)
    weight[...] = jnp.zeros_like(weight)
    for p in range(PIECES):
        copies[p].wait()
        for j in range(PER):
            for m in range(2):
                spot = place[m, ranks[p] * PER + j]
                weight[spot, :, m * TILE:(m + 1) * TILE] = stored[p * PER + j, m]
    for copy in row_copies:
        copy.wait()

    for c in range(COLS):
        dense = weight[c * ROWS:(c + 1) * ROWS].reshape(WIDTH, 2 * TILE)
        total = jnp.dot(tokens[...], dense, preferred_element_type=jnp.float32)
        gate, up = total[:, :TILE], total[:, TILE:]
        lanes = slice(c * TILE, (c + 1) * TILE)
        sigma = 1.0 / (1.0 + jnp.exp(-gate))
        swish = gate * sigma
        hidden[:, lanes] = (swish * up).astype(jnp.bfloat16)
        out_grad = cotangent[:, lanes].astype(jnp.float32)
        grads[c, :, TILE:] = (out_grad * swish).astype(jnp.bfloat16)
        grads[c, :, :TILE] = (
            out_grad * up * sigma * (1.0 + gate * (1.0 - sigma))
        ).astype(jnp.bfloat16)

    span = 256
    out_copies = []
    for part in range(WIDTH // span):
        total = jnp.zeros((GROUP, span), jnp.float32)
        for c in range(COLS):
            dense = weight[c * ROWS + part * 2:c * ROWS + part * 2 + 2].reshape(span, 2 * TILE)
            total += lax.dot_general(
                grads[c], dense, (((1,), (1,)), ((), ())), preferred_element_type=jnp.float32
            )
        lanes = slice(part * span, (part + 1) * span)
        for z in range(ZS):
            for l in range(YL):
                rows[z, l, :, lanes] = total[l * 128 + z * 16:l * 128 + z * 16 + 16]
        if part % 4 == 3:
            wide = pl.ds((part - 3) * span, 4 * span)
            out_copies.append(
                pltpu.make_async_copy(
                    rows.at[:, :, :, wide], rows_out.at[:, :, :, wide], out_sems.at[part // 4]
                )
            )
            out_copies[-1].start()
    for copy in out_copies:
        copy.wait()


def dense_work(place, ranks, low, pieces, gathered, cotangent):
    smem = pl.BlockSpec(memory_space=pltpu.SMEM)
    vmem = pl.BlockSpec(memory_space=pltpu.VMEM)
    hbm = pl.BlockSpec(memory_space=pl.ANY)
    bf16 = jnp.bfloat16
    return pl.pallas_call(
        dense_kernel,
        out_shape=(
            jax.ShapeDtypeStruct((GROUP, HIDE), bf16),
            jax.ShapeDtypeStruct((COLS, GROUP, 2 * TILE), bf16),
            jax.ShapeDtypeStruct((ZS, YL, 16, WIDTH), jnp.float32),
        ),
        in_specs=[smem] * 3 + [hbm] * (PIECES + 1) + [vmem],
        out_specs=(vmem, vmem, hbm),
        scratch_shapes=[
            pltpu.VMEM((DEAD + 1, TILE, 2 * TILE), bf16),
            pltpu.VMEM((CAP, 2, TILE, TILE), bf16),
            pltpu.VMEM((GROUP, WIDTH), bf16),
            pltpu.VMEM((ZS, YL, 16, WIDTH), jnp.float32),
            pltpu.SemaphoreType.DMA((PIECES,)),
            pltpu.SemaphoreType.DMA((ZS * YL,)),
            pltpu.SemaphoreType.DMA((4,)),
        ],
        compiler_params=pltpu.CompilerParams(vmem_limit_bytes=VMEM_LIMIT),
        cost_estimate=pl.CostEstimate(
            flops=4 * GROUP * WIDTH * 2 * HIDE, bytes_accessed=16 << 20, transcendentals=GROUP * HIDE
        ),
        name="forward_and_rows",
    )(place, ranks, low, *pieces, gathered, cotangent)


def tile_kernel(
    target, low, gathered, grads, early_out, late_out, keep_out, tokens, turned, tiles, row_sems, sems
):
    row_copies = start_rows(low, gathered, tokens, row_sems)
    tiles[...] = jnp.zeros_like(tiles)
    for copy in row_copies:
        copy.wait()
    for r in range(0, WIDTH, 512):
        turned[r:r + 512, :] = tokens[:, r:r + 512].T
    span = 256

    def column(c, unused):
        for part in range(WIDTH // span):
            total = jnp.dot(
                turned[part * span:(part + 1) * span, :], grads[c],
                preferred_element_type=jnp.float32,
            ).astype(jnp.bfloat16)
            for i in range(span // TILE):
                for m in range(2):
                    spot = target[m, (part * (span // TILE) + i) * COLS + c]
                    tiles[spot, m] = total[i * TILE:(i + 1) * TILE, m * TILE:(m + 1) * TILE]
        return unused

    lax.fori_loop(0, COLS, column, 0)
    copies = [
        pltpu.make_async_copy(tiles.at[pl.ds(0, EARLY)], early_out, sems.at[0]),
        pltpu.make_async_copy(tiles.at[pl.ds(EARLY, HALF - EARLY)], late_out, sems.at[1]),
        pltpu.make_async_copy(tiles.at[pl.ds(HALF, HALF)], keep_out, sems.at[2]),
    ]
    for copy in copies:
        copy.start()
    for copy in copies:
        copy.wait()


def tile_work(target, low, gathered, grads):
    smem = pl.BlockSpec(memory_space=pltpu.SMEM)
    vmem = pl.BlockSpec(memory_space=pltpu.VMEM)
    hbm = pl.BlockSpec(memory_space=pl.ANY)
    bf16 = jnp.bfloat16
    return pl.pallas_call(
        tile_kernel,
        out_shape=tuple(
            jax.ShapeDtypeStruct((n, 2, TILE, TILE), bf16) for n in (EARLY, HALF - EARLY, HALF)
        ),
        in_specs=[smem] * 2 + [hbm, vmem],
        out_specs=(hbm,) * 3,
        scratch_shapes=[
            pltpu.VMEM((GROUP, WIDTH), bf16),
            pltpu.VMEM((WIDTH, GROUP), bf16),
            pltpu.VMEM((CAP + 1, 2, TILE, TILE), bf16),
            pltpu.SemaphoreType.DMA((ZS * YL,)),
            pltpu.SemaphoreType.DMA((3,)),
        ],
        compiler_params=pltpu.CompilerParams(vmem_limit_bytes=VMEM_LIMIT),
        cost_estimate=pl.CostEstimate(
            flops=2 * GROUP * WIDTH * 2 * HIDE, bytes_accessed=12 << 20, transcendentals=0
        ),
        name="tile_sums",
    )(target, low, gathered, grads)


def tables(keep_local, x, y, c):
    keep = keep_local.reshape(2, ROWS * COLS)
    spots = jnp.arange(ROWS * COLS, dtype=jnp.int32)
    order = jnp.sum(jnp.where(spots[None, :] <= spots[:, None], keep[:, None, :], 0), axis=2) - 1
    dense_spot = (spots % COLS) * ROWS + spots // COLS
    slots = jnp.arange(CAP, dtype=jnp.int32)
    match = (order[:, None, :] == slots[None, :, None]) & (keep[:, None, :] == 1)
    place = DEAD + jnp.sum(jnp.where(match, dense_spot - DEAD, 0), axis=2)
    owner = order >> 3
    dx = ((owner >> 2) - x) & (XS - 1)
    dy = ((owner >> 1) & 1) ^ y
    dc = (owner & 1) ^ c
    block = jnp.zeros_like(owner)
    for (a, b), at in BLOCKS.items():
        block = jnp.where((dx == a) & (dy == b), at, block)
    target = ((1 - dc) * len(BLOCKS) + block) * PER + (order & (PER - 1))
    target = jnp.where(keep == 1, target, CAP)
    return place.astype(jnp.int32), target.astype(jnp.int32)


def piece_ranks(x, y, c):
    spots = [(0, 0), (3, 0), (1, 0), (0, 1), (2, 0), (3, 1), (1, 1), (2, 1)]
    dx = jnp.array([a for a, b in spots] * 2, jnp.int32)
    dy = jnp.array([b for a, b in spots] * 2, jnp.int32)
    dc = jnp.array([0] * len(spots) + [1] * len(spots), jnp.int32)
    return (((x + dx) & (XS - 1)) * YS + (y ^ dy)) * CS + (c ^ dc)


def body(tokens, weight_tiles, keep_mask, cotangent):
    f32, bf16 = jnp.float32, jnp.bfloat16
    rank = lax.axis_index("dp")
    x, y, c = rank >> 2, (rank >> 1) & 1, rank & 1
    low = lax.axis_index("tensor") >> 3

    other = lax.ppermute(tokens, "tensor", L_SWAP)
    own = weight_tiles[0]
    below = lax.ppermute(own, "dp", X_UP)
    above = lax.ppermute(own, "dp", X_DOWN)
    across = lax.ppermute(own, "dp", Y_SWAP)
    gathered = lax.all_gather(
        jnp.stack([tokens, other]), "tensor", axis=0, axis_index_groups=Z_RINGS
    )
    place, target = tables(keep_mask, x, y, c)
    ranks = piece_ranks(x, y, c)
    half = PER // 2
    far_low = lax.ppermute(below[:half], "dp", X_UP)
    far_high = lax.ppermute(above[half:], "dp", X_DOWN)
    far = jnp.concatenate([far_low, far_high])
    below_across = lax.ppermute(across, "dp", X_UP)
    above_across = lax.ppermute(across, "dp", X_DOWN)
    far_across = lax.ppermute(far, "dp", Y_SWAP)
    pieces = [own, below, above, across, far, below_across, above_across, far_across]
    pieces = pieces + [lax.ppermute(piece, "dp", C_SWAP) for piece in pieces]
    low_table = low.reshape(1).astype(jnp.int32)

    hidden, grads, rows = dense_work(place, ranks, low_table, pieces, gathered, cotangent)
    summed = lax.psum_scatter(rows, "tensor", scatter_dimension=0, axis_index_groups=Z_RINGS)
    early, late, keep = tile_work(target, low_table, gathered, grads)

    early_in = lax.ppermute(early, "dp", C_SWAP)

    def block(dx, dy, late_in=None):
        at = BLOCKS[dx, dy] * PER
        came = early_in[at:at + PER] if at < EARLY else late_in[at - EARLY:at - EARLY + PER]
        return keep[at:at + PER].astype(f32) + came.astype(f32)

    sends = [block(*at).astype(bf16) for at in ((2, 1), (1, 1), (3, 1))]
    *sends, late = lax.optimization_barrier((*sends, late))
    far_in = lax.ppermute(sends[0], "dp", Y_SWAP)
    up_in = lax.ppermute(sends[1], "dp", X_UP)
    down_in = lax.ppermute(sends[2], "dp", X_DOWN)
    late_in = lax.ppermute(late, "dp", C_SWAP)
    far_in, up_in, down_in, late_one = lax.optimization_barrier((far_in, up_in, down_in, late_in))
    far_sum = block(2, 0, late_one) + far_in.astype(f32)
    across_sum = block(0, 1, late_one) + up_in.astype(f32) + down_in.astype(f32)
    sends = lax.optimization_barrier(
        (across_sum.astype(bf16), far_sum[:half].astype(bf16), far_sum[half:].astype(bf16))
    )
    across_in = lax.ppermute(sends[0], "dp", Y_SWAP)
    half_up = lax.ppermute(sends[1], "dp", X_UP)
    half_down = lax.ppermute(sends[2], "dp", X_DOWN)
    half_up, half_down, late_two = lax.optimization_barrier((half_up, half_down, late_one))
    none = jnp.zeros_like(half_up)
    up_sum = block(1, 0, late_two) + jnp.concatenate([half_up, none]).astype(f32)
    down_sum = block(3, 0, late_two) + jnp.concatenate([none, half_down]).astype(f32)
    sends = lax.optimization_barrier((up_sum.astype(bf16), down_sum.astype(bf16)))
    up_last = lax.ppermute(sends[0], "dp", X_UP)
    down_last = lax.ppermute(sends[1], "dp", X_DOWN)
    up_last, down_last, across_in, late_three = lax.optimization_barrier(
        (up_last, down_last, across_in, late_two)
    )
    total = block(0, 0, late_three) + across_in.astype(f32)
    total = total + up_last.astype(f32) + down_last.astype(f32)
    tile_grads = (total * (1.0 / (XS * YS * CS)))[None]

    mine = jnp.where(low == 0, summed[0], summed[1])
    theirs = jnp.where(low == 0, summed[1], summed[0])
    back = lax.ppermute(theirs.astype(bf16), "tensor", L_SWAP)
    grad_tokens = (mine + back.astype(f32)).astype(bf16)
    return hidden, grad_tokens, tile_grads


def solution(mesh):
    in_specs = (
        P(("dp", "tensor"), None),
        P("tensor", "dp", None, None, None),
        P(None, None, "tensor"),
        P("dp", "tensor"),
    )
    out_specs = (P("dp", "tensor"), P(("dp", "tensor"), None), P("tensor", "dp", None, None, None))
    return jax.shard_map(body, mesh=mesh, in_specs=in_specs, out_specs=out_specs, check_vma=False)
```

time: 177 us -> 151 us (0.85); the launches traced: 174 us -> 151 us
  Pallas kernels: 36.2 us -> 28.1 us
  starting transfers between devices: 35 us -> 27.6 us
  waiting for transfers between devices: 69.3 us -> 64.9 us
    pallas_call x1 -> x2, Pallas kernels: 36.2 us -> 28.1 us  [the longest x1 16 us: dense_work(): pl.pallas_call(dense_kernel, out_shape=(jax.ShapeDtypeStruct((GROUP, HIDE...]
    ppermute x1, waiting for transfers between devices: 7.78 us -> 0.01 us  [body(): above = lax.ppermute(own, 'dp', X_DOWN)]
    ppermute x1, waiting for transfers between devices: 0.01 us -> 7.78 us  [body(): below = lax.ppermute(own, 'dp', X_UP)]
    ppermute x12 -> x13, starting transfers between devices: 20.6 us -> 14 us  [the longest x1 3.05 us: body(): far_in = lax.ppermute(sends[0], 'dp', Y_SWAP)]
    ppermute x1, waiting for transfers between devices: 1.48 us -> 7.61 us  [body(): far_across = lax.ppermute(far, 'dp', Y_SWAP)]
    ppermute x12 -> x13, waiting for transfers between devices: 47.7 us -> 41.8 us  [the longest x1 10.4 us: body(): far_in = lax.ppermute(sends[0], 'dp', Y_SWAP)]
    another operation x2, other arithmetic: 0.11 us -> 2.99 us  [the longest x1 1.63 us: body(): jnp.stack([tokens, other])]
    all_gather x1, waiting for transfers between devices: 2.85 us -> 0.01 us  [body(): lax.all_gather(jnp.stack([tokens, other]), 'tensor', axis=0, axis_index_g...]
  transfers between devices with their start and end apart: 24 -> 30, of which waited for: 15 -> 17; matrix products, arithmetic and copies ran while one was open for 8% -> 7% of each run, Pallas kernels for 0% -> 8%
where the time goes in v2:
time: 151 us
  waiting for transfers between devices  64.9 us (43%)
  Pallas kernels  28.1 us (19%)
  starting transfers between devices  27.6 us (18%)
  between operations  14.3 us (9%)
  other arithmetic  13.1 us (9%)
  local copies, waits for them, and re-layouts  2.96 us (2%)
    pallas_call x1, Pallas kernels, dense_work(): pl.pallas_call(dense_kernel, out_shape=(jax.ShapeDtypeStruct((GROUP, HIDE...  16 us
    pallas_call x1, Pallas kernels, tile_work(): pl.pallas_call(tile_kernel, out_shape=tuple((jax.ShapeDtypeStruct((n, 2,...  12.1 us
    ppermute x1, waiting for transfers between devices, body(): far_in = lax.ppermute(sends[0], 'dp', Y_SWAP)  10.4 us
    ppermute x1, waiting for transfers between devices, body(): below = lax.ppermute(own, 'dp', X_UP)  7.78 us
    ppermute x1, waiting for transfers between devices, body(): far_across = lax.ppermute(far, 'dp', Y_SWAP)  7.61 us
    ppermute x1, waiting for transfers between devices, body(): up_last = lax.ppermute(sends[0], 'dp', X_UP)  6.53 us
    ppermute x1, waiting for transfers between devices, body(): half_up = lax.ppermute(sends[1], 'dp', X_UP)  4.7 us
    ppermute x1, waiting for transfers between devices, body(): other = lax.ppermute(tokens, 'tensor', L_SWAP)  3.87 us
  transfers between devices with their start and end apart: 30, of which 17 were waited for; matrix products, arithmetic and copies ran while one was open for 7% of the time, Pallas kernels for 8%

profile of v2, /device:TPU:6, one launch (start us, length us, event | category | flops | bytes accessed | tf_op | source)
XLA Modules:
  0.0 151.0 jit_solution(12584305766639111818)
XLA Ops:
  7.2 1.7 %collective-permute-start.16 = (bf16[16,4096]{1,0:T(8,128)(2,1)}, bf16[16,4096]{1,0:T(8,128)(2,1)S(1)}, u32[]{:S(2)}, u32[]{:S(2)}) collective-permute-start(bf16[16,4096]{1,0:T(8,128)(2,1)} %param.7), channel_id=1, source_target_pairs={{0,8},{1,9},{2,10},{3,11},{4,12},{5,13},{6,14},{7,15},{8,0},{9,1},... | collective-permute-start | bytes 393224 | tf_op jit(solution)/shard_map/ppermute | solution.py:249
  8.9 3.9 %collective-permute-done.16 = bf16[16,4096]{1,0:T(8,128)(2,1)S(1)} collective-permute-done((bf16[16,4096]{1,0:T(8,128)(2,1)}, bf16[16,4096]{1,0:T(8,128)(2,1)S(1)}, u32[]{:S(2)}, u32[]{:S(2)}) %collective-permute-start.16) | collective-permute-done | bytes 131104 | tf_op jit(solution)/shard_map/ppermute | solution.py:249
  12.8 1.6 %pad_maximum_fusion = bf16[2,16,4096]{2,1,0:T(8,128)(2,1)} fusion(bf16[1,16,4096]{2,1,0:T(8,128)(2,1)S(1)} %bitcast.14, bf16[1,16,4096]{2,1,0:T(8,128)(2,1)} %bitcast.13), kind=kLoop, calls=%fused_computation.9 | loop fusion | flops 131072 | bytes 524288 | tf_op jit(solution)/shard_map/stack | solution.py:255
  14.5 2.0 %collective-permute-start = (bf16[8,2,128,128]{3,2,1,0:T(8,128)(2,1)}, bf16[8,2,128,128]{3,2,1,0:T(8,128)(2,1)S(1)}, u32[]{:S(2)}, u32[]{:S(2)}) collective-permute-start(bf16[8,2,128,128]{3,2,1,0:T(8,128)(2,1)} %bitcast.17), channel_id=1, source_target_pairs={{0,64},{16,80},{32,96},{48,112},{64,128},{80,144},{96,160},{112,17... | collective-permute-start | bytes 1572872 | tf_op jit(solution)/shard_map/ppermute | solution.py:251
  16.6 3.2 %collective-permute-start.2 = (bf16[8,2,128,128]{3,2,1,0:T(8,128)(2,1)}, bf16[8,2,128,128]{3,2,1,0:T(8,128)(2,1)S(1)}, u32[]{:S(2)}, u32[]{:S(2)}) collective-permute-start(bf16[8,2,128,128]{3,2,1,0:T(8,128)(2,1)} %bitcast.19), channel_id=1, source_target_pairs={{0,32},{16,48},{32,0},{48,16},{64,96},{80,112},{96,64},{112,80},{1... | collective-permute-start | bytes 1572872 | tf_op jit(solution)/shard_map/ppermute | solution.py:253
  19.8 7.8 %collective-permute-done.refs_4_ = bf16[8,2,128,128]{3,2,1,0:T(8,128)(2,1)S(1)} collective-permute-done((bf16[8,2,128,128]{3,2,1,0:T(8,128)(2,1)}, bf16[8,2,128,128]{3,2,1,0:T(8,128)(2,1)S(1)}, u32[]{:S(2)}, u32[]{:S(2)}) %collective-permute-start) | collective-permute-done | bytes 524320 | tf_op jit(solution)/shard_map/ppermute | solution.py:251
  27.6 1.6 %collective-permute-start.3 = (bf16[4,2,128,128]{3,2,1,0:T(8,128)(2,1)S(1)}, bf16[4,2,128,128]{3,2,1,0:T(8,128)(2,1)S(1)}, u32[]{:S(2)}, u32[]{:S(2)}) collective-permute-start(bf16[4,2,128,128]{3,2,1,0:T(8,128)(2,1)S(1)} %slice.94), channel_id=1, source_target_pairs={{0,64},{16,80},{32,96},{48,112},{64,128},{80,144},{96,160},{112,17... | collective-permute-start | bytes 786440 | tf_op jit(solution)/shard_map/ppermute | solution.py:260
  29.2 0.6 collective-permute-start.4
  29.8 0.8 copy.13
  30.7 2.8 %collective-permute-start.5 = (bf16[8,2,128,128]{3,2,1,0:T(8,128)(2,1)S(1)}, bf16[8,2,128,128]{3,2,1,0:T(8,128)(2,1)S(1)}, u32[]{:S(2)}, u32[]{:S(2)}) collective-permute-start(bf16[8,2,128,128]{3,2,1,0:T(8,128)(2,1)S(1)} %collective-permute-done.2.refs_6_), channel_id=1, source_target_pairs={{0,64},{16,80},{32,96},{48,112},{64,128},{80,144},{96,160},{112,17... | collective-permute-start | bytes 1572872 | tf_op jit(solution)/shard_map/ppermute | solution.py:263
  33.5 3.4 %collective-permute-done.3 = bf16[4,2,128,128]{3,2,1,0:T(8,128)(2,1)S(1)} collective-permute-done((bf16[4,2,128,128]{3,2,1,0:T(8,128)(2,1)S(1)}, bf16[4,2,128,128]{3,2,1,0:T(8,128)(2,1)S(1)}, u32[]{:S(2)}, u32[]{:S(2)}) %collective-permute-start.3) | collective-permute-done | bytes 262176 | tf_op jit(solution)/shard_map/ppermute | solution.py:260
  36.9 2.7 %collective-permute-done.4 = bf16[4,2,128,128]{3,2,1,0:T(8,128)(2,1)S(1)} collective-permute-done((bf16[4,2,128,128]{3,2,1,0:T(8,128)(2,1)S(1)}, bf16[4,2,128,128]{3,2,1,0:T(8,128)(2,1)S(1)}, u32[]{:S(2)}, u32[]{:S(2)}) %collective-permute-start.4) | collective-permute-done | bytes 262176 | tf_op jit(solution)/shard_map/ppermute | solution.py:261
  39.7 3.1 %collective-permute-start.7 = (bf16[8,2,128,128]{3,2,1,0:T(8,128)(2,1)S(1)}, bf16[8,2,128,128]{3,2,1,0:T(8,128)(2,1)S(1)}, u32[]{:S(2)}, u32[]{:S(2)}) collective-permute-start(bf16[8,2,128,128]{3,2,1,0:T(8,128)(2,1)S(1)} %constant_dynamic-update-slice_fusion.refs_7_), channel_id=1, source_target_pairs={{0,32},{16,48},{32,0},{48,16},{64,96},{80,112},{96,64},{112,80},{1... | collective-permute-start | bytes 1572872 | tf_op jit(solution)/shard_map/ppermute | solution.py:265
  43.0 0.6 fusion.6
  43.6 1.5 %collective-permute-done.5.refs_8_ = bf16[8,2,128,128]{3,2,1,0:T(8,128)(2,1)S(1)} collective-permute-done((bf16[8,2,128,128]{3,2,1,0:T(8,128)(2,1)S(1)}, bf16[8,2,128,128]{3,2,1,0:T(8,128)(2,1)S(1)}, u32[]{:S(2)}, u32[]{:S(2)}) %collective-permute-start.5) | collective-permute-done | bytes 524320 | tf_op jit(solution)/shard_map/ppermute | solution.py:263
  45.2 2.2 %collective-permute-done.6.refs_9_ = bf16[8,2,128,128]{3,2,1,0:T(8,128)(2,1)S(1)} collective-permute-done((bf16[8,2,128,128]{3,2,1,0:T(8,128)(2,1)S(1)}, bf16[8,2,128,128]{3,2,1,0:T(8,128)(2,1)S(1)}, u32[]{:S(2)}, u32[]{:S(2)}) %collective-permute-start.6) | collective-permute-done | bytes 524320 | tf_op jit(solution)/shard_map/ppermute | solution.py:264
  47.4 0.5 collective-permute-start.13
  48.0 7.6 %collective-permute-done.7.refs_10_ = bf16[8,2,128,128]{3,2,1,0:T(8,128)(2,1)S(1)} collective-permute-done((bf16[8,2,128,128]{3,2,1,0:T(8,128)(2,1)S(1)}, bf16[8,2,128,128]{3,2,1,0:T(8,128)(2,1)S(1)}, u32[]{:S(2)}, u32[]{:S(2)}) %collective-permute-start.7) | collective-permute-done | bytes 524320 | tf_op jit(solution)/shard_map/ppermute | solution.py:265
  55.8 0.6 broadcast_add_fusion.1.refs_0_
  56.4 0.6 xor_add_fusion.refs_1_
  57.1 0.7 copy-done.14
  58.2 0.8 copy-done.17
  59.0 16.0 %forward_and_rows.1 = (bf16[256,896]{1,0:T(8,128)(2,1)}, bf16[7,256,256]{2,1,0:T(8,128)(2,1)}, f32[8,2,16,4096]{3,2,1,0:T(8,128)}) custom-call(s32[2,128]{1,0:T(2,128)} %broadcast_add_fusion.1.refs_0_, s32[16]{0:T(128)} %xor_add_fusion.refs_1_, s32[1]{0:T(128)} %bitcast.refs_2_.low, bf16[8,2,128,128]{3,2,1,0:T(8,128)(2,1)} %bitcast.21, ...), custom_call_target="tpu_custom_call" | custom-call | flops 7516192768 | bytes 16777216 | tf_op jit(solution)/shard_map/forward_and_rows/pallas_call | solution.py:127
  75.0 12.1 %tile_sums.1 = (bf16[24,2,128,128]{3,2,1,0:T(8,128)(2,1)}, bf16[40,2,128,128]{3,2,1,0:T(8,128)(2,1)}, bf16[64,2,128,128]{3,2,1,0:T(8,128)(2,1)}) custom-call(s32[2,224]{1,0:T(2,128)} %get-tuple-element.55.target, s32[1]{0:T(128)} %bitcast.refs_2_.low, bf16[8,2,16,4096]{3,2,1,0:T(8,128)(2,1)} %bitcast.16, bf16[7,256,256]{2,1,0:T(8,128)(2,1)} %get-tuple-element.31.grads), custom_call_target="tpu_custom_call" | custom-call | flops 3758096384 | bytes 12582912 | tf_op jit(solution)/shard_map/tile_sums/pallas_call | solution.py:193
  87.2 0.8 collective-permute-start.18
  88.0 3.2 %collective-permute-done.18 = bf16[24,2,128,128]{3,2,1,0:T(8,128)(2,1)S(1)} collective-permute-done((bf16[24,2,128,128]{3,2,1,0:T(8,128)(2,1)}, bf16[24,2,128,128]{3,2,1,0:T(8,128)(2,1)S(1)}, u32[]{:S(2)}, u32[]{:S(2)}) %collective-permute-start.18) | collective-permute-done | bytes 1572896 | tf_op jit(solution)/shard_map/ppermute | solution.py:274
  91.3 1.9 %add_convert_fusion.4 = (bf16[8,2,128,128]{3,2,1,0:T(8,128)(2,1)S(1)}, bf16[8,2,128,128]{3,2,1,0:T(8,128)(2,1)S(1)}, bf16[8,2,128,128]{3,2,1,0:T(8,128)(2,1)S(1)}) fusion(bf16[24,2,128,128]{3,2,1,0:T(8,128)(2,1)S(1)} %collective-permute-done.18, bf16[64,2,128,128]{3,2,1,0:T(8,128)(2,1)} %get-tuple-element.32), kind=kLoop, calls=%fused_computation.5 | loop fusion | flops 3145728 | bytes 4718592 | tf_op jit(solution)/shard_map/convert_element_type | solution.py:281
  93.2 0.5 collective-permute-start.22
  93.7 3.0 %collective-permute-start.19 = (bf16[8,2,128,128]{3,2,1,0:T(8,128)(2,1)S(1)}, bf16[8,2,128,128]{3,2,1,0:T(8,128)(2,1)S(1)}, u32[]{:S(2)}, u32[]{:S(2)}) collective-permute-start(bf16[8,2,128,128]{3,2,1,0:T(8,128)(2,1)S(1)} %get-tuple-element.35), channel_id=1, source_target_pairs={{0,32},{16,48},{32,0},{48,16},{64,96},{80,112},{96,64},{112,80},{1... | collective-permute-start | bytes 1572872 | tf_op jit(solution)/shard_map/ppermute | solution.py:283
  96.9 1.9 %collective-permute-start.21 = (bf16[8,2,128,128]{3,2,1,0:T(8,128)(2,1)S(1)}, bf16[8,2,128,128]{3,2,1,0:T(8,128)(2,1)S(1)}, u32[]{:S(2)}, u32[]{:S(2)}) collective-permute-start(bf16[8,2,128,128]{3,2,1,0:T(8,128)(2,1)S(1)} %get-tuple-element.37), channel_id=1, source_target_pairs={{0,192},{16,208},{32,224},{48,240},{64,0},{80,16},{96,32},{112,48}... | collective-permute-start | bytes 1572872 | tf_op jit(solution)/shard_map/ppermute | solution.py:285
  98.8 10.4 %collective-permute-done.19 = bf16[8,2,128,128]{3,2,1,0:T(8,128)(2,1)S(1)} collective-permute-done((bf16[8,2,128,128]{3,2,1,0:T(8,128)(2,1)S(1)}, bf16[8,2,128,128]{3,2,1,0:T(8,128)(2,1)S(1)}, u32[]{:S(2)}, u32[]{:S(2)}) %collective-permute-start.19) | collective-permute-done | bytes 524320 | tf_op jit(solution)/shard_map/ppermute | solution.py:283
  109.2 1.3 collective-permute-done.20
  110.4 1.3 collective-permute-done.21
  111.7 1.4 add_convert_fusion.2
  113.5 1.7 %collective-permute-start.24 = (bf16[4,2,128,128]{3,2,1,0:T(8,128)(2,1)S(1)}, bf16[4,2,128,128]{3,2,1,0:T(8,128)(2,1)S(1)}, u32[]{:S(2)}, u32[]{:S(2)}) collective-permute-start(bf16[4,2,128,128]{3,2,1,0:T(8,128)(2,1)S(1)} %get-tuple-element.44), channel_id=1, source_target_pairs={{0,192},{16,208},{32,224},{48,240},{64,0},{80,16},{96,32},{112,48}... | collective-permute-start | bytes 786440 | tf_op jit(solution)/shard_map/ppermute | solution.py:295
  115.2 0.5 collective-permute-start.27
  115.7 4.7 %collective-permute-done.23 = bf16[4,2,128,128]{3,2,1,0:T(8,128)(2,1)S(1)} collective-permute-done((bf16[4,2,128,128]{3,2,1,0:T(8,128)(2,1)S(1)}, bf16[4,2,128,128]{3,2,1,0:T(8,128)(2,1)S(1)}, u32[]{:S(2)}, u32[]{:S(2)}) %collective-permute-start.23) | collective-permute-done | bytes 262176 | tf_op jit(solution)/shard_map/ppermute | solution.py:294
  120.4 1.5 %collective-permute-done.24 = bf16[4,2,128,128]{3,2,1,0:T(8,128)(2,1)S(1)} collective-permute-done((bf16[4,2,128,128]{3,2,1,0:T(8,128)(2,1)S(1)}, bf16[4,2,128,128]{3,2,1,0:T(8,128)(2,1)S(1)}, u32[]{:S(2)}, u32[]{:S(2)}) %collective-permute-start.24) | collective-permute-done | bytes 262176 | tf_op jit(solution)/shard_map/ppermute | solution.py:295
  122.0 1.4 add_convert_fusion
  123.6 1.7 %collective-permute-start.26 = (bf16[8,2,128,128]{3,2,1,0:T(8,128)(2,1)}, bf16[8,2,128,128]{3,2,1,0:T(8,128)(2,1)}, u32[]{:S(2)}, u32[]{:S(2)}) collective-permute-start(bf16[8,2,128,128]{3,2,1,0:T(8,128)(2,1)} %get-tuple-element.49), channel_id=1, source_target_pairs={{0,192},{16,208},{32,224},{48,240},{64,0},{80,16},{96,32},{112,48}... | collective-permute-start | bytes 1572872 | tf_op jit(solution)/shard_map/ppermute | solution.py:302
  125.4 3.8 %collective-permute-done.27 = bf16[8,2,128,128]{3,2,1,0:T(8,128)(2,1)S(1)} collective-permute-done((bf16[8,2,128,128]{3,2,1,0:T(8,128)(2,1)}, bf16[8,2,128,128]{3,2,1,0:T(8,128)(2,1)S(1)}, u32[]{:S(2)}, u32[]{:S(2)}) %collective-permute-start.27) | collective-permute-done | bytes 524320 | tf_op jit(solution)/shard_map/ppermute | solution.py:293
  129.2 6.5 %collective-permute-done.25 = bf16[8,2,128,128]{3,2,1,0:T(8,128)(2,1)} collective-permute-done((bf16[8,2,128,128]{3,2,1,0:T(8,128)(2,1)}, bf16[8,2,128,128]{3,2,1,0:T(8,128)(2,1)}, u32[]{:S(2)}, u32[]{:S(2)}) %collective-permute-start.25) | collective-permute-done | bytes 524320 | tf_op jit(solution)/shard_map/ppermute | solution.py:301
  135.8 1.5 collective-permute-done.26
  137.2 1.1 fusion.2
  138.4 0.8 collective-permute-start.17
  139.2 2.7 %multiply_bitcast_fusion = f32[1,8,2,128,128]{4,3,2,1,0:T(8,128)} fusion(bf16[8,2,128,128]{3,2,1,0:T(8,128)(2,1)} %collective-permute-done.26, bf16[8,2,128,128]{3,2,1,0:T(8,128)(2,1)} %collective-permute-done.25, bf16[8,2,128,128]{3,2,1,0:T(8,128)(2,1)S(1)} %collective-permute-done.27, bf16[40,2,128,128]{3,2,1,0:T(8,128)(2,1)S(1)} %collective-permute-done.22, ...), kind=kLoop, calls=%fused_computation | loop fusion | flops 2621440 | bytes 3670016 | tf_op jit(solution)/shard_map/broadcast_in_dim | solution.py:308
  142.0 1.5 collective-permute-done.17
  143.4 0.7 fusion
  (73 shorter events, 2.2 us)
Async XLA Ops:
  7.2 49.3 %copy-start.5 = (s32[16]{0:T(128)S(1)}, s32[16]{0:T(128)}, u32[]{:S(2)}) copy-start(s32[16]{0:T(128)} %constant.71.clone) | copy-start | bytes 196
  7.2 49.3 %copy-start.6 = (s32[16]{0:T(128)S(1)}, s32[16]{0:T(128)}, u32[]{:S(2)}) copy-start(s32[16]{0:T(128)} %constant.70.clone) | copy-start | bytes 196
  7.2 49.3 %copy-start.7 = (s32[16]{0:T(128)S(1)}, s32[16]{0:T(128)}, u32[]{:S(2)}) copy-start(s32[16]{0:T(128)} %constant.69.clone) | copy-start | bytes 196
  7.2 51.8 %all-gather.3.cloned.1.call-start = ((), (), s32[]{:S(2)}) async-start(), calls=%async_computation.2 | async-start | bytes 2359296 | tf_op jit(solution)/shard_map/all_gather | solution.py:254
  7.2 5.5 %collective-permute-start.16 = (bf16[16,4096]{1,0:T(8,128)(2,1)}, bf16[16,4096]{1,0:T(8,128)(2,1)S(1)}, u32[]{:S(2)}, u32[]{:S(2)}) collective-permute-start(bf16[16,4096]{1,0:T(8,128)(2,1)} %param.7), channel_id=1, source_target_pairs={{0,8},{1,9},{2,10},{3,11},{4,12},{5,13},{6,14},{7,15},{8,0},{9,1},... | collective-permute-start | bytes 393224 | tf_op jit(solution)/shard_map/ppermute | solution.py:249
  14.4 122.8 %reduce-scatter.2.cloned.1.call-start = ((), (), s32[]{:S(2)}) async-start(), calls=%async_computation.1 | async-start | bytes 4718592 | tf_op jit(solution)/shard_map/reduce_scatter | solution.py:271
  14.5 13.1 %collective-permute-start = (bf16[8,2,128,128]{3,2,1,0:T(8,128)(2,1)}, bf16[8,2,128,128]{3,2,1,0:T(8,128)(2,1)S(1)}, u32[]{:S(2)}, u32[]{:S(2)}) collective-permute-start(bf16[8,2,128,128]{3,2,1,0:T(8,128)(2,1)} %bitcast.17), channel_id=1, source_target_pairs={{0,64},{16,80},{32,96},{48,112},{64,128},{80,144},{96,160},{112,17... | collective-permute-start | bytes 1572872 | tf_op jit(solution)/shard_map/ppermute | solution.py:251
  16.5 12.7 %collective-permute-start.1 = (bf16[8,2,128,128]{3,2,1,0:T(8,128)(2,1)}, bf16[8,2,128,128]{3,2,1,0:T(8,128)(2,1)S(1)}, u32[]{:S(2)}, u32[]{:S(2)}) collective-permute-start(bf16[8,2,128,128]{3,2,1,0:T(8,128)(2,1)} %bitcast.18), channel_id=1, source_target_pairs={{0,192},{16,208},{32,224},{48,240},{64,0},{80,16},{96,32},{112,48}... | collective-permute-start | bytes 1572872 | tf_op jit(solution)/shard_map/ppermute | solution.py:252
  16.6 14.1 %collective-permute-start.2 = (bf16[8,2,128,128]{3,2,1,0:T(8,128)(2,1)}, bf16[8,2,128,128]{3,2,1,0:T(8,128)(2,1)S(1)}, u32[]{:S(2)}, u32[]{:S(2)}) collective-permute-start(bf16[8,2,128,128]{3,2,1,0:T(8,128)(2,1)} %bitcast.19), channel_id=1, source_target_pairs={{0,32},{16,48},{32,0},{48,16},{64,96},{80,112},{96,64},{112,80},{1... | collective-permute-start | bytes 1572872 | tf_op jit(solution)/shard_map/ppermute | solution.py:253
  19.8 19.9 %collective-permute-start.8 = (bf16[8,2,128,128]{3,2,1,0:T(8,128)(2,1)}, bf16[8,2,128,128]{3,2,1,0:T(8,128)(2,1)}, u32[]{:S(2)}, u32[]{:S(2)}) collective-permute-start(bf16[8,2,128,128]{3,2,1,0:T(8,128)(2,1)} %bitcast.20), channel_id=1, source_target_pairs={{0,16},{16,0},{32,48},{48,32},{64,80},{80,64},{96,112},{112,96},{1... | collective-permute-start | bytes 1572872 | tf_op jit(solution)/shard_map/ppermute | solution.py:267
  27.6 31.4 %copy-start.2 = (bf16[8,2,128,128]{3,2,1,0:T(8,128)(2,1)}, bf16[8,2,128,128]{3,2,1,0:T(8,128)(2,1)S(1)}, u32[]{:S(2)}) copy-start(bf16[8,2,128,128]{3,2,1,0:T(8,128)(2,1)S(1)} %collective-permute-done.refs_4_) | copy-start | bytes 1572868
  27.6 9.3 %collective-permute-start.3 = (bf16[4,2,128,128]{3,2,1,0:T(8,128)(2,1)S(1)}, bf16[4,2,128,128]{3,2,1,0:T(8,128)(2,1)S(1)}, u32[]{:S(2)}, u32[]{:S(2)}) collective-permute-start(bf16[4,2,128,128]{3,2,1,0:T(8,128)(2,1)S(1)} %slice.94), channel_id=1, source_target_pairs={{0,64},{16,80},{32,96},{48,112},{64,128},{80,144},{96,160},{112,17... | collective-permute-start | bytes 786440 | tf_op jit(solution)/shard_map/ppermute | solution.py:260
  29.2 29.8 %copy-start.3 = (bf16[8,2,128,128]{3,2,1,0:T(8,128)(2,1)}, bf16[8,2,128,128]{3,2,1,0:T(8,128)(2,1)S(1)}, u32[]{:S(2)}) copy-start(bf16[8,2,128,128]{3,2,1,0:T(8,128)(2,1)S(1)} %collective-permute-done.1.refs_5_) | copy-start | bytes 1572868
  29.2 10.4 %collective-permute-start.4 = (bf16[4,2,128,128]{3,2,1,0:T(8,128)(2,1)S(1)}, bf16[4,2,128,128]{3,2,1,0:T(8,128)(2,1)S(1)}, u32[]{:S(2)}, u32[]{:S(2)}) collective-permute-start(bf16[4,2,128,128]{3,2,1,0:T(8,128)(2,1)S(1)} %slice.95), channel_id=1, source_target_pairs={{0,192},{16,208},{32,224},{48,240},{64,0},{80,16},{96,32},{112,48}... | collective-permute-start | bytes 786440 | tf_op jit(solution)/shard_map/ppermute | solution.py:261
  30.7 28.3 %copy-start.8 = (bf16[8,2,128,128]{3,2,1,0:T(8,128)(2,1)}, bf16[8,2,128,128]{3,2,1,0:T(8,128)(2,1)S(1)}, u32[]{:S(2)}) copy-start(bf16[8,2,128,128]{3,2,1,0:T(8,128)(2,1)S(1)} %collective-permute-done.2.refs_6_) | copy-start | bytes 1572868
  30.7 14.4 %collective-permute-start.5 = (bf16[8,2,128,128]{3,2,1,0:T(8,128)(2,1)S(1)}, bf16[8,2,128,128]{3,2,1,0:T(8,128)(2,1)S(1)}, u32[]{:S(2)}, u32[]{:S(2)}) collective-permute-start(bf16[8,2,128,128]{3,2,1,0:T(8,128)(2,1)S(1)} %collective-permute-done.2.refs_6_), channel_id=1, source_target_pairs={{0,64},{16,80},{32,96},{48,112},{64,128},{80,144},{96,160},{112,17... | collective-permute-start | bytes 1572872 | tf_op jit(solution)/shard_map/ppermute | solution.py:263
  33.5 13.9 %collective-permute-start.6 = (bf16[8,2,128,128]{3,2,1,0:T(8,128)(2,1)S(1)}, bf16[8,2,128,128]{3,2,1,0:T(8,128)(2,1)S(1)}, u32[]{:S(2)}, u32[]{:S(2)}) collective-permute-start(bf16[8,2,128,128]{3,2,1,0:T(8,128)(2,1)S(1)} %collective-permute-done.2.refs_6_), channel_id=1, source_target_pairs={{0,192},{16,208},{32,224},{48,240},{64,0},{80,16},{96,32},{112,48}... | collective-permute-start | bytes 1572872 | tf_op jit(solution)/shard_map/ppermute | solution.py:264
  36.9 10.5 %collective-permute-start.9 = (bf16[8,2,128,128]{3,2,1,0:T(8,128)(2,1)S(1)}, bf16[8,2,128,128]{3,2,1,0:T(8,128)(2,1)S(1)}, u32[]{:S(2)}, u32[]{:S(2)}) collective-permute-start(bf16[8,2,128,128]{3,2,1,0:T(8,128)(2,1)S(1)} %collective-permute-done.refs_4_), channel_id=1, source_target_pairs={{0,16},{16,0},{32,48},{48,32},{64,80},{80,64},{96,112},{112,96},{1... | collective-permute-start | bytes 1572872 | tf_op jit(solution)/shard_map/ppermute | solution.py:267
  39.6 8.3 %collective-permute-start.10 = (bf16[8,2,128,128]{3,2,1,0:T(8,128)(2,1)S(1)}, bf16[8,2,128,128]{3,2,1,0:T(8,128)(2,1)S(1)}, u32[]{:S(2)}, u32[]{:S(2)}) collective-permute-start(bf16[8,2,128,128]{3,2,1,0:T(8,128)(2,1)S(1)} %collective-permute-done.1.refs_5_), channel_id=1, source_target_pairs={{0,16},{16,0},{32,48},{48,32},{64,80},{80,64},{96,112},{112,96},{1... | collective-permute-start | bytes 1572872 | tf_op jit(solution)/shard_map/ppermute | solution.py:267
  39.7 19.4 %copy-start.4 = (bf16[8,2,128,128]{3,2,1,0:T(8,128)(2,1)}, bf16[8,2,128,128]{3,2,1,0:T(8,128)(2,1)S(1)}, u32[]{:S(2)}) copy-start(bf16[8,2,128,128]{3,2,1,0:T(8,128)(2,1)S(1)} %constant_dynamic-update-slice_fusion.refs_7_) | copy-start | bytes 1572868
  39.7 15.9 %collective-permute-start.7 = (bf16[8,2,128,128]{3,2,1,0:T(8,128)(2,1)S(1)}, bf16[8,2,128,128]{3,2,1,0:T(8,128)(2,1)S(1)}, u32[]{:S(2)}, u32[]{:S(2)}) collective-permute-start(bf16[8,2,128,128]{3,2,1,0:T(8,128)(2,1)S(1)} %constant_dynamic-update-slice_fusion.refs_7_), channel_id=1, source_target_pairs={{0,32},{16,48},{32,0},{48,16},{64,96},{80,112},{96,64},{112,80},{1... | collective-permute-start | bytes 1572872 | tf_op jit(solution)/shard_map/ppermute | solution.py:265
  45.2 11.9 %copy-start.9 = (bf16[8,2,128,128]{3,2,1,0:T(8,128)(2,1)}, bf16[8,2,128,128]{3,2,1,0:T(8,128)(2,1)S(1)}, u32[]{:S(2)}) copy-start(bf16[8,2,128,128]{3,2,1,0:T(8,128)(2,1)S(1)} %collective-permute-done.5.refs_8_) | copy-start | bytes 1572868
  45.2 11.9 %collective-permute-start.11 = (bf16[8,2,128,128]{3,2,1,0:T(8,128)(2,1)S(1)}, bf16[8,2,128,128]{3,2,1,0:T(8,128)(2,1)S(1)}, u32[]{:S(2)}, u32[]{:S(2)}) collective-permute-start(bf16[8,2,128,128]{3,2,1,0:T(8,128)(2,1)S(1)} %collective-permute-done.2.refs_6_), channel_id=1, source_target_pairs={{0,16},{16,0},{32,48},{48,32},{64,80},{80,64},{96,112},{112,96},{1... | collective-permute-start | bytes 1572872 | tf_op jit(solution)/shard_map/ppermute | solution.py:267
  47.4 9.7 %copy-start.10 = (bf16[8,2,128,128]{3,2,1,0:T(8,128)(2,1)}, bf16[8,2,128,128]{3,2,1,0:T(8,128)(2,1)S(1)}, u32[]{:S(2)}) copy-start(bf16[8,2,128,128]{3,2,1,0:T(8,128)(2,1)S(1)} %collective-permute-done.6.refs_9_) | copy-start | bytes 1572868
  47.4 9.7 %collective-permute-start.12 = (bf16[8,2,128,128]{3,2,1,0:T(8,128)(2,1)S(1)}, bf16[8,2,128,128]{3,2,1,0:T(8,128)(2,1)S(1)}, u32[]{:S(2)}, u32[]{:S(2)}) collective-permute-start(bf16[8,2,128,128]{3,2,1,0:T(8,128)(2,1)S(1)} %constant_dynamic-update-slice_fusion.refs_7_), channel_id=1, source_target_pairs={{0,16},{16,0},{32,48},{48,32},{64,80},{80,64},{96,112},{112,96},{1... | collective-permute-start | bytes 1572872 | tf_op jit(solution)/shard_map/ppermute | solution.py:267
  47.4 9.7 %copy-start.11 = (bf16[8,2,128,128]{3,2,1,0:T(8,128)(2,1)}, bf16[8,2,128,128]{3,2,1,0:T(8,128)(2,1)S(1)}, u32[]{:S(2)}) copy-start(bf16[8,2,128,128]{3,2,1,0:T(8,128)(2,1)S(1)} %collective-permute-done.9.refs_12_) | copy-start | bytes 1572868
  47.4 9.7 %collective-permute-start.13 = (bf16[8,2,128,128]{3,2,1,0:T(8,128)(2,1)S(1)}, bf16[8,2,128,128]{3,2,1,0:T(8,128)(2,1)S(1)}, u32[]{:S(2)}, u32[]{:S(2)}) collective-permute-start(bf16[8,2,128,128]{3,2,1,0:T(8,128)(2,1)S(1)} %collective-permute-done.5.refs_8_), channel_id=1, source_target_pairs={{0,16},{16,0},{32,48},{48,32},{64,80},{80,64},{96,112},{112,96},{1... | collective-permute-start | bytes 1572872 | tf_op jit(solution)/shard_map/ppermute | solution.py:267
  47.9 11.1 %copy-start.12 = (bf16[8,2,128,128]{3,2,1,0:T(8,128)(2,1)}, bf16[8,2,128,128]{3,2,1,0:T(8,128)(2,1)S(1)}, u32[]{:S(2)}) copy-start(bf16[8,2,128,128]{3,2,1,0:T(8,128)(2,1)S(1)} %collective-permute-done.10.refs_13_) | copy-start | bytes 1572868
  47.9 9.2 %collective-permute-start.14 = (bf16[8,2,128,128]{3,2,1,0:T(8,128)(2,1)S(1)}, bf16[8,2,128,128]{3,2,1,0:T(8,128)(2,1)S(1)}, u32[]{:S(2)}, u32[]{:S(2)}) collective-permute-start(bf16[8,2,128,128]{3,2,1,0:T(8,128)(2,1)S(1)} %collective-permute-done.6.refs_9_), channel_id=1, source_target_pairs={{0,16},{16,0},{32,48},{48,32},{64,80},{80,64},{96,112},{112,96},{1... | collective-permute-start | bytes 1572872 | tf_op jit(solution)/shard_map/ppermute | solution.py:267
  55.6 1.5 copy-start.13
  55.6 3.4 %collective-permute-start.15 = (bf16[8,2,128,128]{3,2,1,0:T(8,128)(2,1)S(1)}, bf16[8,2,128,128]{3,2,1,0:T(8,128)(2,1)}, u32[]{:S(2)}, u32[]{:S(2)}) collective-permute-start(bf16[8,2,128,128]{3,2,1,0:T(8,128)(2,1)S(1)} %collective-permute-done.7.refs_10_), channel_id=1, source_target_pairs={{0,16},{16,0},{32,48},{48,32},{64,80},{80,64},{96,112},{112,96},{1... | collective-permute-start | bytes 1572872 | tf_op jit(solution)/shard_map/ppermute | solution.py:267
  57.0 0.8 copy-start.14
  57.0 1.0 copy-start.15
  57.1 1.1 copy-start.16
  58.2 0.8 copy-start.17
  87.2 24.5 %copy-start = (bf16[64,2,128,128]{3,2,1,0:T(8,128)(2,1)S(1)}, bf16[64,2,128,128]{3,2,1,0:T(8,128)(2,1)}, u32[]{:S(2)}) copy-start(bf16[64,2,128,128]{3,2,1,0:T(8,128)(2,1)} %get-tuple-element.32) | copy-start | bytes 12582916
  87.2 4.1 %collective-permute-start.18 = (bf16[24,2,128,128]{3,2,1,0:T(8,128)(2,1)}, bf16[24,2,128,128]{3,2,1,0:T(8,128)(2,1)S(1)}, u32[]{:S(2)}, u32[]{:S(2)}) collective-permute-start(bf16[24,2,128,128]{3,2,1,0:T(8,128)(2,1)} %get-tuple-element.33), channel_id=1, source_target_pairs={{0,16},{16,0},{32,48},{48,32},{64,80},{80,64},{96,112},{112,96},{1... | collective-permute-start | bytes 4718600 | tf_op jit(solution)/shard_map/ppermute | solution.py:274
  93.2 18.5 %collective-permute-start.22 = (bf16[40,2,128,128]{3,2,1,0:T(8,128)(2,1)}, bf16[40,2,128,128]{3,2,1,0:T(8,128)(2,1)S(1)}, u32[]{:S(2)}, u32[]{:S(2)}) collective-permute-start(bf16[40,2,128,128]{3,2,1,0:T(8,128)(2,1)} %get-tuple-element.38), channel_id=1, source_target_pairs={{0,16},{16,0},{32,48},{48,32},{64,80},{80,64},{96,112},{112,96},{1... | collective-permute-start | bytes 7864328 | tf_op jit(solution)/shard_map/ppermute | solution.py:286
  93.7 15.5 %collective-permute-start.19 = (bf16[8,2,128,128]{3,2,1,0:T(8,128)(2,1)S(1)}, bf16[8,2,128,128]{3,2,1,0:T(8,128)(2,1)S(1)}, u32[]{:S(2)}, u32[]{:S(2)}) collective-permute-start(bf16[8,2,128,128]{3,2,1,0:T(8,128)(2,1)S(1)} %get-tuple-element.35), channel_id=1, source_target_pairs={{0,32},{16,48},{32,0},{48,16},{64,96},{80,112},{96,64},{112,80},{1... | collective-permute-start | bytes 1572872 | tf_op jit(solution)/shard_map/ppermute | solution.py:283
  96.7 13.7 %collective-permute-start.20 = (bf16[8,2,128,128]{3,2,1,0:T(8,128)(2,1)S(1)}, bf16[8,2,128,128]{3,2,1,0:T(8,128)(2,1)S(1)}, u32[]{:S(2)}, u32[]{:S(2)}) collective-permute-start(bf16[8,2,128,128]{3,2,1,0:T(8,128)(2,1)S(1)} %get-tuple-element.36), channel_id=1, source_target_pairs={{0,64},{16,80},{32,96},{48,112},{64,128},{80,144},{96,160},{112,17... | collective-permute-start | bytes 1572872 | tf_op jit(solution)/shard_map/ppermute | solution.py:284
  96.9 14.8 %collective-permute-start.21 = (bf16[8,2,128,128]{3,2,1,0:T(8,128)(2,1)S(1)}, bf16[8,2,128,128]{3,2,1,0:T(8,128)(2,1)S(1)}, u32[]{:S(2)}, u32[]{:S(2)}) collective-permute-start(bf16[8,2,128,128]{3,2,1,0:T(8,128)(2,1)S(1)} %get-tuple-element.37), channel_id=1, source_target_pairs={{0,192},{16,208},{32,224},{48,240},{64,0},{80,16},{96,32},{112,48}... | collective-permute-start | bytes 1572872 | tf_op jit(solution)/shard_map/ppermute | solution.py:285
  113.1 7.3 %collective-permute-start.23 = (bf16[4,2,128,128]{3,2,1,0:T(8,128)(2,1)S(1)}, bf16[4,2,128,128]{3,2,1,0:T(8,128)(2,1)S(1)}, u32[]{:S(2)}, u32[]{:S(2)}) collective-permute-start(bf16[4,2,128,128]{3,2,1,0:T(8,128)(2,1)S(1)} %get-tuple-element.43), channel_id=1, source_target_pairs={{0,64},{16,80},{32,96},{48,112},{64,128},{80,144},{96,160},{112,17... | collective-permute-start | bytes 786440 | tf_op jit(solution)/shard_map/ppermute | solution.py:294
  113.5 8.5 %collective-permute-start.24 = (bf16[4,2,128,128]{3,2,1,0:T(8,128)(2,1)S(1)}, bf16[4,2,128,128]{3,2,1,0:T(8,128)(2,1)S(1)}, u32[]{:S(2)}, u32[]{:S(2)}) collective-permute-start(bf16[4,2,128,128]{3,2,1,0:T(8,128)(2,1)S(1)} %get-tuple-element.44), channel_id=1, source_target_pairs={{0,192},{16,208},{32,224},{48,240},{64,0},{80,16},{96,32},{112,48}... | collective-permute-start | bytes 786440 | tf_op jit(solution)/shard_map/ppermute | solution.py:295
  115.2 14.0 %collective-permute-start.27 = (bf16[8,2,128,128]{3,2,1,0:T(8,128)(2,1)}, bf16[8,2,128,128]{3,2,1,0:T(8,128)(2,1)S(1)}, u32[]{:S(2)}, u32[]{:S(2)}) collective-permute-start(bf16[8,2,128,128]{3,2,1,0:T(8,128)(2,1)} %get-tuple-element.50), channel_id=1, source_target_pairs={{0,32},{16,48},{32,0},{48,16},{64,96},{80,112},{96,64},{112,80},{1... | collective-permute-start | bytes 1572872 | tf_op jit(solution)/shard_map/ppermute | solution.py:293
  123.4 12.4 %collective-permute-start.25 = (bf16[8,2,128,128]{3,2,1,0:T(8,128)(2,1)}, bf16[8,2,128,128]{3,2,1,0:T(8,128)(2,1)}, u32[]{:S(2)}, u32[]{:S(2)}) collective-permute-start(bf16[8,2,128,128]{3,2,1,0:T(8,128)(2,1)} %get-tuple-element.48), channel_id=1, source_target_pairs={{0,64},{16,80},{32,96},{48,112},{64,128},{80,144},{96,160},{112,17... | collective-permute-start | bytes 1572872 | tf_op jit(solution)/shard_map/ppermute | solution.py:301
  123.6 13.6 %collective-permute-start.26 = (bf16[8,2,128,128]{3,2,1,0:T(8,128)(2,1)}, bf16[8,2,128,128]{3,2,1,0:T(8,128)(2,1)}, u32[]{:S(2)}, u32[]{:S(2)}) collective-permute-start(bf16[8,2,128,128]{3,2,1,0:T(8,128)(2,1)} %get-tuple-element.49), channel_id=1, source_target_pairs={{0,192},{16,208},{32,224},{48,240},{64,0},{80,16},{96,32},{112,48}... | collective-permute-start | bytes 1572872 | tf_op jit(solution)/shard_map/ppermute | solution.py:302
  137.2 6.2 %copy-start.1 = (f32[1,2,16,4096]{3,2,1,0:T(8,128)S(1)}, f32[1,2,16,4096]{3,2,1,0:T(8,128)}, u32[]{:S(2)}) copy-start(f32[1,2,16,4096]{3,2,1,0:T(8,128)} %reduce-scatter.2.cloned.1.call-done) | copy-start | bytes 1572868
  138.4 5.1 %collective-permute-start.17 = (bf16[16,4096]{1,0:T(8,128)(2,1)S(1)}, bf16[16,4096]{1,0:T(8,128)(2,1)S(1)}, u32[]{:S(2)}, u32[]{:S(2)}) collective-permute-start(bf16[16,4096]{1,0:T(8,128)(2,1)S(1)} %fusion.2), channel_id=1, source_target_pairs={{0,8},{1,9},{2,10},{3,11},{4,12},{5,13},{6,14},{7,15},{8,0},{9,1},... | collective-permute-start | bytes 393224 | tf_op jit(solution)/shard_map/ppermute | solution.py:312
Sparse Core Ops, SparseCore 0:
  14.6 44.2 all-gather.2
  75.2 57.9 reduce-scatter.1

commit v3 on v2

--- a/solution.py
+++ b/solution.py
@@ -41,6 +41,7 @@
 EARLY = 3 * PER
 HALF = len(BLOCKS) * PER
 PIECES = 2 * len(BLOCKS)
+SPAN = 512
 VMEM_LIMIT = 58 * 1024 * 1024
 
 
@@ -151,7 +152,8 @@
 
 
 def tile_kernel(
-    target, low, gathered, grads, early_out, late_out, keep_out, tokens, turned, tiles, row_sems, sems
+    target, ready, spots, low, gathered, grads, early_out, late_out, keep_out,
+    tokens, turned, tiles, row_sems, sems,
 ):
     row_copies = start_rows(low, gathered, tokens, row_sems)
     tiles[...] = jnp.zeros_like(tiles)
@@ -159,33 +161,37 @@
         copy.wait()
     for r in range(0, WIDTH, 512):
         turned[r:r + 512, :] = tokens[:, r:r + 512].T
-    span = 256
-
-    def column(c, unused):
-        for part in range(WIDTH // span):
+    outs = [(early_out, 0, EARLY), (late_out, EARLY, HALF - EARLY), (keep_out, HALF, HALF)]
+
+    def send_block(k, unused):
+        spot = pl.multiple_of(spots[k], PER)
+        for i, (out, first, count) in enumerate(outs):
+            @pl.when((spot >= first) & (spot < first + count))
+            def _():
+                pltpu.make_async_copy(
+                    tiles.at[pl.ds(spot, PER)], out.at[pl.ds(spot - first, PER)], sems.at[i]
+                ).start()
+        return unused
+
+    def chunk(part, done):
+        rows = pl.ds(pl.multiple_of(part * SPAN, SPAN), SPAN)
+        for c in range(COLS):
             total = jnp.dot(
-                turned[part * span:(part + 1) * span, :], grads[c],
-                preferred_element_type=jnp.float32,
+                turned[rows, :], grads[c], preferred_element_type=jnp.float32
             ).astype(jnp.bfloat16)
-            for i in range(span // TILE):
+            for i in range(SPAN // TILE):
                 for m in range(2):
-                    spot = target[m, (part * (span // TILE) + i) * COLS + c]
+                    spot = target[m, (part * (SPAN // TILE) + i) * COLS + c]
                     tiles[spot, m] = total[i * TILE:(i + 1) * TILE, m * TILE:(m + 1) * TILE]
-        return unused
-
-    lax.fori_loop(0, COLS, column, 0)
-    copies = [
-        pltpu.make_async_copy(tiles.at[pl.ds(0, EARLY)], early_out, sems.at[0]),
-        pltpu.make_async_copy(tiles.at[pl.ds(EARLY, HALF - EARLY)], late_out, sems.at[1]),
-        pltpu.make_async_copy(tiles.at[pl.ds(HALF, HALF)], keep_out, sems.at[2]),
-    ]
-    for copy in copies:
-        copy.start()
-    for copy in copies:
-        copy.wait()
-
-
-def tile_work(target, low, gathered, grads):
+        lax.fori_loop(done, ready[part], send_block, 0)
+        return ready[part]
+
+    lax.fori_loop(0, WIDTH // SPAN, chunk, 0)
+    for i, (out, first, count) in enumerate(outs):
+        pltpu.make_async_copy(tiles.at[pl.ds(first, count)], out, sems.at[i]).wait()
+
+
+def tile_work(target, ready, spots, low, gathered, grads):
     smem = pl.BlockSpec(memory_space=pltpu.SMEM)
     vmem = pl.BlockSpec(memory_space=pltpu.VMEM)
     hbm = pl.BlockSpec(memory_space=pl.ANY)
@@ -195,7 +201,7 @@
         out_shape=tuple(
             jax.ShapeDtypeStruct((n, 2, TILE, TILE), bf16) for n in (EARLY, HALF - EARLY, HALF)
         ),
-        in_specs=[smem] * 2 + [hbm, vmem],
+        in_specs=[smem] * 4 + [hbm, vmem],
         out_specs=(hbm,) * 3,
         scratch_shapes=[
             pltpu.VMEM((GROUP, WIDTH), bf16),
@@ -209,27 +215,34 @@
             flops=2 * GROUP * WIDTH * 2 * HIDE, bytes_accessed=12 << 20, transcendentals=0
         ),
         name="tile_sums",
-    )(target, low, gathered, grads)
+    )(target, ready, spots, low, gathered, grads)
 
 
 def tables(keep_local, x, y, c):
     keep = keep_local.reshape(2, ROWS * COLS)
-    spots = jnp.arange(ROWS * COLS, dtype=jnp.int32)
-    order = jnp.sum(jnp.where(spots[None, :] <= spots[:, None], keep[:, None, :], 0), axis=2) - 1
-    dense_spot = (spots % COLS) * ROWS + spots // COLS
+    places = jnp.arange(ROWS * COLS, dtype=jnp.int32)
+    order = jnp.sum(jnp.where(places[None, :] <= places[:, None], keep[:, None, :], 0), axis=2) - 1
+    dense_spot = (places % COLS) * ROWS + places // COLS
     slots = jnp.arange(CAP, dtype=jnp.int32)
     match = (order[:, None, :] == slots[None, :, None]) & (keep[:, None, :] == 1)
     place = DEAD + jnp.sum(jnp.where(match, dense_spot - DEAD, 0), axis=2)
-    owner = order >> 3
-    dx = ((owner >> 2) - x) & (XS - 1)
-    dy = ((owner >> 1) & 1) ^ y
-    dc = (owner & 1) ^ c
-    block = jnp.zeros_like(owner)
-    for (a, b), at in BLOCKS.items():
-        block = jnp.where((dx == a) & (dy == b), at, block)
-    target = ((1 - dc) * len(BLOCKS) + block) * PER + (order & (PER - 1))
-    target = jnp.where(keep == 1, target, CAP)
-    return place.astype(jnp.int32), target.astype(jnp.int32)
+
+    def spot_of(owner):
+        dx = ((owner >> 2) - x) & (XS - 1)
+        dy = ((owner >> 1) & 1) ^ y
+        dc = (owner & 1) ^ c
+        block = jnp.zeros_like(owner)
+        for (a, b), at in BLOCKS.items():
+            block = jnp.where((dx == a) & (dy == b), at, block)
+        return ((1 - dc) * len(BLOCKS) + block) * PER
+
+    target = jnp.where(keep == 1, spot_of(order >> 3) + (order & (PER - 1)), CAP)
+    spots = spot_of(jnp.arange(XS * YS * CS, dtype=jnp.int32))
+    chunks = jnp.arange(1, WIDTH // SPAN + 1, dtype=jnp.int32)
+    inside = places[None, :] < (chunks * (SPAN // TILE * COLS))[:, None]
+    counts = jnp.sum(jnp.where(inside[None], keep[:, None, :], 0), axis=2)
+    ready = jnp.where(chunks == WIDTH // SPAN, XS * YS * CS, jnp.min(counts, axis=0) >> 3)
+    return place.astype(jnp.int32), target.astype(jnp.int32), ready.astype(jnp.int32), spots
 
 
 def piece_ranks(x, y, c):
@@ -240,6 +253,22 @@
     return (((x + dx) & (XS - 1)) * YS + (y ^ dy)) * CS + (c ^ dc)
 
 
+def join_kernel(low, high, out):
+    out[:PER // 2] = low[...]
+    out[PER // 2:] = high[...]
+
+
+def join(low, high):
+    return pl.pallas_call(
+        join_kernel,
+        out_shape=jax.ShapeDtypeStruct((PER, 2, TILE, TILE), low.dtype),
+        in_specs=[pl.BlockSpec(memory_space=pltpu.VMEM)] * 2,
+        out_specs=pl.BlockSpec(memory_space=pltpu.VMEM),
+        cost_estimate=pl.CostEstimate(flops=20000000000, bytes_accessed=2 << 20, transcendentals=0),
+        name="join_halves",
+    )(low, high)
+
+
 def body(tokens, weight_tiles, keep_mask, cotangent):
     f32, bf16 = jnp.float32, jnp.bfloat16
     rank = lax.axis_index("dp")
@@ -251,15 +280,14 @@
     below = lax.ppermute(own, "dp", X_UP)
     above = lax.ppermute(own, "dp", X_DOWN)
     across = lax.ppermute(own, "dp", Y_SWAP)
-    gathered = lax.all_gather(
-        jnp.stack([tokens, other]), "tensor", axis=0, axis_index_groups=Z_RINGS
-    )
-    place, target = tables(keep_mask, x, y, c)
+    pair = jnp.stack([tokens, other])
+    gathered = lax.all_gather(pair, "tensor", axis=0, axis_index_groups=Z_RINGS)
+    place, target, ready, spots = lax.optimization_barrier(tables(keep_mask, x, y, c))
     ranks = piece_ranks(x, y, c)
     half = PER // 2
     far_low = lax.ppermute(below[:half], "dp", X_UP)
     far_high = lax.ppermute(above[half:], "dp", X_DOWN)
-    far = jnp.concatenate([far_low, far_high])
+    far = join(far_low, far_high)
     below_across = lax.ppermute(across, "dp", X_UP)
     above_across = lax.ppermute(across, "dp", X_DOWN)
     far_across = lax.ppermute(far, "dp", Y_SWAP)
@@ -269,7 +297,7 @@
 
     hidden, grads, rows = dense_work(place, ranks, low_table, pieces, gathered, cotangent)
     summed = lax.psum_scatter(rows, "tensor", scatter_dimension=0, axis_index_groups=Z_RINGS)
-    early, late, keep = tile_work(target, low_table, gathered, grads)
+    early, late, keep = tile_work(target, ready, spots, low_table, gathered, grads)
 
     early_in = lax.ppermute(early, "dp", C_SWAP)
 

time: 151 us -> 151 us (level)
  starting transfers between devices: 27.6 us -> 25.5 us
  local copies, waits for them, and re-layouts: 2.96 us -> 1.02 us
  waiting for transfers between devices: 64.9 us -> 66.6 us
    all_gather x1, waiting for transfers between devices: 0.01 us -> 4.51 us  [body(): gathered = lax.all_gather(pair, 'tensor', axis=0, axis_index_groups=Z_RINGS)]
    ppermute x1, waiting for transfers between devices: 3.87 us -> 0.01 us  [body(): other = lax.ppermute(tokens, 'tensor', L_SWAP)]
    ppermute x1, waiting for transfers between devices: 7.78 us -> 5.84 us  [body(): below = lax.ppermute(own, 'dp', X_UP)]
    unnamed x38 -> x29, local copies, waits for them, and re-layouts: 2.75 us -> 0.84 us
    pallas_call x0 -> x1, Pallas kernels: none -> 1.88 us  [join(): pl.pallas_call(join_kernel, out_shape=jax.ShapeDtypeStruct((PER, 2, TILE,...]
    ppermute x1, waiting for transfers between devices: 1.52 us -> 0.01 us  [body(): below_across = lax.ppermute(across, 'dp', X_UP)]
  transfers between devices with their start and end apart: 30 -> 30, of which waited for: 17 -> 18; matrix products, arithmetic and copies ran while one was open for 7% -> 9% of each run, Pallas kernels for 8% -> 9%
where the time goes in v3:
time: 151 us
  waiting for transfers between devices  66.6 us (44%)
  Pallas kernels  29 us (19%)
  starting transfers between devices  25.5 us (17%)
  other arithmetic  14.3 us (9%)
  between operations  14.2 us (9%)
    pallas_call x1, Pallas kernels, dense_work(): pl.pallas_call(dense_kernel, out_shape=(jax.ShapeDtypeStruct((GROUP, HIDE...  16 us
    pallas_call x1, Pallas kernels, tile_work(): pl.pallas_call(tile_kernel, out_shape=tuple((jax.ShapeDtypeStruct((n, 2,...  11.1 us
    ppermute x1, waiting for transfers between devices, body(): far_in = lax.ppermute(sends[0], 'dp', Y_SWAP)  10.5 us
    ppermute x1, waiting for transfers between devices, body(): far_across = lax.ppermute(far, 'dp', Y_SWAP)  8.91 us
    ppermute x1, waiting for transfers between devices, body(): up_last = lax.ppermute(sends[0], 'dp', X_UP)  6.54 us
    ppermute x1, waiting for transfers between devices, body(): below = lax.ppermute(own, 'dp', X_UP)  5.84 us
    ppermute x1, waiting for transfers between devices, body(): half_up = lax.ppermute(sends[1], 'dp', X_UP)  4.81 us
    all_gather x1, waiting for transfers between devices, body(): gathered = lax.all_gather(pair, 'tensor', axis=0, axis_index_groups=Z_RINGS)  4.51 us
  transfers between devices with their start and end apart: 30, of which 18 were waited for; matrix products, arithmetic and copies ran while one was open for 9% of the time, Pallas kernels for 9%

profile of v3, /device:TPU:6, one launch (start us, length us, event | category | flops | bytes accessed | tf_op | source)
XLA Modules:
  0.0 150.7 jit_solution(14236600237017587713)
XLA Ops:
  7.2 1.7 %collective-permute-start.16 = (bf16[16,4096]{1,0:T(8,128)(2,1)}, bf16[16,4096]{1,0:T(8,128)(2,1)S(1)}, u32[]{:S(2)}, u32[]{:S(2)}) collective-permute-start(bf16[16,4096]{1,0:T(8,128)(2,1)} %param.7), channel_id=1, source_target_pairs={{0,8},{1,9},{2,10},{3,11},{4,12},{5,13},{6,14},{7,15},{8,0},{9,1},... | collective-permute-start | bytes 393224 | tf_op jit(solution)/shard_map/ppermute | solution.py:278
  8.9 0.7 collective-permute-start
  9.6 1.3 collective-permute-start.1
  10.9 2.9 %collective-permute-start.2 = (bf16[8,2,128,128]{3,2,1,0:T(8,128)(2,1)}, bf16[8,2,128,128]{3,2,1,0:T(8,128)(2,1)S(1)}, u32[]{:S(2)}, u32[]{:S(2)}) collective-permute-start(bf16[8,2,128,128]{3,2,1,0:T(8,128)(2,1)} %bitcast.19), channel_id=1, source_target_pairs={{0,32},{16,48},{32,0},{48,16},{64,96},{80,112},{96,64},{112,80},{1... | collective-permute-start | bytes 1572872 | tf_op jit(solution)/shard_map/ppermute | solution.py:282
  13.8 1.6 %pad_maximum_fusion = bf16[2,16,4096]{2,1,0:T(8,128)(2,1)} fusion(bf16[1,16,4096]{2,1,0:T(8,128)(2,1)S(1)} %bitcast.14, bf16[1,16,4096]{2,1,0:T(8,128)(2,1)} %bitcast.13), kind=kLoop, calls=%fused_computation.9 | loop fusion | flops 131072 | bytes 524288 | tf_op jit(solution)/shard_map/stack | solution.py:283
  15.6 0.8 copy.13
  16.6 5.8 %collective-permute-done.refs_4_ = bf16[8,2,128,128]{3,2,1,0:T(8,128)(2,1)S(1)} collective-permute-done((bf16[8,2,128,128]{3,2,1,0:T(8,128)(2,1)}, bf16[8,2,128,128]{3,2,1,0:T(8,128)(2,1)S(1)}, u32[]{:S(2)}, u32[]{:S(2)}) %collective-permute-start) | collective-permute-done | bytes 524320 | tf_op jit(solution)/shard_map/ppermute | solution.py:280
  22.5 1.8 %collective-permute-start.3 = (bf16[4,2,128,128]{3,2,1,0:T(8,128)(2,1)S(1)}, bf16[4,2,128,128]{3,2,1,0:T(8,128)(2,1)S(1)}, u32[]{:S(2)}, u32[]{:S(2)}) collective-permute-start(bf16[4,2,128,128]{3,2,1,0:T(8,128)(2,1)S(1)} %slice.94), channel_id=1, source_target_pairs={{0,64},{16,80},{32,96},{48,112},{64,128},{80,144},{96,160},{112,17... | collective-permute-start | bytes 786440 | tf_op jit(solution)/shard_map/ppermute | solution.py:288
  25.0 1.5 collective-permute-done.2.refs_6_
  26.4 1.5 %collective-permute-start.5 = (bf16[8,2,128,128]{3,2,1,0:T(8,128)(2,1)S(1)}, bf16[8,2,128,128]{3,2,1,0:T(8,128)(2,1)S(1)}, u32[]{:S(2)}, u32[]{:S(2)}) collective-permute-start(bf16[8,2,128,128]{3,2,1,0:T(8,128)(2,1)S(1)} %collective-permute-done.2.refs_6_), channel_id=1, source_target_pairs={{0,64},{16,80},{32,96},{48,112},{64,128},{80,144},{96,160},{112,17... | collective-permute-start | bytes 1572872 | tf_op jit(solution)/shard_map/ppermute | solution.py:291
  28.0 0.5 collective-permute-start.6
  28.5 2.4 %collective-permute-done.3.low = bf16[4,2,128,128]{3,2,1,0:T(8,128)(2,1)S(1)} collective-permute-done((bf16[4,2,128,128]{3,2,1,0:T(8,128)(2,1)S(1)}, bf16[4,2,128,128]{3,2,1,0:T(8,128)(2,1)S(1)}, u32[]{:S(2)}, u32[]{:S(2)}) %collective-permute-start.3) | collective-permute-done | bytes 262176 | tf_op jit(solution)/shard_map/ppermute | solution.py:288
  30.9 3.8 %collective-permute-done.4.high = bf16[4,2,128,128]{3,2,1,0:T(8,128)(2,1)} collective-permute-done((bf16[4,2,128,128]{3,2,1,0:T(8,128)(2,1)S(1)}, bf16[4,2,128,128]{3,2,1,0:T(8,128)(2,1)}, u32[]{:S(2)}, u32[]{:S(2)}) %collective-permute-start.4) | collective-permute-done | bytes 262176 | tf_op jit(solution)/shard_map/ppermute | solution.py:289
  34.7 1.9 %join_halves.1.refs_7_ = bf16[8,2,128,128]{3,2,1,0:T(8,128)(2,1)} custom-call(bf16[4,2,128,128]{3,2,1,0:T(8,128)(2,1)} %copy-done.13, bf16[4,2,128,128]{3,2,1,0:T(8,128)(2,1)} %collective-permute-done.4.high), custom_call_target="tpu_custom_call" | custom-call | flops 20000000000 | bytes 2097152 | tf_op jit(solution)/shard_map/join_halves/pallas_call | solution.py:262
  36.6 3.1 %collective-permute-start.7 = (bf16[8,2,128,128]{3,2,1,0:T(8,128)(2,1)}, bf16[8,2,128,128]{3,2,1,0:T(8,128)(2,1)}, u32[]{:S(2)}, u32[]{:S(2)}) collective-permute-start(bf16[8,2,128,128]{3,2,1,0:T(8,128)(2,1)} %join_halves.1.refs_7_), channel_id=1, source_target_pairs={{0,32},{16,48},{32,0},{48,16},{64,96},{80,112},{96,64},{112,80},{1... | collective-permute-start | bytes 1572872 | tf_op jit(solution)/shard_map/ppermute | solution.py:293
  39.7 0.6 fusion.6
  40.5 0.5 compare_select_fusion.ready
  41.4 1.9 %collective-permute-done.6.refs_9_ = bf16[8,2,128,128]{3,2,1,0:T(8,128)(2,1)} collective-permute-done((bf16[8,2,128,128]{3,2,1,0:T(8,128)(2,1)S(1)}, bf16[8,2,128,128]{3,2,1,0:T(8,128)(2,1)}, u32[]{:S(2)}, u32[]{:S(2)}) %collective-permute-start.6) | collective-permute-done | bytes 524320 | tf_op jit(solution)/shard_map/ppermute | solution.py:292
  43.3 0.5 collective-permute-start.13
  43.9 8.9 %collective-permute-done.7.refs_10_ = bf16[8,2,128,128]{3,2,1,0:T(8,128)(2,1)} collective-permute-done((bf16[8,2,128,128]{3,2,1,0:T(8,128)(2,1)}, bf16[8,2,128,128]{3,2,1,0:T(8,128)(2,1)}, u32[]{:S(2)}, u32[]{:S(2)}) %collective-permute-start.7) | collective-permute-done | bytes 524320 | tf_op jit(solution)/shard_map/ppermute | solution.py:293
  52.8 0.5 fusion.16.spots
  53.3 0.6 broadcast_add_fusion.1.refs_0_
  53.9 0.6 xor_add_fusion.refs_1_
  54.6 0.5 collective-permute-done.15.refs_18_
  55.1 4.5 %all-gather.3.cloned.1.call-done = bf16[16,16,4096]{2,1,0:T(8,128)(2,1)} async-done(((bf16[2,16,4096]{2,1,0:T(8,128)(2,1)}), bf16[16,16,4096]{2,1,0:T(8,128)(2,1)}) %all-gather.3.cloned.1.call-update) | async-done | bytes 2097168 | tf_op jit(solution)/shard_map/all_gather | solution.py:284
  59.6 16.0 %forward_and_rows.1 = (bf16[256,896]{1,0:T(8,128)(2,1)}, bf16[7,256,256]{2,1,0:T(8,128)(2,1)}, f32[8,2,16,4096]{3,2,1,0:T(8,128)}) custom-call(s32[2,128]{1,0:T(2,128)} %broadcast_add_fusion.1.refs_0_, s32[16]{0:T(128)} %xor_add_fusion.refs_1_, s32[1]{0:T(128)} %bitcast.refs_2_.low, bf16[8,2,128,128]{3,2,1,0:T(8,128)(2,1)} %bitcast.21, ...), custom_call_target="tpu_custom_call" | custom-call | flops 7516192768 | bytes 16777216 | tf_op jit(solution)/shard_map/forward_and_rows/pallas_call | solution.py:128
  75.7 11.1 %tile_sums.1 = (bf16[24,2,128,128]{3,2,1,0:T(8,128)(2,1)}, bf16[40,2,128,128]{3,2,1,0:T(8,128)(2,1)}, bf16[64,2,128,128]{3,2,1,0:T(8,128)(2,1)}) custom-call(s32[2,224]{1,0:T(2,128)} %get-tuple-element.36.target, s32[8]{0:T(128)} %compare_select_fusion.ready, s32[16]{0:T(128)} %fusion.16.spots, s32[1]{0:T(128)} %bitcast.refs_2_.low, ...), custom_call_target="tpu_custom_call" | custom-call | flops 3758096384 | bytes 12582912 | tf_op jit(solution)/shard_map/tile_sums/pallas_call | solution.py:199
  87.1 3.6 %collective-permute-done.18 = bf16[24,2,128,128]{3,2,1,0:T(8,128)(2,1)S(1)} collective-permute-done((bf16[24,2,128,128]{3,2,1,0:T(8,128)(2,1)}, bf16[24,2,128,128]{3,2,1,0:T(8,128)(2,1)S(1)}, u32[]{:S(2)}, u32[]{:S(2)}) %collective-permute-start.18) | collective-permute-done | bytes 1572896 | tf_op jit(solution)/shard_map/ppermute | solution.py:302
  90.7 1.9 %add_convert_fusion.4 = (bf16[8,2,128,128]{3,2,1,0:T(8,128)(2,1)S(1)}, bf16[8,2,128,128]{3,2,1,0:T(8,128)(2,1)S(1)}, bf16[8,2,128,128]{3,2,1,0:T(8,128)(2,1)S(1)}) fusion(bf16[24,2,128,128]{3,2,1,0:T(8,128)(2,1)S(1)} %collective-permute-done.18, bf16[64,2,128,128]{3,2,1,0:T(8,128)(2,1)} %get-tuple-element.40), kind=kLoop, calls=%fused_computation.5 | loop fusion | flops 3145728 | bytes 4718592 | tf_op jit(solution)/shard_map/convert_element_type | solution.py:309
  92.8 3.2 %collective-permute-start.19 = (bf16[8,2,128,128]{3,2,1,0:T(8,128)(2,1)S(1)}, bf16[8,2,128,128]{3,2,1,0:T(8,128)(2,1)S(1)}, u32[]{:S(2)}, u32[]{:S(2)}) collective-permute-start(bf16[8,2,128,128]{3,2,1,0:T(8,128)(2,1)S(1)} %get-tuple-element.43), channel_id=1, source_target_pairs={{0,32},{16,48},{32,0},{48,16},{64,96},{80,112},{96,64},{112,80},{1... | collective-permute-start | bytes 1572872 | tf_op jit(solution)/shard_map/ppermute | solution.py:311
  96.0 0.6 collective-permute-start.20
  96.6 1.5 collective-permute-start.21
  98.1 10.5 %collective-permute-done.19 = bf16[8,2,128,128]{3,2,1,0:T(8,128)(2,1)S(1)} collective-permute-done((bf16[8,2,128,128]{3,2,1,0:T(8,128)(2,1)S(1)}, bf16[8,2,128,128]{3,2,1,0:T(8,128)(2,1)S(1)}, u32[]{:S(2)}, u32[]{:S(2)}) %collective-permute-start.19) | collective-permute-done | bytes 524320 | tf_op jit(solution)/shard_map/ppermute | solution.py:311
  108.5 1.4 collective-permute-done.20
  109.9 1.5 collective-permute-done.21
  111.4 1.4 add_convert_fusion.2
  113.2 1.7 %collective-permute-start.24 = (bf16[4,2,128,128]{3,2,1,0:T(8,128)(2,1)S(1)}, bf16[4,2,128,128]{3,2,1,0:T(8,128)(2,1)S(1)}, u32[]{:S(2)}, u32[]{:S(2)}) collective-permute-start(bf16[4,2,128,128]{3,2,1,0:T(8,128)(2,1)S(1)} %get-tuple-element.52), channel_id=1, source_target_pairs={{0,192},{16,208},{32,224},{48,240},{64,0},{80,16},{96,32},{112,48}... | collective-permute-start | bytes 786440 | tf_op jit(solution)/shard_map/ppermute | solution.py:323
  115.3 4.8 %collective-permute-done.23 = bf16[4,2,128,128]{3,2,1,0:T(8,128)(2,1)S(1)} collective-permute-done((bf16[4,2,128,128]{3,2,1,0:T(8,128)(2,1)S(1)}, bf16[4,2,128,128]{3,2,1,0:T(8,128)(2,1)S(1)}, u32[]{:S(2)}, u32[]{:S(2)}) %collective-permute-start.23) | collective-permute-done | bytes 262176 | tf_op jit(solution)/shard_map/ppermute | solution.py:322
  120.1 1.5 %collective-permute-done.24 = bf16[4,2,128,128]{3,2,1,0:T(8,128)(2,1)S(1)} collective-permute-done((bf16[4,2,128,128]{3,2,1,0:T(8,128)(2,1)S(1)}, bf16[4,2,128,128]{3,2,1,0:T(8,128)(2,1)S(1)}, u32[]{:S(2)}, u32[]{:S(2)}) %collective-permute-start.24) | collective-permute-done | bytes 262176 | tf_op jit(solution)/shard_map/ppermute | solution.py:323
  121.7 1.4 add_convert_fusion
  123.4 1.7 %collective-permute-start.26 = (bf16[8,2,128,128]{3,2,1,0:T(8,128)(2,1)}, bf16[8,2,128,128]{3,2,1,0:T(8,128)(2,1)}, u32[]{:S(2)}, u32[]{:S(2)}) collective-permute-start(bf16[8,2,128,128]{3,2,1,0:T(8,128)(2,1)} %get-tuple-element.57), channel_id=1, source_target_pairs={{0,192},{16,208},{32,224},{48,240},{64,0},{80,16},{96,32},{112,48}... | collective-permute-start | bytes 1572872 | tf_op jit(solution)/shard_map/ppermute | solution.py:330
  125.1 3.8 %collective-permute-done.27 = bf16[8,2,128,128]{3,2,1,0:T(8,128)(2,1)S(1)} collective-permute-done((bf16[8,2,128,128]{3,2,1,0:T(8,128)(2,1)}, bf16[8,2,128,128]{3,2,1,0:T(8,128)(2,1)S(1)}, u32[]{:S(2)}, u32[]{:S(2)}) %collective-permute-start.27) | collective-permute-done | bytes 524320 | tf_op jit(solution)/shard_map/ppermute | solution.py:321
  128.9 6.5 %collective-permute-done.25 = bf16[8,2,128,128]{3,2,1,0:T(8,128)(2,1)} collective-permute-done((bf16[8,2,128,128]{3,2,1,0:T(8,128)(2,1)}, bf16[8,2,128,128]{3,2,1,0:T(8,128)(2,1)}, u32[]{:S(2)}, u32[]{:S(2)}) %collective-permute-start.25) | collective-permute-done | bytes 524320 | tf_op jit(solution)/shard_map/ppermute | solution.py:329
  135.5 1.5 collective-permute-done.26
  137.0 1.1 fusion.2
  138.3 2.7 %multiply_bitcast_fusion = f32[1,8,2,128,128]{4,3,2,1,0:T(8,128)} fusion(bf16[8,2,128,128]{3,2,1,0:T(8,128)(2,1)} %collective-permute-done.26, bf16[8,2,128,128]{3,2,1,0:T(8,128)(2,1)} %collective-permute-done.25, bf16[8,2,128,128]{3,2,1,0:T(8,128)(2,1)S(1)} %collective-permute-done.27, bf16[40,2,128,128]{3,2,1,0:T(8,128)(2,1)S(1)} %collective-permute-done.22, ...), kind=kLoop, calls=%fused_computation | loop fusion | flops 2621440 | bytes 3670016 | tf_op jit(solution)/shard_map/broadcast_in_dim | solution.py:336
  141.1 2.1 %collective-permute-done.17 = bf16[16,4096]{1,0:T(8,128)(2,1)S(1)} collective-permute-done((bf16[16,4096]{1,0:T(8,128)(2,1)S(1)}, bf16[16,4096]{1,0:T(8,128)(2,1)S(1)}, u32[]{:S(2)}, u32[]{:S(2)}) %collective-permute-start.17) | collective-permute-done | bytes 131104 | tf_op jit(solution)/shard_map/ppermute | solution.py:340
  143.1 0.7 fusion
  (70 shorter events, 3.7 us)
Async XLA Ops:
  7.2 52.4 %all-gather.3.cloned.1.call-start = ((), (), s32[]{:S(2)}) async-start(), calls=%async_computation.2 | async-start | bytes 2359296 | tf_op jit(solution)/shard_map/all_gather | solution.py:284
  7.2 6.6 %collective-permute-start.16 = (bf16[16,4096]{1,0:T(8,128)(2,1)}, bf16[16,4096]{1,0:T(8,128)(2,1)S(1)}, u32[]{:S(2)}, u32[]{:S(2)}) collective-permute-start(bf16[16,4096]{1,0:T(8,128)(2,1)} %param.7), channel_id=1, source_target_pairs={{0,8},{1,9},{2,10},{3,11},{4,12},{5,13},{6,14},{7,15},{8,0},{9,1},... | collective-permute-start | bytes 393224 | tf_op jit(solution)/shard_map/ppermute | solution.py:278
  8.9 13.6 %collective-permute-start = (bf16[8,2,128,128]{3,2,1,0:T(8,128)(2,1)}, bf16[8,2,128,128]{3,2,1,0:T(8,128)(2,1)S(1)}, u32[]{:S(2)}, u32[]{:S(2)}) collective-permute-start(bf16[8,2,128,128]{3,2,1,0:T(8,128)(2,1)} %bitcast.17), channel_id=1, source_target_pairs={{0,64},{16,80},{32,96},{48,112},{64,128},{80,144},{96,160},{112,17... | collective-permute-start | bytes 1572872 | tf_op jit(solution)/shard_map/ppermute | solution.py:280
  9.6 14.7 %collective-permute-start.1 = (bf16[8,2,128,128]{3,2,1,0:T(8,128)(2,1)}, bf16[8,2,128,128]{3,2,1,0:T(8,128)(2,1)S(1)}, u32[]{:S(2)}, u32[]{:S(2)}) collective-permute-start(bf16[8,2,128,128]{3,2,1,0:T(8,128)(2,1)} %bitcast.18), channel_id=1, source_target_pairs={{0,192},{16,208},{32,224},{48,240},{64,0},{80,16},{96,32},{112,48}... | collective-permute-start | bytes 1572872 | tf_op jit(solution)/shard_map/ppermute | solution.py:281
  10.9 15.5 %collective-permute-start.2 = (bf16[8,2,128,128]{3,2,1,0:T(8,128)(2,1)}, bf16[8,2,128,128]{3,2,1,0:T(8,128)(2,1)S(1)}, u32[]{:S(2)}, u32[]{:S(2)}) collective-permute-start(bf16[8,2,128,128]{3,2,1,0:T(8,128)(2,1)} %bitcast.19), channel_id=1, source_target_pairs={{0,32},{16,48},{32,0},{48,16},{64,96},{80,112},{96,64},{112,80},{1... | collective-permute-start | bytes 1572872 | tf_op jit(solution)/shard_map/ppermute | solution.py:282
  13.8 22.8 %collective-permute-start.8 = (bf16[8,2,128,128]{3,2,1,0:T(8,128)(2,1)}, bf16[8,2,128,128]{3,2,1,0:T(8,128)(2,1)S(1)}, u32[]{:S(2)}, u32[]{:S(2)}) collective-permute-start(bf16[8,2,128,128]{3,2,1,0:T(8,128)(2,1)} %bitcast.20), channel_id=1, source_target_pairs={{0,16},{16,0},{32,48},{48,32},{64,80},{80,64},{96,112},{112,96},{1... | collective-permute-start | bytes 1572872 | tf_op jit(solution)/shard_map/ppermute | solution.py:295
  15.5 121.5 %reduce-scatter.2.cloned.1.call-start = ((), (), s32[]{:S(2)}) async-start(), calls=%async_computation.1 | async-start | bytes 4718592 | tf_op jit(solution)/shard_map/reduce_scatter | solution.py:299
  22.5 14.1 %copy-start.2 = (bf16[8,2,128,128]{3,2,1,0:T(8,128)(2,1)}, bf16[8,2,128,128]{3,2,1,0:T(8,128)(2,1)S(1)}, u32[]{:S(2)}) copy-start(bf16[8,2,128,128]{3,2,1,0:T(8,128)(2,1)S(1)} %collective-permute-done.refs_4_) | copy-start | bytes 1572868
  22.5 8.4 %collective-permute-start.3 = (bf16[4,2,128,128]{3,2,1,0:T(8,128)(2,1)S(1)}, bf16[4,2,128,128]{3,2,1,0:T(8,128)(2,1)S(1)}, u32[]{:S(2)}, u32[]{:S(2)}) collective-permute-start(bf16[4,2,128,128]{3,2,1,0:T(8,128)(2,1)S(1)} %slice.94), channel_id=1, source_target_pairs={{0,64},{16,80},{32,96},{48,112},{64,128},{80,144},{96,160},{112,17... | collective-permute-start | bytes 786440 | tf_op jit(solution)/shard_map/ppermute | solution.py:288
  24.3 12.3 %copy-start.3 = (bf16[8,2,128,128]{3,2,1,0:T(8,128)(2,1)}, bf16[8,2,128,128]{3,2,1,0:T(8,128)(2,1)S(1)}, u32[]{:S(2)}) copy-start(bf16[8,2,128,128]{3,2,1,0:T(8,128)(2,1)S(1)} %collective-permute-done.1.refs_5_) | copy-start | bytes 1572868
  24.3 10.4 %collective-permute-start.4 = (bf16[4,2,128,128]{3,2,1,0:T(8,128)(2,1)S(1)}, bf16[4,2,128,128]{3,2,1,0:T(8,128)(2,1)}, u32[]{:S(2)}, u32[]{:S(2)}) collective-permute-start(bf16[4,2,128,128]{3,2,1,0:T(8,128)(2,1)S(1)} %slice.95), channel_id=1, source_target_pairs={{0,192},{16,208},{32,224},{48,240},{64,0},{80,16},{96,32},{112,48}... | collective-permute-start | bytes 786440 | tf_op jit(solution)/shard_map/ppermute | solution.py:289
  24.9 29.0 %copy-start.4 = (s32[16]{0:T(128)S(1)}, s32[16]{0:T(128)}, u32[]{:S(2)}) copy-start(s32[16]{0:T(128)} %constant.23.clone) | copy-start | bytes 196
  25.0 29.0 %copy-start.5 = (s32[16]{0:T(128)S(1)}, s32[16]{0:T(128)}, u32[]{:S(2)}) copy-start(s32[16]{0:T(128)} %constant.22.clone) | copy-start | bytes 196
  25.0 29.0 %copy-start.6 = (s32[16]{0:T(128)S(1)}, s32[16]{0:T(128)}, u32[]{:S(2)}) copy-start(s32[16]{0:T(128)} %constant.21.clone) | copy-start | bytes 196
  26.4 14.7 %copy-start.7 = (bf16[8,2,128,128]{3,2,1,0:T(8,128)(2,1)}, bf16[8,2,128,128]{3,2,1,0:T(8,128)(2,1)S(1)}, u32[]{:S(2)}) copy-start(bf16[8,2,128,128]{3,2,1,0:T(8,128)(2,1)S(1)} %collective-permute-done.2.refs_6_) | copy-start | bytes 1572868
  26.4 14.7 %collective-permute-start.5 = (bf16[8,2,128,128]{3,2,1,0:T(8,128)(2,1)S(1)}, bf16[8,2,128,128]{3,2,1,0:T(8,128)(2,1)S(1)}, u32[]{:S(2)}, u32[]{:S(2)}) collective-permute-start(bf16[8,2,128,128]{3,2,1,0:T(8,128)(2,1)S(1)} %collective-permute-done.2.refs_6_), channel_id=1, source_target_pairs={{0,64},{16,80},{32,96},{48,112},{64,128},{80,144},{96,160},{112,17... | collective-permute-start | bytes 1572872 | tf_op jit(solution)/shard_map/ppermute | solution.py:291
  28.0 15.3 %collective-permute-start.6 = (bf16[8,2,128,128]{3,2,1,0:T(8,128)(2,1)S(1)}, bf16[8,2,128,128]{3,2,1,0:T(8,128)(2,1)}, u32[]{:S(2)}, u32[]{:S(2)}) collective-permute-start(bf16[8,2,128,128]{3,2,1,0:T(8,128)(2,1)S(1)} %collective-permute-done.2.refs_6_), channel_id=1, source_target_pairs={{0,192},{16,208},{32,224},{48,240},{64,0},{80,16},{96,32},{112,48}... | collective-permute-start | bytes 1572872 | tf_op jit(solution)/shard_map/ppermute | solution.py:292
  30.9 3.8 %copy-start.13 = (bf16[4,2,128,128]{3,2,1,0:T(8,128)(2,1)}, bf16[4,2,128,128]{3,2,1,0:T(8,128)(2,1)S(1)}, u32[]{:S(2)}) copy-start(bf16[4,2,128,128]{3,2,1,0:T(8,128)(2,1)S(1)} %collective-permute-done.3.low) | copy-start | bytes 786436
  30.9 12.4 %collective-permute-start.9 = (bf16[8,2,128,128]{3,2,1,0:T(8,128)(2,1)S(1)}, bf16[8,2,128,128]{3,2,1,0:T(8,128)(2,1)}, u32[]{:S(2)}, u32[]{:S(2)}) collective-permute-start(bf16[8,2,128,128]{3,2,1,0:T(8,128)(2,1)S(1)} %collective-permute-done.refs_4_), channel_id=1, source_target_pairs={{0,16},{16,0},{32,48},{48,32},{64,80},{80,64},{96,112},{112,96},{1... | collective-permute-start | bytes 1572872 | tf_op jit(solution)/shard_map/ppermute | solution.py:295
  34.7 9.1 %collective-permute-start.10 = (bf16[8,2,128,128]{3,2,1,0:T(8,128)(2,1)S(1)}, bf16[8,2,128,128]{3,2,1,0:T(8,128)(2,1)S(1)}, u32[]{:S(2)}, u32[]{:S(2)}) collective-permute-start(bf16[8,2,128,128]{3,2,1,0:T(8,128)(2,1)S(1)} %collective-permute-done.1.refs_5_), channel_id=1, source_target_pairs={{0,16},{16,0},{32,48},{48,32},{64,80},{80,64},{96,112},{112,96},{1... | collective-permute-start | bytes 1572872 | tf_op jit(solution)/shard_map/ppermute | solution.py:295
  36.6 23.0 %copy-start.8 = (bf16[8,2,128,128]{3,2,1,0:T(8,128)(2,1)}, bf16[8,2,128,128]{3,2,1,0:T(8,128)(2,1)S(1)}, u32[]{:S(2)}) copy-start(bf16[8,2,128,128]{3,2,1,0:T(8,128)(2,1)S(1)} %collective-permute-done.8.refs_11_) | copy-start | bytes 1572868
  36.6 16.2 %collective-permute-start.7 = (bf16[8,2,128,128]{3,2,1,0:T(8,128)(2,1)}, bf16[8,2,128,128]{3,2,1,0:T(8,128)(2,1)}, u32[]{:S(2)}, u32[]{:S(2)}) collective-permute-start(bf16[8,2,128,128]{3,2,1,0:T(8,128)(2,1)} %join_halves.1.refs_7_), channel_id=1, source_target_pairs={{0,32},{16,48},{32,0},{48,16},{64,96},{80,112},{96,64},{112,80},{1... | collective-permute-start | bytes 1572872 | tf_op jit(solution)/shard_map/ppermute | solution.py:293
  41.1 18.5 %copy-start.9 = (bf16[8,2,128,128]{3,2,1,0:T(8,128)(2,1)}, bf16[8,2,128,128]{3,2,1,0:T(8,128)(2,1)S(1)}, u32[]{:S(2)}) copy-start(bf16[8,2,128,128]{3,2,1,0:T(8,128)(2,1)S(1)} %collective-permute-done.5.refs_8_) | copy-start | bytes 1572868
  41.1 13.4 %collective-permute-start.11 = (bf16[8,2,128,128]{3,2,1,0:T(8,128)(2,1)S(1)}, bf16[8,2,128,128]{3,2,1,0:T(8,128)(2,1)}, u32[]{:S(2)}, u32[]{:S(2)}) collective-permute-start(bf16[8,2,128,128]{3,2,1,0:T(8,128)(2,1)S(1)} %collective-permute-done.2.refs_6_), channel_id=1, source_target_pairs={{0,16},{16,0},{32,48},{48,32},{64,80},{80,64},{96,112},{112,96},{1... | collective-permute-start | bytes 1572872 | tf_op jit(solution)/shard_map/ppermute | solution.py:295
  43.3 11.2 %collective-permute-start.12 = (bf16[8,2,128,128]{3,2,1,0:T(8,128)(2,1)}, bf16[8,2,128,128]{3,2,1,0:T(8,128)(2,1)}, u32[]{:S(2)}, u32[]{:S(2)}) collective-permute-start(bf16[8,2,128,128]{3,2,1,0:T(8,128)(2,1)} %join_halves.1.refs_7_), channel_id=1, source_target_pairs={{0,16},{16,0},{32,48},{48,32},{64,80},{80,64},{96,112},{112,96},{1... | collective-permute-start | bytes 1572872 | tf_op jit(solution)/shard_map/ppermute | solution.py:295
  43.3 11.2 %collective-permute-start.13 = (bf16[8,2,128,128]{3,2,1,0:T(8,128)(2,1)S(1)}, bf16[8,2,128,128]{3,2,1,0:T(8,128)(2,1)S(1)}, u32[]{:S(2)}, u32[]{:S(2)}) collective-permute-start(bf16[8,2,128,128]{3,2,1,0:T(8,128)(2,1)S(1)} %collective-permute-done.5.refs_8_), channel_id=1, source_target_pairs={{0,16},{16,0},{32,48},{48,32},{64,80},{80,64},{96,112},{112,96},{1... | collective-permute-start | bytes 1572872 | tf_op jit(solution)/shard_map/ppermute | solution.py:295
  43.8 15.8 %copy-start.10 = (bf16[8,2,128,128]{3,2,1,0:T(8,128)(2,1)}, bf16[8,2,128,128]{3,2,1,0:T(8,128)(2,1)S(1)}, u32[]{:S(2)}) copy-start(bf16[8,2,128,128]{3,2,1,0:T(8,128)(2,1)S(1)} %collective-permute-done.10.refs_13_) | copy-start | bytes 1572868
  43.8 10.7 %collective-permute-start.14 = (bf16[8,2,128,128]{3,2,1,0:T(8,128)(2,1)}, bf16[8,2,128,128]{3,2,1,0:T(8,128)(2,1)S(1)}, u32[]{:S(2)}, u32[]{:S(2)}) collective-permute-start(bf16[8,2,128,128]{3,2,1,0:T(8,128)(2,1)} %collective-permute-done.6.refs_9_), channel_id=1, source_target_pairs={{0,16},{16,0},{32,48},{48,32},{64,80},{80,64},{96,112},{112,96},{1... | collective-permute-start | bytes 1572872 | tf_op jit(solution)/shard_map/ppermute | solution.py:295
  52.8 2.3 %collective-permute-start.15 = (bf16[8,2,128,128]{3,2,1,0:T(8,128)(2,1)}, bf16[8,2,128,128]{3,2,1,0:T(8,128)(2,1)}, u32[]{:S(2)}, u32[]{:S(2)}) collective-permute-start(bf16[8,2,128,128]{3,2,1,0:T(8,128)(2,1)} %collective-permute-done.7.refs_10_), channel_id=1, source_target_pairs={{0,16},{16,0},{32,48},{48,32},{64,80},{80,64},{96,112},{112,96},{1... | collective-permute-start | bytes 1572872 | tf_op jit(solution)/shard_map/ppermute | solution.py:295
  54.5 5.1 %copy-start.11 = (bf16[8,2,128,128]{3,2,1,0:T(8,128)(2,1)}, bf16[8,2,128,128]{3,2,1,0:T(8,128)(2,1)S(1)}, u32[]{:S(2)}) copy-start(bf16[8,2,128,128]{3,2,1,0:T(8,128)(2,1)S(1)} %collective-permute-done.13.refs_16_) | copy-start | bytes 1572868
  54.6 5.1 %copy-start.12 = (bf16[8,2,128,128]{3,2,1,0:T(8,128)(2,1)}, bf16[8,2,128,128]{3,2,1,0:T(8,128)(2,1)S(1)}, u32[]{:S(2)}) copy-start(bf16[8,2,128,128]{3,2,1,0:T(8,128)(2,1)S(1)} %collective-permute-done.14.refs_17_) | copy-start | bytes 1572868
  86.8 24.6 %copy-start = (bf16[64,2,128,128]{3,2,1,0:T(8,128)(2,1)S(1)}, bf16[64,2,128,128]{3,2,1,0:T(8,128)(2,1)}, u32[]{:S(2)}) copy-start(bf16[64,2,128,128]{3,2,1,0:T(8,128)(2,1)} %get-tuple-element.40) | copy-start | bytes 12582916
  86.8 3.9 %collective-permute-start.18 = (bf16[24,2,128,128]{3,2,1,0:T(8,128)(2,1)}, bf16[24,2,128,128]{3,2,1,0:T(8,128)(2,1)S(1)}, u32[]{:S(2)}, u32[]{:S(2)}) collective-permute-start(bf16[24,2,128,128]{3,2,1,0:T(8,128)(2,1)} %get-tuple-element.41), channel_id=1, source_target_pairs={{0,16},{16,0},{32,48},{48,32},{64,80},{80,64},{96,112},{112,96},{1... | collective-permute-start | bytes 4718600 | tf_op jit(solution)/shard_map/ppermute | solution.py:302
  92.6 18.8 %collective-permute-start.22 = (bf16[40,2,128,128]{3,2,1,0:T(8,128)(2,1)}, bf16[40,2,128,128]{3,2,1,0:T(8,128)(2,1)S(1)}, u32[]{:S(2)}, u32[]{:S(2)}) collective-permute-start(bf16[40,2,128,128]{3,2,1,0:T(8,128)(2,1)} %get-tuple-element.46), channel_id=1, source_target_pairs={{0,16},{16,0},{32,48},{48,32},{64,80},{80,64},{96,112},{112,96},{1... | collective-permute-start | bytes 7864328 | tf_op jit(solution)/shard_map/ppermute | solution.py:314
  92.8 15.7 %collective-permute-start.19 = (bf16[8,2,128,128]{3,2,1,0:T(8,128)(2,1)S(1)}, bf16[8,2,128,128]{3,2,1,0:T(8,128)(2,1)S(1)}, u32[]{:S(2)}, u32[]{:S(2)}) collective-permute-start(bf16[8,2,128,128]{3,2,1,0:T(8,128)(2,1)S(1)} %get-tuple-element.43), channel_id=1, source_target_pairs={{0,32},{16,48},{32,0},{48,16},{64,96},{80,112},{96,64},{112,80},{1... | collective-permute-start | bytes 1572872 | tf_op jit(solution)/shard_map/ppermute | solution.py:311
  96.0 13.9 %collective-permute-start.20 = (bf16[8,2,128,128]{3,2,1,0:T(8,128)(2,1)S(1)}, bf16[8,2,128,128]{3,2,1,0:T(8,128)(2,1)S(1)}, u32[]{:S(2)}, u32[]{:S(2)}) collective-permute-start(bf16[8,2,128,128]{3,2,1,0:T(8,128)(2,1)S(1)} %get-tuple-element.44), channel_id=1, source_target_pairs={{0,64},{16,80},{32,96},{48,112},{64,128},{80,144},{96,160},{112,17... | collective-permute-start | bytes 1572872 | tf_op jit(solution)/shard_map/ppermute | solution.py:312
  96.6 14.8 %collective-permute-start.21 = (bf16[8,2,128,128]{3,2,1,0:T(8,128)(2,1)S(1)}, bf16[8,2,128,128]{3,2,1,0:T(8,128)(2,1)S(1)}, u32[]{:S(2)}, u32[]{:S(2)}) collective-permute-start(bf16[8,2,128,128]{3,2,1,0:T(8,128)(2,1)S(1)} %get-tuple-element.45), channel_id=1, source_target_pairs={{0,192},{16,208},{32,224},{48,240},{64,0},{80,16},{96,32},{112,48}... | collective-permute-start | bytes 1572872 | tf_op jit(solution)/shard_map/ppermute | solution.py:313
  112.8 7.3 %collective-permute-start.23 = (bf16[4,2,128,128]{3,2,1,0:T(8,128)(2,1)S(1)}, bf16[4,2,128,128]{3,2,1,0:T(8,128)(2,1)S(1)}, u32[]{:S(2)}, u32[]{:S(2)}) collective-permute-start(bf16[4,2,128,128]{3,2,1,0:T(8,128)(2,1)S(1)} %get-tuple-element.51), channel_id=1, source_target_pairs={{0,64},{16,80},{32,96},{48,112},{64,128},{80,144},{96,160},{112,17... | collective-permute-start | bytes 786440 | tf_op jit(solution)/shard_map/ppermute | solution.py:322
  113.2 8.5 %collective-permute-start.24 = (bf16[4,2,128,128]{3,2,1,0:T(8,128)(2,1)S(1)}, bf16[4,2,128,128]{3,2,1,0:T(8,128)(2,1)S(1)}, u32[]{:S(2)}, u32[]{:S(2)}) collective-permute-start(bf16[4,2,128,128]{3,2,1,0:T(8,128)(2,1)S(1)} %get-tuple-element.52), channel_id=1, source_target_pairs={{0,192},{16,208},{32,224},{48,240},{64,0},{80,16},{96,32},{112,48}... | collective-permute-start | bytes 786440 | tf_op jit(solution)/shard_map/ppermute | solution.py:323
  114.9 14.0 %collective-permute-start.27 = (bf16[8,2,128,128]{3,2,1,0:T(8,128)(2,1)}, bf16[8,2,128,128]{3,2,1,0:T(8,128)(2,1)S(1)}, u32[]{:S(2)}, u32[]{:S(2)}) collective-permute-start(bf16[8,2,128,128]{3,2,1,0:T(8,128)(2,1)} %get-tuple-element.58), channel_id=1, source_target_pairs={{0,32},{16,48},{32,0},{48,16},{64,96},{80,112},{96,64},{112,80},{1... | collective-permute-start | bytes 1572872 | tf_op jit(solution)/shard_map/ppermute | solution.py:321
  123.1 12.4 %collective-permute-start.25 = (bf16[8,2,128,128]{3,2,1,0:T(8,128)(2,1)}, bf16[8,2,128,128]{3,2,1,0:T(8,128)(2,1)}, u32[]{:S(2)}, u32[]{:S(2)}) collective-permute-start(bf16[8,2,128,128]{3,2,1,0:T(8,128)(2,1)} %get-tuple-element.56), channel_id=1, source_target_pairs={{0,64},{16,80},{32,96},{48,112},{64,128},{80,144},{96,160},{112,17... | collective-permute-start | bytes 1572872 | tf_op jit(solution)/shard_map/ppermute | solution.py:329
  123.4 13.6 %collective-permute-start.26 = (bf16[8,2,128,128]{3,2,1,0:T(8,128)(2,1)}, bf16[8,2,128,128]{3,2,1,0:T(8,128)(2,1)}, u32[]{:S(2)}, u32[]{:S(2)}) collective-permute-start(bf16[8,2,128,128]{3,2,1,0:T(8,128)(2,1)} %get-tuple-element.57), channel_id=1, source_target_pairs={{0,192},{16,208},{32,224},{48,240},{64,0},{80,16},{96,32},{112,48}... | collective-permute-start | bytes 1572872 | tf_op jit(solution)/shard_map/ppermute | solution.py:330
  137.0 6.2 %copy-start.1 = (f32[1,2,16,4096]{3,2,1,0:T(8,128)S(1)}, f32[1,2,16,4096]{3,2,1,0:T(8,128)}, u32[]{:S(2)}) copy-start(f32[1,2,16,4096]{3,2,1,0:T(8,128)} %reduce-scatter.2.cloned.1.call-done) | copy-start | bytes 1572868
  138.1 5.1 %collective-permute-start.17 = (bf16[16,4096]{1,0:T(8,128)(2,1)S(1)}, bf16[16,4096]{1,0:T(8,128)(2,1)S(1)}, u32[]{:S(2)}, u32[]{:S(2)}) collective-permute-start(bf16[16,4096]{1,0:T(8,128)(2,1)S(1)} %fusion.2), channel_id=1, source_target_pairs={{0,8},{1,9},{2,10},{3,11},{4,12},{5,13},{6,14},{7,15},{8,0},{9,1},... | collective-permute-start | bytes 393224 | tf_op jit(solution)/shard_map/ppermute | solution.py:340
Sparse Core Ops, SparseCore 0:
  15.6 43.9 all-gather.2
  75.8 53.8 reduce-scatter.1

commit v4 on v3

--- a/solution.py
+++ b/solution.py
@@ -42,7 +42,8 @@
 HALF = len(BLOCKS) * PER
 PIECES = 2 * len(BLOCKS)
 SPAN = 512
-VMEM_LIMIT = 58 * 1024 * 1024
+DENSE_LIMIT = 58 * 1024 * 1024
+TILE_LIMIT = 20 * 1024 * 1024
 
 
 def start_rows(low, gathered, tokens, sems):
@@ -143,7 +144,7 @@
             pltpu.SemaphoreType.DMA((ZS * YL,)),
             pltpu.SemaphoreType.DMA((4,)),
         ],
-        compiler_params=pltpu.CompilerParams(vmem_limit_bytes=VMEM_LIMIT),
+        compiler_params=pltpu.CompilerParams(vmem_limit_bytes=DENSE_LIMIT),
         cost_estimate=pl.CostEstimate(
             flops=4 * GROUP * WIDTH * 2 * HIDE, bytes_accessed=16 << 20, transcendentals=GROUP * HIDE
         ),
@@ -210,7 +211,7 @@
             pltpu.SemaphoreType.DMA((ZS * YL,)),
             pltpu.SemaphoreType.DMA((3,)),
         ],
-        compiler_params=pltpu.CompilerParams(vmem_limit_bytes=VMEM_LIMIT),
+        compiler_params=pltpu.CompilerParams(vmem_limit_bytes=TILE_LIMIT),
         cost_estimate=pl.CostEstimate(
             flops=2 * GROUP * WIDTH * 2 * HIDE, bytes_accessed=12 << 20, transcendentals=0
         ),

time: 151 us -> 152 us (level)
  other arithmetic: 14.3 us -> 11.6 us
  local copies, waits for them, and re-layouts: 1.02 us -> 2.78 us
    unnamed x29 -> x31, local copies, waits for them, and re-layouts: 0.84 us -> 2.61 us
  transfers between devices with their start and end apart: 30 -> 30, of which waited for: 18 -> 19; matrix products, arithmetic and copies ran while one was open for 9% -> 7% of each run, Pallas kernels for 9% -> 9%
where the time goes in v4:
time: 152 us
  waiting for transfers between devices  68.1 us (45%)
  Pallas kernels  29.8 us (20%)
  starting transfers between devices  25.4 us (17%)
  between operations  14.3 us (9%)
  other arithmetic  11.6 us (8%)
  local copies, waits for them, and re-layouts  2.78 us (2%)
    pallas_call x1, Pallas kernels, dense_work(): pl.pallas_call(dense_kernel, out_shape=(jax.ShapeDtypeStruct((GROUP, HIDE...  16 us
    pallas_call x1, Pallas kernels, tile_work(): pl.pallas_call(tile_kernel, out_shape=tuple((jax.ShapeDtypeStruct((n, 2,...  12 us
    ppermute x1, waiting for transfers between devices, body(): far_in = lax.ppermute(sends[0], 'dp', Y_SWAP)  10.5 us
    ppermute x1, waiting for transfers between devices, body(): far_across = lax.ppermute(far, 'dp', Y_SWAP)  8.96 us
    ppermute x1, waiting for transfers between devices, body(): up_last = lax.ppermute(sends[0], 'dp', X_UP)  6.56 us
    ppermute x1, waiting for transfers between devices, body(): below = lax.ppermute(own, 'dp', X_UP)  5.84 us
    ppermute x1, waiting for transfers between devices, body(): half_up = lax.ppermute(sends[1], 'dp', X_UP)  4.81 us
    all_gather x1, waiting for transfers between devices, body(): gathered = lax.all_gather(pair, 'tensor', axis=0, axis_index_groups=Z_RINGS)  4.48 us
  transfers between devices with their start and end apart: 30, of which 19 were waited for; matrix products, arithmetic and copies ran while one was open for 7% of the time, Pallas kernels for 9%

profile of v4, /device:TPU:6, one launch (start us, length us, event | category | flops | bytes accessed | tf_op | source)
XLA Modules:
  0.0 152.0 jit_solution(14156152244385493663)
XLA Ops:
  7.2 1.7 %collective-permute-start.16 = (bf16[16,4096]{1,0:T(8,128)(2,1)}, bf16[16,4096]{1,0:T(8,128)(2,1)S(1)}, u32[]{:S(2)}, u32[]{:S(2)}) collective-permute-start(bf16[16,4096]{1,0:T(8,128)(2,1)} %param.7), channel_id=1, source_target_pairs={{0,8},{1,9},{2,10},{3,11},{4,12},{5,13},{6,14},{7,15},{8,0},{9,1},... | collective-permute-start | bytes 393224 | tf_op jit(solution)/shard_map/ppermute | solution.py:279
  8.9 0.7 collective-permute-start
  9.6 1.3 collective-permute-start.1
  10.9 2.9 %collective-permute-start.2 = (bf16[8,2,128,128]{3,2,1,0:T(8,128)(2,1)}, bf16[8,2,128,128]{3,2,1,0:T(8,128)(2,1)S(1)}, u32[]{:S(2)}, u32[]{:S(2)}) collective-permute-start(bf16[8,2,128,128]{3,2,1,0:T(8,128)(2,1)} %bitcast.19), channel_id=1, source_target_pairs={{0,32},{16,48},{32,0},{48,16},{64,96},{80,112},{96,64},{112,80},{1... | collective-permute-start | bytes 1572872 | tf_op jit(solution)/shard_map/ppermute | solution.py:283
  13.8 1.6 %pad_maximum_fusion = bf16[2,16,4096]{2,1,0:T(8,128)(2,1)} fusion(bf16[1,16,4096]{2,1,0:T(8,128)(2,1)S(1)} %bitcast.16, bf16[1,16,4096]{2,1,0:T(8,128)(2,1)} %bitcast.15), kind=kLoop, calls=%fused_computation.9 | loop fusion | flops 131072 | bytes 524288 | tf_op jit(solution)/shard_map/stack | solution.py:284
  15.6 0.8 copy.13
  16.6 5.8 %collective-permute-done.refs_4_ = bf16[8,2,128,128]{3,2,1,0:T(8,128)(2,1)S(1)} collective-permute-done((bf16[8,2,128,128]{3,2,1,0:T(8,128)(2,1)}, bf16[8,2,128,128]{3,2,1,0:T(8,128)(2,1)S(1)}, u32[]{:S(2)}, u32[]{:S(2)}) %collective-permute-start) | collective-permute-done | bytes 524320 | tf_op jit(solution)/shard_map/ppermute | solution.py:281
  22.5 1.8 %collective-permute-start.3 = (bf16[4,2,128,128]{3,2,1,0:T(8,128)(2,1)S(1)}, bf16[4,2,128,128]{3,2,1,0:T(8,128)(2,1)S(1)}, u32[]{:S(2)}, u32[]{:S(2)}) collective-permute-start(bf16[4,2,128,128]{3,2,1,0:T(8,128)(2,1)S(1)} %slice.94), channel_id=1, source_target_pairs={{0,64},{16,80},{32,96},{48,112},{64,128},{80,144},{96,160},{112,17... | collective-permute-start | bytes 786440 | tf_op jit(solution)/shard_map/ppermute | solution.py:289
  25.0 1.5 collective-permute-done.2.refs_6_
  26.4 1.5 %collective-permute-start.5 = (bf16[8,2,128,128]{3,2,1,0:T(8,128)(2,1)S(1)}, bf16[8,2,128,128]{3,2,1,0:T(8,128)(2,1)S(1)}, u32[]{:S(2)}, u32[]{:S(2)}) collective-permute-start(bf16[8,2,128,128]{3,2,1,0:T(8,128)(2,1)S(1)} %collective-permute-done.2.refs_6_), channel_id=1, source_target_pairs={{0,64},{16,80},{32,96},{48,112},{64,128},{80,144},{96,160},{112,17... | collective-permute-start | bytes 1572872 | tf_op jit(solution)/shard_map/ppermute | solution.py:292
  28.0 0.5 collective-permute-start.6
  28.5 2.4 %collective-permute-done.3.low = bf16[4,2,128,128]{3,2,1,0:T(8,128)(2,1)S(1)} collective-permute-done((bf16[4,2,128,128]{3,2,1,0:T(8,128)(2,1)S(1)}, bf16[4,2,128,128]{3,2,1,0:T(8,128)(2,1)S(1)}, u32[]{:S(2)}, u32[]{:S(2)}) %collective-permute-start.3) | collective-permute-done | bytes 262176 | tf_op jit(solution)/shard_map/ppermute | solution.py:289
  30.9 3.8 %collective-permute-done.4.high = bf16[4,2,128,128]{3,2,1,0:T(8,128)(2,1)} collective-permute-done((bf16[4,2,128,128]{3,2,1,0:T(8,128)(2,1)S(1)}, bf16[4,2,128,128]{3,2,1,0:T(8,128)(2,1)}, u32[]{:S(2)}, u32[]{:S(2)}) %collective-permute-start.4) | collective-permute-done | bytes 262176 | tf_op jit(solution)/shard_map/ppermute | solution.py:290
  34.7 1.9 %join_halves.1.refs_7_ = bf16[8,2,128,128]{3,2,1,0:T(8,128)(2,1)} custom-call(bf16[4,2,128,128]{3,2,1,0:T(8,128)(2,1)} %copy-done.14, bf16[4,2,128,128]{3,2,1,0:T(8,128)(2,1)} %collective-permute-done.4.high), custom_call_target="tpu_custom_call" | custom-call | flops 20000000000 | bytes 2097152 | tf_op jit(solution)/shard_map/join_halves/pallas_call | solution.py:263
  36.6 3.1 %collective-permute-start.7 = (bf16[8,2,128,128]{3,2,1,0:T(8,128)(2,1)}, bf16[8,2,128,128]{3,2,1,0:T(8,128)(2,1)}, u32[]{:S(2)}, u32[]{:S(2)}) collective-permute-start(bf16[8,2,128,128]{3,2,1,0:T(8,128)(2,1)} %join_halves.1.refs_7_), channel_id=1, source_target_pairs={{0,32},{16,48},{32,0},{48,16},{64,96},{80,112},{96,64},{112,80},{1... | collective-permute-start | bytes 1572872 | tf_op jit(solution)/shard_map/ppermute | solution.py:294
  40.0 0.6 collective-permute-done.5.refs_8_
  40.7 2.6 %collective-permute-done.6.refs_9_ = bf16[8,2,128,128]{3,2,1,0:T(8,128)(2,1)} collective-permute-done((bf16[8,2,128,128]{3,2,1,0:T(8,128)(2,1)S(1)}, bf16[8,2,128,128]{3,2,1,0:T(8,128)(2,1)}, u32[]{:S(2)}, u32[]{:S(2)}) %collective-permute-start.6) | collective-permute-done | bytes 524320 | tf_op jit(solution)/shard_map/ppermute | solution.py:293
  43.3 0.5 collective-permute-start.13
  43.9 9.0 %collective-permute-done.7.refs_10_ = bf16[8,2,128,128]{3,2,1,0:T(8,128)(2,1)} collective-permute-done((bf16[8,2,128,128]{3,2,1,0:T(8,128)(2,1)}, bf16[8,2,128,128]{3,2,1,0:T(8,128)(2,1)}, u32[]{:S(2)}, u32[]{:S(2)}) %collective-permute-start.7) | collective-permute-done | bytes 524320 | tf_op jit(solution)/shard_map/ppermute | solution.py:294
  52.9 0.6 broadcast_add_fusion.1.refs_0_
  53.5 0.5 xor_add_fusion.refs_1_
  54.0 1.1 collective-permute-done.15.refs_18_
  55.1 4.5 %all-gather.3.cloned.1.call-done = bf16[16,16,4096]{2,1,0:T(8,128)(2,1)} async-done(((bf16[2,16,4096]{2,1,0:T(8,128)(2,1)}), bf16[16,16,4096]{2,1,0:T(8,128)(2,1)}) %all-gather.3.cloned.1.call-update) | async-done | bytes 2097168 | tf_op jit(solution)/shard_map/all_gather | solution.py:285
  59.6 16.0 %forward_and_rows.1 = (bf16[256,896]{1,0:T(8,128)(2,1)}, bf16[7,256,256]{2,1,0:T(8,128)(2,1)}, f32[8,2,16,4096]{3,2,1,0:T(8,128)}) custom-call(s32[2,128]{1,0:T(2,128)} %broadcast_add_fusion.1.refs_0_, s32[16]{0:T(128)} %xor_add_fusion.refs_1_, s32[1]{0:T(128)} %bitcast.refs_2_.low, bf16[8,2,128,128]{3,2,1,0:T(8,128)(2,1)} %bitcast.21, ...), custom_call_target="tpu_custom_call" | custom-call | flops 7516192768 | bytes 16777216 | tf_op jit(solution)/shard_map/forward_and_rows/pallas_call | solution.py:129
  75.6 1.5 %copy-done.1 = bf16[16,16,4096]{2,1,0:T(8,128)(2,1)S(1)} copy-done((bf16[16,16,4096]{2,1,0:T(8,128)(2,1)S(1)}, bf16[16,16,4096]{2,1,0:T(8,128)(2,1)}, u32[]{:S(2)}) %copy-start.1) | copy-done | bytes 2097176
  77.4 12.0 %tile_sums.1 = (bf16[24,2,128,128]{3,2,1,0:T(8,128)(2,1)S(1)}, bf16[40,2,128,128]{3,2,1,0:T(8,128)(2,1)S(1)}, bf16[64,2,128,128]{3,2,1,0:T(8,128)(2,1)S(1)}) custom-call(s32[2,224]{1,0:T(2,128)S(1)} %get-tuple-element.36.target, s32[8]{0:T(128)S(1)} %compare_select_fusion.ready, s32[16]{0:T(128)S(1)} %fusion.16.spots, s32[1]{0:T(128)} %bitcast.refs_2_.low, ...), custom_call_target="tpu_custom_call" | custom-call | flops 3758096384 | bytes 12582912 | tf_op jit(solution)/shard_map/tile_sums/pallas_call | solution.py:200
  89.7 3.4 %collective-permute-done.18 = bf16[24,2,128,128]{3,2,1,0:T(8,128)(2,1)S(1)} collective-permute-done((bf16[24,2,128,128]{3,2,1,0:T(8,128)(2,1)S(1)}, bf16[24,2,128,128]{3,2,1,0:T(8,128)(2,1)S(1)}, u32[]{:S(2)}, u32[]{:S(2)}) %collective-permute-start.18) | collective-permute-done | bytes 1572896 | tf_op jit(solution)/shard_map/ppermute | solution.py:303
  93.1 0.8 add_convert_fusion.4
  94.1 3.1 %collective-permute-start.19 = (bf16[8,2,128,128]{3,2,1,0:T(8,128)(2,1)S(1)}, bf16[8,2,128,128]{3,2,1,0:T(8,128)(2,1)S(1)}, u32[]{:S(2)}, u32[]{:S(2)}) collective-permute-start(bf16[8,2,128,128]{3,2,1,0:T(8,128)(2,1)S(1)} %get-tuple-element.43), channel_id=1, source_target_pairs={{0,32},{16,48},{32,0},{48,16},{64,96},{80,112},{96,64},{112,80},{1... | collective-permute-start | bytes 1572872 | tf_op jit(solution)/shard_map/ppermute | solution.py:312
  97.2 0.6 collective-permute-start.20
  97.8 1.5 collective-permute-start.21
  99.3 10.5 %collective-permute-done.19 = bf16[8,2,128,128]{3,2,1,0:T(8,128)(2,1)S(1)} collective-permute-done((bf16[8,2,128,128]{3,2,1,0:T(8,128)(2,1)S(1)}, bf16[8,2,128,128]{3,2,1,0:T(8,128)(2,1)S(1)}, u32[]{:S(2)}, u32[]{:S(2)}) %collective-permute-start.19) | collective-permute-done | bytes 524320 | tf_op jit(solution)/shard_map/ppermute | solution.py:312
  109.8 1.3 collective-permute-done.20
  111.1 1.5 collective-permute-done.21
  112.6 1.4 add_convert_fusion.2
  114.5 1.7 %collective-permute-start.24 = (bf16[4,2,128,128]{3,2,1,0:T(8,128)(2,1)S(1)}, bf16[4,2,128,128]{3,2,1,0:T(8,128)(2,1)S(1)}, u32[]{:S(2)}, u32[]{:S(2)}) collective-permute-start(bf16[4,2,128,128]{3,2,1,0:T(8,128)(2,1)S(1)} %get-tuple-element.52), channel_id=1, source_target_pairs={{0,192},{16,208},{32,224},{48,240},{64,0},{80,16},{96,32},{112,48}... | collective-permute-start | bytes 786440 | tf_op jit(solution)/shard_map/ppermute | solution.py:324
  116.6 4.8 %collective-permute-done.23 = bf16[4,2,128,128]{3,2,1,0:T(8,128)(2,1)S(1)} collective-permute-done((bf16[4,2,128,128]{3,2,1,0:T(8,128)(2,1)S(1)}, bf16[4,2,128,128]{3,2,1,0:T(8,128)(2,1)S(1)}, u32[]{:S(2)}, u32[]{:S(2)}) %collective-permute-start.23) | collective-permute-done | bytes 262176 | tf_op jit(solution)/shard_map/ppermute | solution.py:323
  121.4 1.5 %collective-permute-done.24 = bf16[4,2,128,128]{3,2,1,0:T(8,128)(2,1)S(1)} collective-permute-done((bf16[4,2,128,128]{3,2,1,0:T(8,128)(2,1)S(1)}, bf16[4,2,128,128]{3,2,1,0:T(8,128)(2,1)S(1)}, u32[]{:S(2)}, u32[]{:S(2)}) %collective-permute-start.24) | collective-permute-done | bytes 262176 | tf_op jit(solution)/shard_map/ppermute | solution.py:324
  122.9 1.4 add_convert_fusion
  124.7 1.7 %collective-permute-start.26 = (bf16[8,2,128,128]{3,2,1,0:T(8,128)(2,1)}, bf16[8,2,128,128]{3,2,1,0:T(8,128)(2,1)}, u32[]{:S(2)}, u32[]{:S(2)}) collective-permute-start(bf16[8,2,128,128]{3,2,1,0:T(8,128)(2,1)} %get-tuple-element.57), channel_id=1, source_target_pairs={{0,192},{16,208},{32,224},{48,240},{64,0},{80,16},{96,32},{112,48}... | collective-permute-start | bytes 1572872 | tf_op jit(solution)/shard_map/ppermute | solution.py:331
  126.4 3.8 %collective-permute-done.27 = bf16[8,2,128,128]{3,2,1,0:T(8,128)(2,1)S(1)} collective-permute-done((bf16[8,2,128,128]{3,2,1,0:T(8,128)(2,1)}, bf16[8,2,128,128]{3,2,1,0:T(8,128)(2,1)S(1)}, u32[]{:S(2)}, u32[]{:S(2)}) %collective-permute-start.27) | collective-permute-done | bytes 524320 | tf_op jit(solution)/shard_map/ppermute | solution.py:322
  130.2 6.6 %collective-permute-done.25 = bf16[8,2,128,128]{3,2,1,0:T(8,128)(2,1)} collective-permute-done((bf16[8,2,128,128]{3,2,1,0:T(8,128)(2,1)}, bf16[8,2,128,128]{3,2,1,0:T(8,128)(2,1)}, u32[]{:S(2)}, u32[]{:S(2)}) %collective-permute-start.25) | collective-permute-done | bytes 524320 | tf_op jit(solution)/shard_map/ppermute | solution.py:330
  136.8 1.5 collective-permute-done.26
  138.3 1.1 fusion.2
  139.4 0.6 collective-permute-start.17
  139.9 2.7 %multiply_bitcast_fusion = f32[1,8,2,128,128]{4,3,2,1,0:T(8,128)} fusion(bf16[8,2,128,128]{3,2,1,0:T(8,128)(2,1)} %collective-permute-done.26, bf16[8,2,128,128]{3,2,1,0:T(8,128)(2,1)} %collective-permute-done.25, bf16[8,2,128,128]{3,2,1,0:T(8,128)(2,1)S(1)} %collective-permute-done.27, bf16[40,2,128,128]{3,2,1,0:T(8,128)(2,1)S(1)} %collective-permute-done.22, ...), kind=kLoop, calls=%fused_computation | loop fusion | flops 2621440 | bytes 3670016 | tf_op jit(solution)/shard_map/broadcast_in_dim | solution.py:337
  142.7 1.7 %collective-permute-done.17 = bf16[16,4096]{1,0:T(8,128)(2,1)S(1)} collective-permute-done((bf16[16,4096]{1,0:T(8,128)(2,1)S(1)}, bf16[16,4096]{1,0:T(8,128)(2,1)S(1)}, u32[]{:S(2)}, u32[]{:S(2)}) %collective-permute-start.17) | collective-permute-done | bytes 131104 | tf_op jit(solution)/shard_map/ppermute | solution.py:341
  144.4 0.7 fusion
  (72 shorter events, 3.4 us)
Async XLA Ops:
  7.2 52.4 %all-gather.3.cloned.1.call-start = ((), (), s32[]{:S(2)}) async-start(), calls=%async_computation.2 | async-start | bytes 2359296 | tf_op jit(solution)/shard_map/all_gather | solution.py:285
  7.2 6.6 %collective-permute-start.16 = (bf16[16,4096]{1,0:T(8,128)(2,1)}, bf16[16,4096]{1,0:T(8,128)(2,1)S(1)}, u32[]{:S(2)}, u32[]{:S(2)}) collective-permute-start(bf16[16,4096]{1,0:T(8,128)(2,1)} %param.7), channel_id=1, source_target_pairs={{0,8},{1,9},{2,10},{3,11},{4,12},{5,13},{6,14},{7,15},{8,0},{9,1},... | collective-permute-start | bytes 393224 | tf_op jit(solution)/shard_map/ppermute | solution.py:279
  8.9 13.6 %collective-permute-start = (bf16[8,2,128,128]{3,2,1,0:T(8,128)(2,1)}, bf16[8,2,128,128]{3,2,1,0:T(8,128)(2,1)S(1)}, u32[]{:S(2)}, u32[]{:S(2)}) collective-permute-start(bf16[8,2,128,128]{3,2,1,0:T(8,128)(2,1)} %bitcast.17), channel_id=1, source_target_pairs={{0,64},{16,80},{32,96},{48,112},{64,128},{80,144},{96,160},{112,17... | collective-permute-start | bytes 1572872 | tf_op jit(solution)/shard_map/ppermute | solution.py:281
  9.6 14.7 %collective-permute-start.1 = (bf16[8,2,128,128]{3,2,1,0:T(8,128)(2,1)}, bf16[8,2,128,128]{3,2,1,0:T(8,128)(2,1)S(1)}, u32[]{:S(2)}, u32[]{:S(2)}) collective-permute-start(bf16[8,2,128,128]{3,2,1,0:T(8,128)(2,1)} %bitcast.18), channel_id=1, source_target_pairs={{0,192},{16,208},{32,224},{48,240},{64,0},{80,16},{96,32},{112,48}... | collective-permute-start | bytes 1572872 | tf_op jit(solution)/shard_map/ppermute | solution.py:282
  10.9 15.5 %collective-permute-start.2 = (bf16[8,2,128,128]{3,2,1,0:T(8,128)(2,1)}, bf16[8,2,128,128]{3,2,1,0:T(8,128)(2,1)S(1)}, u32[]{:S(2)}, u32[]{:S(2)}) collective-permute-start(bf16[8,2,128,128]{3,2,1,0:T(8,128)(2,1)} %bitcast.19), channel_id=1, source_target_pairs={{0,32},{16,48},{32,0},{48,16},{64,96},{80,112},{96,64},{112,80},{1... | collective-permute-start | bytes 1572872 | tf_op jit(solution)/shard_map/ppermute | solution.py:283
  13.8 22.8 %collective-permute-start.8 = (bf16[8,2,128,128]{3,2,1,0:T(8,128)(2,1)}, bf16[8,2,128,128]{3,2,1,0:T(8,128)(2,1)S(1)}, u32[]{:S(2)}, u32[]{:S(2)}) collective-permute-start(bf16[8,2,128,128]{3,2,1,0:T(8,128)(2,1)} %bitcast.20), channel_id=1, source_target_pairs={{0,16},{16,0},{32,48},{48,32},{64,80},{80,64},{96,112},{112,96},{1... | collective-permute-start | bytes 1572872 | tf_op jit(solution)/shard_map/ppermute | solution.py:296
  15.5 122.8 %reduce-scatter.2.cloned.1.call-start = ((), (), s32[]{:S(2)}) async-start(), calls=%async_computation.1 | async-start | bytes 4718592 | tf_op jit(solution)/shard_map/reduce_scatter | solution.py:300
  22.5 14.1 %copy-start.4 = (bf16[8,2,128,128]{3,2,1,0:T(8,128)(2,1)}, bf16[8,2,128,128]{3,2,1,0:T(8,128)(2,1)S(1)}, u32[]{:S(2)}) copy-start(bf16[8,2,128,128]{3,2,1,0:T(8,128)(2,1)S(1)} %collective-permute-done.refs_4_) | copy-start | bytes 1572868
  22.5 8.4 %collective-permute-start.3 = (bf16[4,2,128,128]{3,2,1,0:T(8,128)(2,1)S(1)}, bf16[4,2,128,128]{3,2,1,0:T(8,128)(2,1)S(1)}, u32[]{:S(2)}, u32[]{:S(2)}) collective-permute-start(bf16[4,2,128,128]{3,2,1,0:T(8,128)(2,1)S(1)} %slice.94), channel_id=1, source_target_pairs={{0,64},{16,80},{32,96},{48,112},{64,128},{80,144},{96,160},{112,17... | collective-permute-start | bytes 786440 | tf_op jit(solution)/shard_map/ppermute | solution.py:289
  24.3 12.3 %copy-start.5 = (bf16[8,2,128,128]{3,2,1,0:T(8,128)(2,1)}, bf16[8,2,128,128]{3,2,1,0:T(8,128)(2,1)S(1)}, u32[]{:S(2)}) copy-start(bf16[8,2,128,128]{3,2,1,0:T(8,128)(2,1)S(1)} %collective-permute-done.1.refs_5_) | copy-start | bytes 1572868
  24.3 10.4 %collective-permute-start.4 = (bf16[4,2,128,128]{3,2,1,0:T(8,128)(2,1)S(1)}, bf16[4,2,128,128]{3,2,1,0:T(8,128)(2,1)}, u32[]{:S(2)}, u32[]{:S(2)}) collective-permute-start(bf16[4,2,128,128]{3,2,1,0:T(8,128)(2,1)S(1)} %slice.95), channel_id=1, source_target_pairs={{0,192},{16,208},{32,224},{48,240},{64,0},{80,16},{96,32},{112,48}... | collective-permute-start | bytes 786440 | tf_op jit(solution)/shard_map/ppermute | solution.py:290
  24.9 28.5 %copy-start.6 = (s32[16]{0:T(128)S(1)}, s32[16]{0:T(128)}, u32[]{:S(2)}) copy-start(s32[16]{0:T(128)} %constant.23.clone) | copy-start | bytes 196
  25.0 28.5 %copy-start.7 = (s32[16]{0:T(128)S(1)}, s32[16]{0:T(128)}, u32[]{:S(2)}) copy-start(s32[16]{0:T(128)} %constant.22.clone) | copy-start | bytes 196
  25.0 28.5 %copy-start.8 = (s32[16]{0:T(128)S(1)}, s32[16]{0:T(128)}, u32[]{:S(2)}) copy-start(s32[16]{0:T(128)} %constant.21.clone) | copy-start | bytes 196
  26.4 14.2 %copy-start.9 = (bf16[8,2,128,128]{3,2,1,0:T(8,128)(2,1)}, bf16[8,2,128,128]{3,2,1,0:T(8,128)(2,1)S(1)}, u32[]{:S(2)}) copy-start(bf16[8,2,128,128]{3,2,1,0:T(8,128)(2,1)S(1)} %collective-permute-done.2.refs_6_) | copy-start | bytes 1572868
  26.4 14.2 %collective-permute-start.5 = (bf16[8,2,128,128]{3,2,1,0:T(8,128)(2,1)S(1)}, bf16[8,2,128,128]{3,2,1,0:T(8,128)(2,1)S(1)}, u32[]{:S(2)}, u32[]{:S(2)}) collective-permute-start(bf16[8,2,128,128]{3,2,1,0:T(8,128)(2,1)S(1)} %collective-permute-done.2.refs_6_), channel_id=1, source_target_pairs={{0,64},{16,80},{32,96},{48,112},{64,128},{80,144},{96,160},{112,17... | collective-permute-start | bytes 1572872 | tf_op jit(solution)/shard_map/ppermute | solution.py:292
  28.0 15.3 %collective-permute-start.6 = (bf16[8,2,128,128]{3,2,1,0:T(8,128)(2,1)S(1)}, bf16[8,2,128,128]{3,2,1,0:T(8,128)(2,1)}, u32[]{:S(2)}, u32[]{:S(2)}) collective-permute-start(bf16[8,2,128,128]{3,2,1,0:T(8,128)(2,1)S(1)} %collective-permute-done.2.refs_6_), channel_id=1, source_target_pairs={{0,192},{16,208},{32,224},{48,240},{64,0},{80,16},{96,32},{112,48}... | collective-permute-start | bytes 1572872 | tf_op jit(solution)/shard_map/ppermute | solution.py:293
  30.9 3.8 %copy-start.14 = (bf16[4,2,128,128]{3,2,1,0:T(8,128)(2,1)}, bf16[4,2,128,128]{3,2,1,0:T(8,128)(2,1)S(1)}, u32[]{:S(2)}) copy-start(bf16[4,2,128,128]{3,2,1,0:T(8,128)(2,1)S(1)} %collective-permute-done.3.low) | copy-start | bytes 786436
  30.9 12.4 %collective-permute-start.9 = (bf16[8,2,128,128]{3,2,1,0:T(8,128)(2,1)S(1)}, bf16[8,2,128,128]{3,2,1,0:T(8,128)(2,1)}, u32[]{:S(2)}, u32[]{:S(2)}) collective-permute-start(bf16[8,2,128,128]{3,2,1,0:T(8,128)(2,1)S(1)} %collective-permute-done.refs_4_), channel_id=1, source_target_pairs={{0,16},{16,0},{32,48},{48,32},{64,80},{80,64},{96,112},{112,96},{1... | collective-permute-start | bytes 1572872 | tf_op jit(solution)/shard_map/ppermute | solution.py:296
  34.7 9.1 %collective-permute-start.10 = (bf16[8,2,128,128]{3,2,1,0:T(8,128)(2,1)S(1)}, bf16[8,2,128,128]{3,2,1,0:T(8,128)(2,1)}, u32[]{:S(2)}, u32[]{:S(2)}) collective-permute-start(bf16[8,2,128,128]{3,2,1,0:T(8,128)(2,1)S(1)} %collective-permute-done.1.refs_5_), channel_id=1, source_target_pairs={{0,16},{16,0},{32,48},{48,32},{64,80},{80,64},{96,112},{112,96},{1... | collective-permute-start | bytes 1572872 | tf_op jit(solution)/shard_map/ppermute | solution.py:296
  36.6 23.0 %copy-start.10 = (bf16[8,2,128,128]{3,2,1,0:T(8,128)(2,1)}, bf16[8,2,128,128]{3,2,1,0:T(8,128)(2,1)S(1)}, u32[]{:S(2)}) copy-start(bf16[8,2,128,128]{3,2,1,0:T(8,128)(2,1)S(1)} %collective-permute-done.8.refs_11_) | copy-start | bytes 1572868
  36.6 16.2 %collective-permute-start.7 = (bf16[8,2,128,128]{3,2,1,0:T(8,128)(2,1)}, bf16[8,2,128,128]{3,2,1,0:T(8,128)(2,1)}, u32[]{:S(2)}, u32[]{:S(2)}) collective-permute-start(bf16[8,2,128,128]{3,2,1,0:T(8,128)(2,1)} %join_halves.1.refs_7_), channel_id=1, source_target_pairs={{0,32},{16,48},{32,0},{48,16},{64,96},{80,112},{96,64},{112,80},{1... | collective-permute-start | bytes 1572872 | tf_op jit(solution)/shard_map/ppermute | solution.py:294
  40.7 18.9 %copy-start.11 = (bf16[8,2,128,128]{3,2,1,0:T(8,128)(2,1)}, bf16[8,2,128,128]{3,2,1,0:T(8,128)(2,1)S(1)}, u32[]{:S(2)}) copy-start(bf16[8,2,128,128]{3,2,1,0:T(8,128)(2,1)S(1)} %collective-permute-done.5.refs_8_) | copy-start | bytes 1572868
  40.7 13.3 %collective-permute-start.11 = (bf16[8,2,128,128]{3,2,1,0:T(8,128)(2,1)S(1)}, bf16[8,2,128,128]{3,2,1,0:T(8,128)(2,1)}, u32[]{:S(2)}, u32[]{:S(2)}) collective-permute-start(bf16[8,2,128,128]{3,2,1,0:T(8,128)(2,1)S(1)} %collective-permute-done.2.refs_6_), channel_id=1, source_target_pairs={{0,16},{16,0},{32,48},{48,32},{64,80},{80,64},{96,112},{112,96},{1... | collective-permute-start | bytes 1572872 | tf_op jit(solution)/shard_map/ppermute | solution.py:296
  43.3 10.7 %collective-permute-start.12 = (bf16[8,2,128,128]{3,2,1,0:T(8,128)(2,1)}, bf16[8,2,128,128]{3,2,1,0:T(8,128)(2,1)}, u32[]{:S(2)}, u32[]{:S(2)}) collective-permute-start(bf16[8,2,128,128]{3,2,1,0:T(8,128)(2,1)} %join_halves.1.refs_7_), channel_id=1, source_target_pairs={{0,16},{16,0},{32,48},{48,32},{64,80},{80,64},{96,112},{112,96},{1... | collective-permute-start | bytes 1572872 | tf_op jit(solution)/shard_map/ppermute | solution.py:296
  43.3 10.7 %collective-permute-start.13 = (bf16[8,2,128,128]{3,2,1,0:T(8,128)(2,1)S(1)}, bf16[8,2,128,128]{3,2,1,0:T(8,128)(2,1)S(1)}, u32[]{:S(2)}, u32[]{:S(2)}) collective-permute-start(bf16[8,2,128,128]{3,2,1,0:T(8,128)(2,1)S(1)} %collective-permute-done.5.refs_8_), channel_id=1, source_target_pairs={{0,16},{16,0},{32,48},{48,32},{64,80},{80,64},{96,112},{112,96},{1... | collective-permute-start | bytes 1572872 | tf_op jit(solution)/shard_map/ppermute | solution.py:296
  43.8 10.2 %collective-permute-start.14 = (bf16[8,2,128,128]{3,2,1,0:T(8,128)(2,1)}, bf16[8,2,128,128]{3,2,1,0:T(8,128)(2,1)S(1)}, u32[]{:S(2)}, u32[]{:S(2)}) collective-permute-start(bf16[8,2,128,128]{3,2,1,0:T(8,128)(2,1)} %collective-permute-done.6.refs_9_), channel_id=1, source_target_pairs={{0,16},{16,0},{32,48},{48,32},{64,80},{80,64},{96,112},{112,96},{1... | collective-permute-start | bytes 1572872 | tf_op jit(solution)/shard_map/ppermute | solution.py:296
  52.9 2.3 %collective-permute-start.15 = (bf16[8,2,128,128]{3,2,1,0:T(8,128)(2,1)}, bf16[8,2,128,128]{3,2,1,0:T(8,128)(2,1)}, u32[]{:S(2)}, u32[]{:S(2)}) collective-permute-start(bf16[8,2,128,128]{3,2,1,0:T(8,128)(2,1)} %collective-permute-done.7.refs_10_), channel_id=1, source_target_pairs={{0,16},{16,0},{32,48},{48,32},{64,80},{80,64},{96,112},{112,96},{1... | collective-permute-start | bytes 1572872 | tf_op jit(solution)/shard_map/ppermute | solution.py:296
  54.0 5.6 %copy-start.12 = (bf16[8,2,128,128]{3,2,1,0:T(8,128)(2,1)}, bf16[8,2,128,128]{3,2,1,0:T(8,128)(2,1)S(1)}, u32[]{:S(2)}) copy-start(bf16[8,2,128,128]{3,2,1,0:T(8,128)(2,1)S(1)} %collective-permute-done.13.refs_16_) | copy-start | bytes 1572868
  54.0 5.6 %copy-start.13 = (bf16[8,2,128,128]{3,2,1,0:T(8,128)(2,1)}, bf16[8,2,128,128]{3,2,1,0:T(8,128)(2,1)S(1)}, u32[]{:S(2)}) copy-start(bf16[8,2,128,128]{3,2,1,0:T(8,128)(2,1)S(1)} %collective-permute-done.14.refs_17_) | copy-start | bytes 1572868
  75.6 1.6 %copy-start.1 = (bf16[16,16,4096]{2,1,0:T(8,128)(2,1)S(1)}, bf16[16,16,4096]{2,1,0:T(8,128)(2,1)}, u32[]{:S(2)}) copy-start(bf16[16,16,4096]{2,1,0:T(8,128)(2,1)} %all-gather.3.cloned.1.call-done) | copy-start | bytes 6291460
  75.6 1.8 %copy-start.2 = (bf16[7,256,256]{2,1,0:T(8,128)(2,1)S(1)}, bf16[7,256,256]{2,1,0:T(8,128)(2,1)}, u32[]{:S(2)}) copy-start(bf16[7,256,256]{2,1,0:T(8,128)(2,1)} %get-tuple-element.39.grads) | copy-start | bytes 2752516
  89.4 33.6 %copy-start = (bf16[64,2,128,128]{3,2,1,0:T(8,128)(2,1)}, bf16[64,2,128,128]{3,2,1,0:T(8,128)(2,1)S(1)}, u32[]{:S(2)}) copy-start(bf16[64,2,128,128]{3,2,1,0:T(8,128)(2,1)S(1)} %get-tuple-element.40) | copy-start | bytes 12582916
  89.4 3.7 %collective-permute-start.18 = (bf16[24,2,128,128]{3,2,1,0:T(8,128)(2,1)S(1)}, bf16[24,2,128,128]{3,2,1,0:T(8,128)(2,1)S(1)}, u32[]{:S(2)}, u32[]{:S(2)}) collective-permute-start(bf16[24,2,128,128]{3,2,1,0:T(8,128)(2,1)S(1)} %get-tuple-element.41), channel_id=1, source_target_pairs={{0,16},{16,0},{32,48},{48,32},{64,80},{80,64},{96,112},{112,96},{1... | collective-permute-start | bytes 4718600 | tf_op jit(solution)/shard_map/ppermute | solution.py:303
  93.9 18.8 %collective-permute-start.22 = (bf16[40,2,128,128]{3,2,1,0:T(8,128)(2,1)S(1)}, bf16[40,2,128,128]{3,2,1,0:T(8,128)(2,1)S(1)}, u32[]{:S(2)}, u32[]{:S(2)}) collective-permute-start(bf16[40,2,128,128]{3,2,1,0:T(8,128)(2,1)S(1)} %get-tuple-element.46), channel_id=1, source_target_pairs={{0,16},{16,0},{32,48},{48,32},{64,80},{80,64},{96,112},{112,96},{1... | collective-permute-start | bytes 7864328 | tf_op jit(solution)/shard_map/ppermute | solution.py:315
  94.1 15.7 %collective-permute-start.19 = (bf16[8,2,128,128]{3,2,1,0:T(8,128)(2,1)S(1)}, bf16[8,2,128,128]{3,2,1,0:T(8,128)(2,1)S(1)}, u32[]{:S(2)}, u32[]{:S(2)}) collective-permute-start(bf16[8,2,128,128]{3,2,1,0:T(8,128)(2,1)S(1)} %get-tuple-element.43), channel_id=1, source_target_pairs={{0,32},{16,48},{32,0},{48,16},{64,96},{80,112},{96,64},{112,80},{1... | collective-permute-start | bytes 1572872 | tf_op jit(solution)/shard_map/ppermute | solution.py:312
  97.2 13.9 %collective-permute-start.20 = (bf16[8,2,128,128]{3,2,1,0:T(8,128)(2,1)S(1)}, bf16[8,2,128,128]{3,2,1,0:T(8,128)(2,1)S(1)}, u32[]{:S(2)}, u32[]{:S(2)}) collective-permute-start(bf16[8,2,128,128]{3,2,1,0:T(8,128)(2,1)S(1)} %get-tuple-element.44), channel_id=1, source_target_pairs={{0,64},{16,80},{32,96},{48,112},{64,128},{80,144},{96,160},{112,17... | collective-permute-start | bytes 1572872 | tf_op jit(solution)/shard_map/ppermute | solution.py:313
  97.8 14.8 %collective-permute-start.21 = (bf16[8,2,128,128]{3,2,1,0:T(8,128)(2,1)S(1)}, bf16[8,2,128,128]{3,2,1,0:T(8,128)(2,1)S(1)}, u32[]{:S(2)}, u32[]{:S(2)}) collective-permute-start(bf16[8,2,128,128]{3,2,1,0:T(8,128)(2,1)S(1)} %get-tuple-element.45), channel_id=1, source_target_pairs={{0,192},{16,208},{32,224},{48,240},{64,0},{80,16},{96,32},{112,48}... | collective-permute-start | bytes 1572872 | tf_op jit(solution)/shard_map/ppermute | solution.py:314
  114.1 7.3 %collective-permute-start.23 = (bf16[4,2,128,128]{3,2,1,0:T(8,128)(2,1)S(1)}, bf16[4,2,128,128]{3,2,1,0:T(8,128)(2,1)S(1)}, u32[]{:S(2)}, u32[]{:S(2)}) collective-permute-start(bf16[4,2,128,128]{3,2,1,0:T(8,128)(2,1)S(1)} %get-tuple-element.51), channel_id=1, source_target_pairs={{0,64},{16,80},{32,96},{48,112},{64,128},{80,144},{96,160},{112,17... | collective-permute-start | bytes 786440 | tf_op jit(solution)/shard_map/ppermute | solution.py:323
  114.5 8.5 %collective-permute-start.24 = (bf16[4,2,128,128]{3,2,1,0:T(8,128)(2,1)S(1)}, bf16[4,2,128,128]{3,2,1,0:T(8,128)(2,1)S(1)}, u32[]{:S(2)}, u32[]{:S(2)}) collective-permute-start(bf16[4,2,128,128]{3,2,1,0:T(8,128)(2,1)S(1)} %get-tuple-element.52), channel_id=1, source_target_pairs={{0,192},{16,208},{32,224},{48,240},{64,0},{80,16},{96,32},{112,48}... | collective-permute-start | bytes 786440 | tf_op jit(solution)/shard_map/ppermute | solution.py:324
  116.2 14.0 %collective-permute-start.27 = (bf16[8,2,128,128]{3,2,1,0:T(8,128)(2,1)}, bf16[8,2,128,128]{3,2,1,0:T(8,128)(2,1)S(1)}, u32[]{:S(2)}, u32[]{:S(2)}) collective-permute-start(bf16[8,2,128,128]{3,2,1,0:T(8,128)(2,1)} %get-tuple-element.58), channel_id=1, source_target_pairs={{0,32},{16,48},{32,0},{48,16},{64,96},{80,112},{96,64},{112,80},{1... | collective-permute-start | bytes 1572872 | tf_op jit(solution)/shard_map/ppermute | solution.py:322
  124.4 12.4 %collective-permute-start.25 = (bf16[8,2,128,128]{3,2,1,0:T(8,128)(2,1)}, bf16[8,2,128,128]{3,2,1,0:T(8,128)(2,1)}, u32[]{:S(2)}, u32[]{:S(2)}) collective-permute-start(bf16[8,2,128,128]{3,2,1,0:T(8,128)(2,1)} %get-tuple-element.56), channel_id=1, source_target_pairs={{0,64},{16,80},{32,96},{48,112},{64,128},{80,144},{96,160},{112,17... | collective-permute-start | bytes 1572872 | tf_op jit(solution)/shard_map/ppermute | solution.py:330
  124.7 13.6 %collective-permute-start.26 = (bf16[8,2,128,128]{3,2,1,0:T(8,128)(2,1)}, bf16[8,2,128,128]{3,2,1,0:T(8,128)(2,1)}, u32[]{:S(2)}, u32[]{:S(2)}) collective-permute-start(bf16[8,2,128,128]{3,2,1,0:T(8,128)(2,1)} %get-tuple-element.57), channel_id=1, source_target_pairs={{0,192},{16,208},{32,224},{48,240},{64,0},{80,16},{96,32},{112,48}... | collective-permute-start | bytes 1572872 | tf_op jit(solution)/shard_map/ppermute | solution.py:331
  138.3 6.2 %copy-start.3 = (f32[1,2,16,4096]{3,2,1,0:T(8,128)S(1)}, f32[1,2,16,4096]{3,2,1,0:T(8,128)}, u32[]{:S(2)}) copy-start(f32[1,2,16,4096]{3,2,1,0:T(8,128)} %reduce-scatter.2.cloned.1.call-done) | copy-start | bytes 1572868
  139.4 5.1 %collective-permute-start.17 = (bf16[16,4096]{1,0:T(8,128)(2,1)S(1)}, bf16[16,4096]{1,0:T(8,128)(2,1)S(1)}, u32[]{:S(2)}, u32[]{:S(2)}) collective-permute-start(bf16[16,4096]{1,0:T(8,128)(2,1)S(1)} %fusion.2), channel_id=1, source_target_pairs={{0,8},{1,9},{2,10},{3,11},{4,12},{5,13},{6,14},{7,15},{8,0},{9,1},... | collective-permute-start | bytes 393224 | tf_op jit(solution)/shard_map/ppermute | solution.py:341
Sparse Core Ops, SparseCore 0:
  15.6 43.9 all-gather.2
  75.7 53.8 reduce-scatter.1

commit v5 on v3

--- a/solution.py
+++ b/solution.py
@@ -253,22 +253,6 @@
     return (((x + dx) & (XS - 1)) * YS + (y ^ dy)) * CS + (c ^ dc)
 
 
-def join_kernel(low, high, out):
-    out[:PER // 2] = low[...]
-    out[PER // 2:] = high[...]
-
-
-def join(low, high):
-    return pl.pallas_call(
-        join_kernel,
-        out_shape=jax.ShapeDtypeStruct((PER, 2, TILE, TILE), low.dtype),
-        in_specs=[pl.BlockSpec(memory_space=pltpu.VMEM)] * 2,
-        out_specs=pl.BlockSpec(memory_space=pltpu.VMEM),
-        cost_estimate=pl.CostEstimate(flops=20000000000, bytes_accessed=2 << 20, transcendentals=0),
-        name="join_halves",
-    )(low, high)
-
-
 def body(tokens, weight_tiles, keep_mask, cotangent):
     f32, bf16 = jnp.float32, jnp.bfloat16
     rank = lax.axis_index("dp")
@@ -287,7 +271,7 @@
     half = PER // 2
     far_low = lax.ppermute(below[:half], "dp", X_UP)
     far_high = lax.ppermute(above[half:], "dp", X_DOWN)
-    far = join(far_low, far_high)
+    far = jnp.concatenate([far_low, far_high])
     below_across = lax.ppermute(across, "dp", X_UP)
     above_across = lax.ppermute(across, "dp", X_DOWN)
     far_across = lax.ppermute(far, "dp", Y_SWAP)

time: 151 us -> 150 us (level)
  Pallas kernels: 29 us -> 26.7 us
  starting transfers between devices: 25.5 us -> 27.1 us
    ppermute x1, waiting for transfers between devices: 0.01 us -> 3.87 us  [body(): other = lax.ppermute(tokens, 'tensor', L_SWAP)]
    all_gather x1, waiting for transfers between devices: 4.51 us -> 0.84 us  [body(): gathered = lax.all_gather(pair, 'tensor', axis=0, axis_index_groups=Z_RINGS)]
    pallas_call x1 -> x0, Pallas kernels: 1.88 us -> none  [join(): pl.pallas_call(join_kernel, out_shape=jax.ShapeDtypeStruct((PER, 2, TILE,...]
    ppermute x1, waiting for transfers between devices: 2.43 us -> 3.96 us  [body(): far_low = lax.ppermute(below[:half], 'dp', X_UP)]
  transfers between devices with their start and end apart: 30 -> 30, of which waited for: 18 -> 20; matrix products, arithmetic and copies ran while one was open for 9% -> 8% of each run, Pallas kernels for 9% -> 7%
where the time goes in v5:
time: 150 us; the launch traced here: 149 us
  waiting for transfers between devices  65.8 us (44%)
  starting transfers between devices  27.1 us (18%)
  Pallas kernels  26.7 us (18%)
  other arithmetic  14.5 us (10%)
  between operations  14.3 us (10%)
    pallas_call x1, Pallas kernels, dense_work(): pl.pallas_call(dense_kernel, out_shape=(jax.ShapeDtypeStruct((GROUP, HIDE...  16 us
    pallas_call x1, Pallas kernels, tile_work(): pl.pallas_call(tile_kernel, out_shape=tuple((jax.ShapeDtypeStruct((n, 2,...  10.6 us
    ppermute x1, waiting for transfers between devices, body(): far_in = lax.ppermute(sends[0], 'dp', Y_SWAP)  10.6 us
    ppermute x1, waiting for transfers between devices, body(): far_across = lax.ppermute(far, 'dp', Y_SWAP)  8.4 us
    ppermute x1, waiting for transfers between devices, body(): below = lax.ppermute(own, 'dp', X_UP)  6.77 us
    ppermute x1, waiting for transfers between devices, body(): up_last = lax.ppermute(sends[0], 'dp', X_UP)  6.58 us
    ppermute x1, waiting for transfers between devices, body(): half_up = lax.ppermute(sends[1], 'dp', X_UP)  4.72 us
    ppermute x1, waiting for transfers between devices, body(): far_low = lax.ppermute(below[:half], 'dp', X_UP)  3.96 us
  transfers between devices with their start and end apart: 30, of which 20 were waited for; matrix products, arithmetic and copies ran while one was open for 8% of the time, Pallas kernels for 7%

profile of v5, /device:TPU:6, one launch (start us, length us, event | category | flops | bytes accessed | tf_op | source)
XLA Modules:
  0.0 149.4 jit_solution(7870359426542144923)
XLA Ops:
  7.2 1.7 %collective-permute-start.16 = (bf16[16,4096]{1,0:T(8,128)(2,1)}, bf16[16,4096]{1,0:T(8,128)(2,1)S(1)}, u32[]{:S(2)}, u32[]{:S(2)}) collective-permute-start(bf16[16,4096]{1,0:T(8,128)(2,1)} %param.7), channel_id=1, source_target_pairs={{0,8},{1,9},{2,10},{3,11},{4,12},{5,13},{6,14},{7,15},{8,0},{9,1},... | collective-permute-start | bytes 393224 | tf_op jit(solution)/shard_map/ppermute | solution.py:262
  8.9 3.9 %collective-permute-done.16 = bf16[16,4096]{1,0:T(8,128)(2,1)S(1)} collective-permute-done((bf16[16,4096]{1,0:T(8,128)(2,1)}, bf16[16,4096]{1,0:T(8,128)(2,1)S(1)}, u32[]{:S(2)}, u32[]{:S(2)}) %collective-permute-start.16) | collective-permute-done | bytes 131104 | tf_op jit(solution)/shard_map/ppermute | solution.py:262
  12.8 1.6 %pad_maximum_fusion = bf16[2,16,4096]{2,1,0:T(8,128)(2,1)} fusion(bf16[1,16,4096]{2,1,0:T(8,128)(2,1)S(1)} %bitcast.14, bf16[1,16,4096]{2,1,0:T(8,128)(2,1)} %bitcast.13), kind=kLoop, calls=%fused_computation.9 | loop fusion | flops 131072 | bytes 524288 | tf_op jit(solution)/shard_map/stack | solution.py:267
  14.5 2.0 %collective-permute-start = (bf16[8,2,128,128]{3,2,1,0:T(8,128)(2,1)}, bf16[8,2,128,128]{3,2,1,0:T(8,128)(2,1)S(1)}, u32[]{:S(2)}, u32[]{:S(2)}) collective-permute-start(bf16[8,2,128,128]{3,2,1,0:T(8,128)(2,1)} %bitcast.17), channel_id=1, source_target_pairs={{0,64},{16,80},{32,96},{48,112},{64,128},{80,144},{96,160},{112,17... | collective-permute-start | bytes 1572872 | tf_op jit(solution)/shard_map/ppermute | solution.py:264
  16.6 3.2 %collective-permute-start.2 = (bf16[8,2,128,128]{3,2,1,0:T(8,128)(2,1)}, bf16[8,2,128,128]{3,2,1,0:T(8,128)(2,1)S(1)}, u32[]{:S(2)}, u32[]{:S(2)}) collective-permute-start(bf16[8,2,128,128]{3,2,1,0:T(8,128)(2,1)} %bitcast.19), channel_id=1, source_target_pairs={{0,32},{16,48},{32,0},{48,16},{64,96},{80,112},{96,64},{112,80},{1... | collective-permute-start | bytes 1572872 | tf_op jit(solution)/shard_map/ppermute | solution.py:266
  19.8 0.8 copy.13
  20.8 6.8 %collective-permute-done.refs_4_ = bf16[8,2,128,128]{3,2,1,0:T(8,128)(2,1)S(1)} collective-permute-done((bf16[8,2,128,128]{3,2,1,0:T(8,128)(2,1)}, bf16[8,2,128,128]{3,2,1,0:T(8,128)(2,1)S(1)}, u32[]{:S(2)}, u32[]{:S(2)}) %collective-permute-start) | collective-permute-done | bytes 524320 | tf_op jit(solution)/shard_map/ppermute | solution.py:264
  27.6 1.6 %collective-permute-start.3 = (bf16[4,2,128,128]{3,2,1,0:T(8,128)(2,1)S(1)}, bf16[4,2,128,128]{3,2,1,0:T(8,128)(2,1)S(1)}, u32[]{:S(2)}, u32[]{:S(2)}) collective-permute-start(bf16[4,2,128,128]{3,2,1,0:T(8,128)(2,1)S(1)} %slice.94), channel_id=1, source_target_pairs={{0,64},{16,80},{32,96},{48,112},{64,128},{80,144},{96,160},{112,17... | collective-permute-start | bytes 786440 | tf_op jit(solution)/shard_map/ppermute | solution.py:272
  29.4 0.6 collective-permute-start.4
  30.6 2.4 %collective-permute-start.5 = (bf16[8,2,128,128]{3,2,1,0:T(8,128)(2,1)S(1)}, bf16[8,2,128,128]{3,2,1,0:T(8,128)(2,1)}, u32[]{:S(2)}, u32[]{:S(2)}) collective-permute-start(bf16[8,2,128,128]{3,2,1,0:T(8,128)(2,1)S(1)} %collective-permute-done.2.refs_6_), channel_id=1, source_target_pairs={{0,64},{16,80},{32,96},{48,112},{64,128},{80,144},{96,160},{112,17... | collective-permute-start | bytes 1572872 | tf_op jit(solution)/shard_map/ppermute | solution.py:275
  33.0 4.0 %collective-permute-done.3 = bf16[4,2,128,128]{3,2,1,0:T(8,128)(2,1)S(1)} collective-permute-done((bf16[4,2,128,128]{3,2,1,0:T(8,128)(2,1)S(1)}, bf16[4,2,128,128]{3,2,1,0:T(8,128)(2,1)S(1)}, u32[]{:S(2)}, u32[]{:S(2)}) %collective-permute-start.3) | collective-permute-done | bytes 262176 | tf_op jit(solution)/shard_map/ppermute | solution.py:272
  37.0 2.9 %collective-permute-done.4 = bf16[4,2,128,128]{3,2,1,0:T(8,128)(2,1)S(1)} collective-permute-done((bf16[4,2,128,128]{3,2,1,0:T(8,128)(2,1)S(1)}, bf16[4,2,128,128]{3,2,1,0:T(8,128)(2,1)S(1)}, u32[]{:S(2)}, u32[]{:S(2)}) %collective-permute-start.4) | collective-permute-done | bytes 262176 | tf_op jit(solution)/shard_map/ppermute | solution.py:273
  39.9 3.4 %collective-permute-start.7 = (bf16[8,2,128,128]{3,2,1,0:T(8,128)(2,1)S(1)}, bf16[8,2,128,128]{3,2,1,0:T(8,128)(2,1)S(1)}, u32[]{:S(2)}, u32[]{:S(2)}) collective-permute-start(bf16[8,2,128,128]{3,2,1,0:T(8,128)(2,1)S(1)} %constant_dynamic-update-slice_fusion.refs_7_), channel_id=1, source_target_pairs={{0,32},{16,48},{32,0},{48,16},{64,96},{80,112},{96,64},{112,80},{1... | collective-permute-start | bytes 1572872 | tf_op jit(solution)/shard_map/ppermute | solution.py:277
  43.4 0.6 fusion.6
  44.2 0.6 compare_select_fusion.ready
  44.8 0.5 collective-permute-done.5.refs_8_
  45.3 1.7 %collective-permute-done.6.refs_9_ = bf16[8,2,128,128]{3,2,1,0:T(8,128)(2,1)} collective-permute-done((bf16[8,2,128,128]{3,2,1,0:T(8,128)(2,1)S(1)}, bf16[8,2,128,128]{3,2,1,0:T(8,128)(2,1)}, u32[]{:S(2)}, u32[]{:S(2)}) %collective-permute-start.6) | collective-permute-done | bytes 524320 | tf_op jit(solution)/shard_map/ppermute | solution.py:276
  46.9 0.5 collective-permute-start.13
  47.6 8.4 %collective-permute-done.7.refs_10_ = bf16[8,2,128,128]{3,2,1,0:T(8,128)(2,1)S(1)} collective-permute-done((bf16[8,2,128,128]{3,2,1,0:T(8,128)(2,1)S(1)}, bf16[8,2,128,128]{3,2,1,0:T(8,128)(2,1)S(1)}, u32[]{:S(2)}, u32[]{:S(2)}) %collective-permute-start.7) | collective-permute-done | bytes 524320 | tf_op jit(solution)/shard_map/ppermute | solution.py:277
  56.0 0.6 fusion.16.spots
  56.6 0.6 broadcast_add_fusion.1.refs_0_
  57.2 0.5 xor_add_fusion.refs_1_
  58.0 0.8 all-gather.3.cloned.1.call-done
  58.9 16.0 %forward_and_rows.1 = (bf16[256,896]{1,0:T(8,128)(2,1)}, bf16[7,256,256]{2,1,0:T(8,128)(2,1)}, f32[8,2,16,4096]{3,2,1,0:T(8,128)}) custom-call(s32[2,128]{1,0:T(2,128)} %broadcast_add_fusion.1.refs_0_, s32[16]{0:T(128)} %xor_add_fusion.refs_1_, s32[1]{0:T(128)} %bitcast.refs_2_.low, bf16[8,2,128,128]{3,2,1,0:T(8,128)(2,1)} %bitcast.21, ...), custom_call_target="tpu_custom_call" | custom-call | flops 7516192768 | bytes 16777216 | tf_op jit(solution)/shard_map/forward_and_rows/pallas_call | solution.py:128
  74.9 10.6 %tile_sums.1 = (bf16[24,2,128,128]{3,2,1,0:T(8,128)(2,1)}, bf16[40,2,128,128]{3,2,1,0:T(8,128)(2,1)}, bf16[64,2,128,128]{3,2,1,0:T(8,128)(2,1)}) custom-call(s32[2,224]{1,0:T(2,128)} %get-tuple-element.36.target, s32[8]{0:T(128)} %compare_select_fusion.ready, s32[16]{0:T(128)} %fusion.16.spots, s32[1]{0:T(128)} %bitcast.refs_2_.low, ...), custom_call_target="tpu_custom_call" | custom-call | flops 3758096384 | bytes 12582912 | tf_op jit(solution)/shard_map/tile_sums/pallas_call | solution.py:199
  85.9 3.6 %collective-permute-done.18 = bf16[24,2,128,128]{3,2,1,0:T(8,128)(2,1)S(1)} collective-permute-done((bf16[24,2,128,128]{3,2,1,0:T(8,128)(2,1)}, bf16[24,2,128,128]{3,2,1,0:T(8,128)(2,1)S(1)}, u32[]{:S(2)}, u32[]{:S(2)}) %collective-permute-start.18) | collective-permute-done | bytes 1572896 | tf_op jit(solution)/shard_map/ppermute | solution.py:286
  89.5 1.9 %add_convert_fusion.4 = (bf16[8,2,128,128]{3,2,1,0:T(8,128)(2,1)S(1)}, bf16[8,2,128,128]{3,2,1,0:T(8,128)(2,1)S(1)}, bf16[8,2,128,128]{3,2,1,0:T(8,128)(2,1)S(1)}) fusion(bf16[24,2,128,128]{3,2,1,0:T(8,128)(2,1)S(1)} %collective-permute-done.18, bf16[64,2,128,128]{3,2,1,0:T(8,128)(2,1)} %get-tuple-element.40), kind=kLoop, calls=%fused_computation.5 | loop fusion | flops 3145728 | bytes 4718592 | tf_op jit(solution)/shard_map/convert_element_type | solution.py:293
  91.7 3.1 %collective-permute-start.19 = (bf16[8,2,128,128]{3,2,1,0:T(8,128)(2,1)S(1)}, bf16[8,2,128,128]{3,2,1,0:T(8,128)(2,1)S(1)}, u32[]{:S(2)}, u32[]{:S(2)}) collective-permute-start(bf16[8,2,128,128]{3,2,1,0:T(8,128)(2,1)S(1)} %get-tuple-element.43), channel_id=1, source_target_pairs={{0,32},{16,48},{32,0},{48,16},{64,96},{80,112},{96,64},{112,80},{1... | collective-permute-start | bytes 1572872 | tf_op jit(solution)/shard_map/ppermute | solution.py:295
  94.7 0.5 collective-permute-start.20
  95.3 1.5 %collective-permute-start.21 = (bf16[8,2,128,128]{3,2,1,0:T(8,128)(2,1)S(1)}, bf16[8,2,128,128]{3,2,1,0:T(8,128)(2,1)S(1)}, u32[]{:S(2)}, u32[]{:S(2)}) collective-permute-start(bf16[8,2,128,128]{3,2,1,0:T(8,128)(2,1)S(1)} %get-tuple-element.45), channel_id=1, source_target_pairs={{0,192},{16,208},{32,224},{48,240},{64,0},{80,16},{96,32},{112,48}... | collective-permute-start | bytes 1572872 | tf_op jit(solution)/shard_map/ppermute | solution.py:297
  96.8 10.6 %collective-permute-done.19 = bf16[8,2,128,128]{3,2,1,0:T(8,128)(2,1)S(1)} collective-permute-done((bf16[8,2,128,128]{3,2,1,0:T(8,128)(2,1)S(1)}, bf16[8,2,128,128]{3,2,1,0:T(8,128)(2,1)S(1)}, u32[]{:S(2)}, u32[]{:S(2)}) %collective-permute-start.19) | collective-permute-done | bytes 524320 | tf_op jit(solution)/shard_map/ppermute | solution.py:295
  107.4 1.3 collective-permute-done.20
  108.6 1.5 collective-permute-done.21
  110.1 1.4 add_convert_fusion.2
  111.9 1.7 %collective-permute-start.24 = (bf16[4,2,128,128]{3,2,1,0:T(8,128)(2,1)S(1)}, bf16[4,2,128,128]{3,2,1,0:T(8,128)(2,1)S(1)}, u32[]{:S(2)}, u32[]{:S(2)}) collective-permute-start(bf16[4,2,128,128]{3,2,1,0:T(8,128)(2,1)S(1)} %get-tuple-element.52), channel_id=1, source_target_pairs={{0,192},{16,208},{32,224},{48,240},{64,0},{80,16},{96,32},{112,48}... | collective-permute-start | bytes 786440 | tf_op jit(solution)/shard_map/ppermute | solution.py:307
  113.6 0.5 collective-permute-start.27
  114.1 4.7 %collective-permute-done.23 = bf16[4,2,128,128]{3,2,1,0:T(8,128)(2,1)S(1)} collective-permute-done((bf16[4,2,128,128]{3,2,1,0:T(8,128)(2,1)S(1)}, bf16[4,2,128,128]{3,2,1,0:T(8,128)(2,1)S(1)}, u32[]{:S(2)}, u32[]{:S(2)}) %collective-permute-start.23) | collective-permute-done | bytes 262176 | tf_op jit(solution)/shard_map/ppermute | solution.py:306
  118.8 1.5 %collective-permute-done.24 = bf16[4,2,128,128]{3,2,1,0:T(8,128)(2,1)S(1)} collective-permute-done((bf16[4,2,128,128]{3,2,1,0:T(8,128)(2,1)S(1)}, bf16[4,2,128,128]{3,2,1,0:T(8,128)(2,1)S(1)}, u32[]{:S(2)}, u32[]{:S(2)}) %collective-permute-start.24) | collective-permute-done | bytes 262176 | tf_op jit(solution)/shard_map/ppermute | solution.py:307
  120.4 1.4 add_convert_fusion
  122.1 1.7 %collective-permute-start.26 = (bf16[8,2,128,128]{3,2,1,0:T(8,128)(2,1)}, bf16[8,2,128,128]{3,2,1,0:T(8,128)(2,1)}, u32[]{:S(2)}, u32[]{:S(2)}) collective-permute-start(bf16[8,2,128,128]{3,2,1,0:T(8,128)(2,1)} %get-tuple-element.57), channel_id=1, source_target_pairs={{0,192},{16,208},{32,224},{48,240},{64,0},{80,16},{96,32},{112,48}... | collective-permute-start | bytes 1572872 | tf_op jit(solution)/shard_map/ppermute | solution.py:314
  123.8 3.8 %collective-permute-done.27 = bf16[8,2,128,128]{3,2,1,0:T(8,128)(2,1)S(1)} collective-permute-done((bf16[8,2,128,128]{3,2,1,0:T(8,128)(2,1)}, bf16[8,2,128,128]{3,2,1,0:T(8,128)(2,1)S(1)}, u32[]{:S(2)}, u32[]{:S(2)}) %collective-permute-start.27) | collective-permute-done | bytes 524320 | tf_op jit(solution)/shard_map/ppermute | solution.py:305
  127.6 6.6 %collective-permute-done.25 = bf16[8,2,128,128]{3,2,1,0:T(8,128)(2,1)} collective-permute-done((bf16[8,2,128,128]{3,2,1,0:T(8,128)(2,1)}, bf16[8,2,128,128]{3,2,1,0:T(8,128)(2,1)}, u32[]{:S(2)}, u32[]{:S(2)}) %collective-permute-start.25) | collective-permute-done | bytes 524320 | tf_op jit(solution)/shard_map/ppermute | solution.py:313
  134.2 1.5 collective-permute-done.26
  135.7 1.1 fusion.2
  136.8 1.1 collective-permute-start.17
  137.9 2.7 %multiply_bitcast_fusion = f32[1,8,2,128,128]{4,3,2,1,0:T(8,128)} fusion(bf16[8,2,128,128]{3,2,1,0:T(8,128)(2,1)} %collective-permute-done.26, bf16[8,2,128,128]{3,2,1,0:T(8,128)(2,1)} %collective-permute-done.25, bf16[8,2,128,128]{3,2,1,0:T(8,128)(2,1)S(1)} %collective-permute-done.27, bf16[40,2,128,128]{3,2,1,0:T(8,128)(2,1)S(1)} %collective-permute-done.22, ...), kind=kLoop, calls=%fused_computation | loop fusion | flops 2621440 | bytes 3670016 | tf_op jit(solution)/shard_map/broadcast_in_dim | solution.py:320
  140.7 1.2 collective-permute-done.17
  141.9 0.7 fusion
  (67 shorter events, 3.1 us)
Async XLA Ops:
  7.2 50.0 %copy-start.5 = (s32[16]{0:T(128)S(1)}, s32[16]{0:T(128)}, u32[]{:S(2)}) copy-start(s32[16]{0:T(128)} %constant.23.clone) | copy-start | bytes 196
  7.2 50.0 %copy-start.6 = (s32[16]{0:T(128)S(1)}, s32[16]{0:T(128)}, u32[]{:S(2)}) copy-start(s32[16]{0:T(128)} %constant.22.clone) | copy-start | bytes 196
  7.2 50.0 %copy-start.7 = (s32[16]{0:T(128)S(1)}, s32[16]{0:T(128)}, u32[]{:S(2)}) copy-start(s32[16]{0:T(128)} %constant.21.clone) | copy-start | bytes 196
  7.2 51.6 %all-gather.3.cloned.1.call-start = ((), (), s32[]{:S(2)}) async-start(), calls=%async_computation.2 | async-start | bytes 2359296 | tf_op jit(solution)/shard_map/all_gather | solution.py:268
  7.2 5.5 %collective-permute-start.16 = (bf16[16,4096]{1,0:T(8,128)(2,1)}, bf16[16,4096]{1,0:T(8,128)(2,1)S(1)}, u32[]{:S(2)}, u32[]{:S(2)}) collective-permute-start(bf16[16,4096]{1,0:T(8,128)(2,1)} %param.7), channel_id=1, source_target_pairs={{0,8},{1,9},{2,10},{3,11},{4,12},{5,13},{6,14},{7,15},{8,0},{9,1},... | collective-permute-start | bytes 393224 | tf_op jit(solution)/shard_map/ppermute | solution.py:262
  14.4 121.2 %reduce-scatter.2.cloned.1.call-start = ((), (), s32[]{:S(2)}) async-start(), calls=%async_computation.1 | async-start | bytes 4718592 | tf_op jit(solution)/shard_map/reduce_scatter | solution.py:283
  14.5 13.1 %collective-permute-start = (bf16[8,2,128,128]{3,2,1,0:T(8,128)(2,1)}, bf16[8,2,128,128]{3,2,1,0:T(8,128)(2,1)S(1)}, u32[]{:S(2)}, u32[]{:S(2)}) collective-permute-start(bf16[8,2,128,128]{3,2,1,0:T(8,128)(2,1)} %bitcast.17), channel_id=1, source_target_pairs={{0,64},{16,80},{32,96},{48,112},{64,128},{80,144},{96,160},{112,17... | collective-permute-start | bytes 1572872 | tf_op jit(solution)/shard_map/ppermute | solution.py:264
  16.5 12.8 %collective-permute-start.1 = (bf16[8,2,128,128]{3,2,1,0:T(8,128)(2,1)}, bf16[8,2,128,128]{3,2,1,0:T(8,128)(2,1)S(1)}, u32[]{:S(2)}, u32[]{:S(2)}) collective-permute-start(bf16[8,2,128,128]{3,2,1,0:T(8,128)(2,1)} %bitcast.18), channel_id=1, source_target_pairs={{0,192},{16,208},{32,224},{48,240},{64,0},{80,16},{96,32},{112,48}... | collective-permute-start | bytes 1572872 | tf_op jit(solution)/shard_map/ppermute | solution.py:265
  16.6 14.0 %collective-permute-start.2 = (bf16[8,2,128,128]{3,2,1,0:T(8,128)(2,1)}, bf16[8,2,128,128]{3,2,1,0:T(8,128)(2,1)S(1)}, u32[]{:S(2)}, u32[]{:S(2)}) collective-permute-start(bf16[8,2,128,128]{3,2,1,0:T(8,128)(2,1)} %bitcast.19), channel_id=1, source_target_pairs={{0,32},{16,48},{32,0},{48,16},{64,96},{80,112},{96,64},{112,80},{1... | collective-permute-start | bytes 1572872 | tf_op jit(solution)/shard_map/ppermute | solution.py:266
  19.8 20.2 %collective-permute-start.8 = (bf16[8,2,128,128]{3,2,1,0:T(8,128)(2,1)}, bf16[8,2,128,128]{3,2,1,0:T(8,128)(2,1)}, u32[]{:S(2)}, u32[]{:S(2)}) collective-permute-start(bf16[8,2,128,128]{3,2,1,0:T(8,128)(2,1)} %bitcast.20), channel_id=1, source_target_pairs={{0,16},{16,0},{32,48},{48,32},{64,80},{80,64},{96,112},{112,96},{1... | collective-permute-start | bytes 1572872 | tf_op jit(solution)/shard_map/ppermute | solution.py:279
  27.6 31.3 %copy-start.2 = (bf16[8,2,128,128]{3,2,1,0:T(8,128)(2,1)}, bf16[8,2,128,128]{3,2,1,0:T(8,128)(2,1)S(1)}, u32[]{:S(2)}) copy-start(bf16[8,2,128,128]{3,2,1,0:T(8,128)(2,1)S(1)} %collective-permute-done.refs_4_) | copy-start | bytes 1572868
  27.6 9.3 %collective-permute-start.3 = (bf16[4,2,128,128]{3,2,1,0:T(8,128)(2,1)S(1)}, bf16[4,2,128,128]{3,2,1,0:T(8,128)(2,1)S(1)}, u32[]{:S(2)}, u32[]{:S(2)}) collective-permute-start(bf16[4,2,128,128]{3,2,1,0:T(8,128)(2,1)S(1)} %slice.94), channel_id=1, source_target_pairs={{0,64},{16,80},{32,96},{48,112},{64,128},{80,144},{96,160},{112,17... | collective-permute-start | bytes 786440 | tf_op jit(solution)/shard_map/ppermute | solution.py:272
  29.3 29.5 %copy-start.3 = (bf16[8,2,128,128]{3,2,1,0:T(8,128)(2,1)}, bf16[8,2,128,128]{3,2,1,0:T(8,128)(2,1)S(1)}, u32[]{:S(2)}) copy-start(bf16[8,2,128,128]{3,2,1,0:T(8,128)(2,1)S(1)} %collective-permute-done.1.refs_5_) | copy-start | bytes 1572868
  29.4 10.5 %collective-permute-start.4 = (bf16[4,2,128,128]{3,2,1,0:T(8,128)(2,1)S(1)}, bf16[4,2,128,128]{3,2,1,0:T(8,128)(2,1)S(1)}, u32[]{:S(2)}, u32[]{:S(2)}) collective-permute-start(bf16[4,2,128,128]{3,2,1,0:T(8,128)(2,1)S(1)} %slice.95), channel_id=1, source_target_pairs={{0,192},{16,208},{32,224},{48,240},{64,0},{80,16},{96,32},{112,48}... | collective-permute-start | bytes 786440 | tf_op jit(solution)/shard_map/ppermute | solution.py:273
  30.6 28.3 %copy-start.8 = (bf16[8,2,128,128]{3,2,1,0:T(8,128)(2,1)}, bf16[8,2,128,128]{3,2,1,0:T(8,128)(2,1)S(1)}, u32[]{:S(2)}) copy-start(bf16[8,2,128,128]{3,2,1,0:T(8,128)(2,1)S(1)} %collective-permute-done.2.refs_6_) | copy-start | bytes 1572868
  30.6 14.7 %collective-permute-start.5 = (bf16[8,2,128,128]{3,2,1,0:T(8,128)(2,1)S(1)}, bf16[8,2,128,128]{3,2,1,0:T(8,128)(2,1)}, u32[]{:S(2)}, u32[]{:S(2)}) collective-permute-start(bf16[8,2,128,128]{3,2,1,0:T(8,128)(2,1)S(1)} %collective-permute-done.2.refs_6_), channel_id=1, source_target_pairs={{0,64},{16,80},{32,96},{48,112},{64,128},{80,144},{96,160},{112,17... | collective-permute-start | bytes 1572872 | tf_op jit(solution)/shard_map/ppermute | solution.py:275
  33.0 14.0 %collective-permute-start.6 = (bf16[8,2,128,128]{3,2,1,0:T(8,128)(2,1)S(1)}, bf16[8,2,128,128]{3,2,1,0:T(8,128)(2,1)}, u32[]{:S(2)}, u32[]{:S(2)}) collective-permute-start(bf16[8,2,128,128]{3,2,1,0:T(8,128)(2,1)S(1)} %collective-permute-done.2.refs_6_), channel_id=1, source_target_pairs={{0,192},{16,208},{32,224},{48,240},{64,0},{80,16},{96,32},{112,48}... | collective-permute-start | bytes 1572872 | tf_op jit(solution)/shard_map/ppermute | solution.py:276
  36.9 10.0 %collective-permute-start.9 = (bf16[8,2,128,128]{3,2,1,0:T(8,128)(2,1)S(1)}, bf16[8,2,128,128]{3,2,1,0:T(8,128)(2,1)S(1)}, u32[]{:S(2)}, u32[]{:S(2)}) collective-permute-start(bf16[8,2,128,128]{3,2,1,0:T(8,128)(2,1)S(1)} %collective-permute-done.refs_4_), channel_id=1, source_target_pairs={{0,16},{16,0},{32,48},{48,32},{64,80},{80,64},{96,112},{112,96},{1... | collective-permute-start | bytes 1572872 | tf_op jit(solution)/shard_map/ppermute | solution.py:279
  39.9 7.6 %collective-permute-start.10 = (bf16[8,2,128,128]{3,2,1,0:T(8,128)(2,1)S(1)}, bf16[8,2,128,128]{3,2,1,0:T(8,128)(2,1)S(1)}, u32[]{:S(2)}, u32[]{:S(2)}) collective-permute-start(bf16[8,2,128,128]{3,2,1,0:T(8,128)(2,1)S(1)} %collective-permute-done.1.refs_5_), channel_id=1, source_target_pairs={{0,16},{16,0},{32,48},{48,32},{64,80},{80,64},{96,112},{112,96},{1... | collective-permute-start | bytes 1572872 | tf_op jit(solution)/shard_map/ppermute | solution.py:279
  39.9 18.9 %copy-start.4 = (bf16[8,2,128,128]{3,2,1,0:T(8,128)(2,1)}, bf16[8,2,128,128]{3,2,1,0:T(8,128)(2,1)S(1)}, u32[]{:S(2)}) copy-start(bf16[8,2,128,128]{3,2,1,0:T(8,128)(2,1)S(1)} %constant_dynamic-update-slice_fusion.refs_7_) | copy-start | bytes 1572868
  39.9 16.0 %collective-permute-start.7 = (bf16[8,2,128,128]{3,2,1,0:T(8,128)(2,1)S(1)}, bf16[8,2,128,128]{3,2,1,0:T(8,128)(2,1)S(1)}, u32[]{:S(2)}, u32[]{:S(2)}) collective-permute-start(bf16[8,2,128,128]{3,2,1,0:T(8,128)(2,1)S(1)} %constant_dynamic-update-slice_fusion.refs_7_), channel_id=1, source_target_pairs={{0,32},{16,48},{32,0},{48,16},{64,96},{80,112},{96,64},{112,80},{1... | collective-permute-start | bytes 1572872 | tf_op jit(solution)/shard_map/ppermute | solution.py:277
  45.3 12.4 %collective-permute-start.11 = (bf16[8,2,128,128]{3,2,1,0:T(8,128)(2,1)S(1)}, bf16[8,2,128,128]{3,2,1,0:T(8,128)(2,1)}, u32[]{:S(2)}, u32[]{:S(2)}) collective-permute-start(bf16[8,2,128,128]{3,2,1,0:T(8,128)(2,1)S(1)} %collective-permute-done.2.refs_6_), channel_id=1, source_target_pairs={{0,16},{16,0},{32,48},{48,32},{64,80},{80,64},{96,112},{112,96},{1... | collective-permute-start | bytes 1572872 | tf_op jit(solution)/shard_map/ppermute | solution.py:279
  46.9 10.8 %collective-permute-start.12 = (bf16[8,2,128,128]{3,2,1,0:T(8,128)(2,1)S(1)}, bf16[8,2,128,128]{3,2,1,0:T(8,128)(2,1)}, u32[]{:S(2)}, u32[]{:S(2)}) collective-permute-start(bf16[8,2,128,128]{3,2,1,0:T(8,128)(2,1)S(1)} %constant_dynamic-update-slice_fusion.refs_7_), channel_id=1, source_target_pairs={{0,16},{16,0},{32,48},{48,32},{64,80},{80,64},{96,112},{112,96},{1... | collective-permute-start | bytes 1572872 | tf_op jit(solution)/shard_map/ppermute | solution.py:279
  46.9 10.2 %copy-start.9 = (bf16[8,2,128,128]{3,2,1,0:T(8,128)(2,1)}, bf16[8,2,128,128]{3,2,1,0:T(8,128)(2,1)S(1)}, u32[]{:S(2)}) copy-start(bf16[8,2,128,128]{3,2,1,0:T(8,128)(2,1)S(1)} %collective-permute-done.9.refs_12_) | copy-start | bytes 1572868
  46.9 10.8 %collective-permute-start.13 = (bf16[8,2,128,128]{3,2,1,0:T(8,128)(2,1)}, bf16[8,2,128,128]{3,2,1,0:T(8,128)(2,1)}, u32[]{:S(2)}, u32[]{:S(2)}) collective-permute-start(bf16[8,2,128,128]{3,2,1,0:T(8,128)(2,1)} %collective-permute-done.5.refs_8_), channel_id=1, source_target_pairs={{0,16},{16,0},{32,48},{48,32},{64,80},{80,64},{96,112},{112,96},{1... | collective-permute-start | bytes 1572872 | tf_op jit(solution)/shard_map/ppermute | solution.py:279
  47.4 11.4 %copy-start.10 = (bf16[8,2,128,128]{3,2,1,0:T(8,128)(2,1)}, bf16[8,2,128,128]{3,2,1,0:T(8,128)(2,1)S(1)}, u32[]{:S(2)}) copy-start(bf16[8,2,128,128]{3,2,1,0:T(8,128)(2,1)S(1)} %collective-permute-done.10.refs_13_) | copy-start | bytes 1572868
  47.5 10.3 %collective-permute-start.14 = (bf16[8,2,128,128]{3,2,1,0:T(8,128)(2,1)}, bf16[8,2,128,128]{3,2,1,0:T(8,128)(2,1)}, u32[]{:S(2)}, u32[]{:S(2)}) collective-permute-start(bf16[8,2,128,128]{3,2,1,0:T(8,128)(2,1)} %collective-permute-done.6.refs_9_), channel_id=1, source_target_pairs={{0,16},{16,0},{32,48},{48,32},{64,80},{80,64},{96,112},{112,96},{1... | collective-permute-start | bytes 1572872 | tf_op jit(solution)/shard_map/ppermute | solution.py:279
  56.0 2.9 %copy-start.11 = (bf16[8,2,128,128]{3,2,1,0:T(8,128)(2,1)}, bf16[8,2,128,128]{3,2,1,0:T(8,128)(2,1)S(1)}, u32[]{:S(2)}) copy-start(bf16[8,2,128,128]{3,2,1,0:T(8,128)(2,1)S(1)} %collective-permute-done.7.refs_10_) | copy-start | bytes 1572868
  56.0 2.0 %collective-permute-start.15 = (bf16[8,2,128,128]{3,2,1,0:T(8,128)(2,1)S(1)}, bf16[8,2,128,128]{3,2,1,0:T(8,128)(2,1)}, u32[]{:S(2)}, u32[]{:S(2)}) collective-permute-start(bf16[8,2,128,128]{3,2,1,0:T(8,128)(2,1)S(1)} %collective-permute-done.7.refs_10_), channel_id=1, source_target_pairs={{0,16},{16,0},{32,48},{48,32},{64,80},{80,64},{96,112},{112,96},{1... | collective-permute-start | bytes 1572872 | tf_op jit(solution)/shard_map/ppermute | solution.py:279
  85.6 24.5 %copy-start = (bf16[64,2,128,128]{3,2,1,0:T(8,128)(2,1)S(1)}, bf16[64,2,128,128]{3,2,1,0:T(8,128)(2,1)}, u32[]{:S(2)}) copy-start(bf16[64,2,128,128]{3,2,1,0:T(8,128)(2,1)} %get-tuple-element.40) | copy-start | bytes 12582916
  85.6 3.9 %collective-permute-start.18 = (bf16[24,2,128,128]{3,2,1,0:T(8,128)(2,1)}, bf16[24,2,128,128]{3,2,1,0:T(8,128)(2,1)S(1)}, u32[]{:S(2)}, u32[]{:S(2)}) collective-permute-start(bf16[24,2,128,128]{3,2,1,0:T(8,128)(2,1)} %get-tuple-element.41), channel_id=1, source_target_pairs={{0,16},{16,0},{32,48},{48,32},{64,80},{80,64},{96,112},{112,96},{1... | collective-permute-start | bytes 4718600 | tf_op jit(solution)/shard_map/ppermute | solution.py:286
  91.5 18.7 %collective-permute-start.22 = (bf16[40,2,128,128]{3,2,1,0:T(8,128)(2,1)}, bf16[40,2,128,128]{3,2,1,0:T(8,128)(2,1)S(1)}, u32[]{:S(2)}, u32[]{:S(2)}) collective-permute-start(bf16[40,2,128,128]{3,2,1,0:T(8,128)(2,1)} %get-tuple-element.46), channel_id=1, source_target_pairs={{0,16},{16,0},{32,48},{48,32},{64,80},{80,64},{96,112},{112,96},{1... | collective-permute-start | bytes 7864328 | tf_op jit(solution)/shard_map/ppermute | solution.py:298
  91.7 15.7 %collective-permute-start.19 = (bf16[8,2,128,128]{3,2,1,0:T(8,128)(2,1)S(1)}, bf16[8,2,128,128]{3,2,1,0:T(8,128)(2,1)S(1)}, u32[]{:S(2)}, u32[]{:S(2)}) collective-permute-start(bf16[8,2,128,128]{3,2,1,0:T(8,128)(2,1)S(1)} %get-tuple-element.43), channel_id=1, source_target_pairs={{0,32},{16,48},{32,0},{48,16},{64,96},{80,112},{96,64},{112,80},{1... | collective-permute-start | bytes 1572872 | tf_op jit(solution)/shard_map/ppermute | solution.py:295
  94.7 13.9 %collective-permute-start.20 = (bf16[8,2,128,128]{3,2,1,0:T(8,128)(2,1)S(1)}, bf16[8,2,128,128]{3,2,1,0:T(8,128)(2,1)S(1)}, u32[]{:S(2)}, u32[]{:S(2)}) collective-permute-start(bf16[8,2,128,128]{3,2,1,0:T(8,128)(2,1)S(1)} %get-tuple-element.44), channel_id=1, source_target_pairs={{0,64},{16,80},{32,96},{48,112},{64,128},{80,144},{96,160},{112,17... | collective-permute-start | bytes 1572872 | tf_op jit(solution)/shard_map/ppermute | solution.py:296
  95.3 14.8 %collective-permute-start.21 = (bf16[8,2,128,128]{3,2,1,0:T(8,128)(2,1)S(1)}, bf16[8,2,128,128]{3,2,1,0:T(8,128)(2,1)S(1)}, u32[]{:S(2)}, u32[]{:S(2)}) collective-permute-start(bf16[8,2,128,128]{3,2,1,0:T(8,128)(2,1)S(1)} %get-tuple-element.45), channel_id=1, source_target_pairs={{0,192},{16,208},{32,224},{48,240},{64,0},{80,16},{96,32},{112,48}... | collective-permute-start | bytes 1572872 | tf_op jit(solution)/shard_map/ppermute | solution.py:297
  111.5 7.3 %collective-permute-start.23 = (bf16[4,2,128,128]{3,2,1,0:T(8,128)(2,1)S(1)}, bf16[4,2,128,128]{3,2,1,0:T(8,128)(2,1)S(1)}, u32[]{:S(2)}, u32[]{:S(2)}) collective-permute-start(bf16[4,2,128,128]{3,2,1,0:T(8,128)(2,1)S(1)} %get-tuple-element.51), channel_id=1, source_target_pairs={{0,64},{16,80},{32,96},{48,112},{64,128},{80,144},{96,160},{112,17... | collective-permute-start | bytes 786440 | tf_op jit(solution)/shard_map/ppermute | solution.py:306
  111.9 8.5 %collective-permute-start.24 = (bf16[4,2,128,128]{3,2,1,0:T(8,128)(2,1)S(1)}, bf16[4,2,128,128]{3,2,1,0:T(8,128)(2,1)S(1)}, u32[]{:S(2)}, u32[]{:S(2)}) collective-permute-start(bf16[4,2,128,128]{3,2,1,0:T(8,128)(2,1)S(1)} %get-tuple-element.52), channel_id=1, source_target_pairs={{0,192},{16,208},{32,224},{48,240},{64,0},{80,16},{96,32},{112,48}... | collective-permute-start | bytes 786440 | tf_op jit(solution)/shard_map/ppermute | solution.py:307
  113.6 14.0 %collective-permute-start.27 = (bf16[8,2,128,128]{3,2,1,0:T(8,128)(2,1)}, bf16[8,2,128,128]{3,2,1,0:T(8,128)(2,1)S(1)}, u32[]{:S(2)}, u32[]{:S(2)}) collective-permute-start(bf16[8,2,128,128]{3,2,1,0:T(8,128)(2,1)} %get-tuple-element.58), channel_id=1, source_target_pairs={{0,32},{16,48},{32,0},{48,16},{64,96},{80,112},{96,64},{112,80},{1... | collective-permute-start | bytes 1572872 | tf_op jit(solution)/shard_map/ppermute | solution.py:305
  121.8 12.4 %collective-permute-start.25 = (bf16[8,2,128,128]{3,2,1,0:T(8,128)(2,1)}, bf16[8,2,128,128]{3,2,1,0:T(8,128)(2,1)}, u32[]{:S(2)}, u32[]{:S(2)}) collective-permute-start(bf16[8,2,128,128]{3,2,1,0:T(8,128)(2,1)} %get-tuple-element.56), channel_id=1, source_target_pairs={{0,64},{16,80},{32,96},{48,112},{64,128},{80,144},{96,160},{112,17... | collective-permute-start | bytes 1572872 | tf_op jit(solution)/shard_map/ppermute | solution.py:313
  122.1 13.6 %collective-permute-start.26 = (bf16[8,2,128,128]{3,2,1,0:T(8,128)(2,1)}, bf16[8,2,128,128]{3,2,1,0:T(8,128)(2,1)}, u32[]{:S(2)}, u32[]{:S(2)}) collective-permute-start(bf16[8,2,128,128]{3,2,1,0:T(8,128)(2,1)} %get-tuple-element.57), channel_id=1, source_target_pairs={{0,192},{16,208},{32,224},{48,240},{64,0},{80,16},{96,32},{112,48}... | collective-permute-start | bytes 1572872 | tf_op jit(solution)/shard_map/ppermute | solution.py:314
  135.7 6.2 %copy-start.1 = (f32[1,2,16,4096]{3,2,1,0:T(8,128)S(1)}, f32[1,2,16,4096]{3,2,1,0:T(8,128)}, u32[]{:S(2)}) copy-start(f32[1,2,16,4096]{3,2,1,0:T(8,128)} %reduce-scatter.2.cloned.1.call-done) | copy-start | bytes 1572868
  136.8 5.1 %collective-permute-start.17 = (bf16[16,4096]{1,0:T(8,128)(2,1)S(1)}, bf16[16,4096]{1,0:T(8,128)(2,1)S(1)}, u32[]{:S(2)}, u32[]{:S(2)}) collective-permute-start(bf16[16,4096]{1,0:T(8,128)(2,1)S(1)} %fusion.2), channel_id=1, source_target_pairs={{0,8},{1,9},{2,10},{3,11},{4,12},{5,13},{6,14},{7,15},{8,0},{9,1},... | collective-permute-start | bytes 393224 | tf_op jit(solution)/shard_map/ppermute | solution.py:324
Sparse Core Ops, SparseCore 0:
  14.6 44.2 all-gather.2
  75.0 57.1 reduce-scatter.1

commit v6 on v5

--- a/solution.py
+++ b/solution.py
@@ -312,16 +312,16 @@
     sends = lax.optimization_barrier((up_sum.astype(bf16), down_sum.astype(bf16)))
     up_last = lax.ppermute(sends[0], "dp", X_UP)
     down_last = lax.ppermute(sends[1], "dp", X_DOWN)
-    up_last, down_last, across_in, late_three = lax.optimization_barrier(
-        (up_last, down_last, across_in, late_two)
+    mine = jnp.where(low == 0, summed[0], summed[1])
+    theirs = jnp.where(low == 0, summed[1], summed[0]).astype(bf16)
+    back = lax.ppermute(theirs, "tensor", L_SWAP)
+    up_last, down_last, across_in, late_three, theirs = lax.optimization_barrier(
+        (up_last, down_last, across_in, late_two, theirs)
     )
     total = block(0, 0, late_three) + across_in.astype(f32)
     total = total + up_last.astype(f32) + down_last.astype(f32)
     tile_grads = (total * (1.0 / (XS * YS * CS)))[None]
 
-    mine = jnp.where(low == 0, summed[0], summed[1])
-    theirs = jnp.where(low == 0, summed[1], summed[0])
-    back = lax.ppermute(theirs.astype(bf16), "tensor", L_SWAP)
     grad_tokens = (mine + back.astype(f32)).astype(bf16)
     return hidden, grad_tokens, tile_grads
 

time: 150 us -> 150 us (level)
  waiting for transfers between devices: 65.8 us -> 62.2 us
  other arithmetic: 14.5 us -> 16.4 us
    reduce_scatter x1, waiting for transfers between devices: 0.01 us -> 4.61 us  [body(): lax.psum_scatter(rows, 'tensor', scatter_dimension=0, axis_index_groups=Z...]
    ppermute x1, waiting for transfers between devices: 3.79 us -> 0.01 us  [body(): across_in = lax.ppermute(sends[0], 'dp', Y_SWAP)]
    ppermute x1, waiting for transfers between devices: 6.58 us -> 2.95 us  [body(): up_last = lax.ppermute(sends[0], 'dp', X_UP)]
  transfers between devices with their start and end apart: 30 -> 30, of which waited for: 20 -> 19; matrix products, arithmetic and copies ran while one was open for 8% -> 11% of each run, Pallas kernels for 7% -> 8%
where the time goes in v6:
time: 150 us
  waiting for transfers between devices  62.2 us (41%)
  Pallas kernels  27.7 us (18%)
  starting transfers between devices  27.4 us (18%)
  other arithmetic  16.4 us (11%)
  between operations  14.3 us (10%)
  local copies, waits for them, and re-layouts  1.85 us (1%)
    pallas_call x1, Pallas kernels, dense_work(): pl.pallas_call(dense_kernel, out_shape=(jax.ShapeDtypeStruct((GROUP, HIDE...  16 us
    pallas_call x1, Pallas kernels, tile_work(): pl.pallas_call(tile_kernel, out_shape=tuple((jax.ShapeDtypeStruct((n, 2,...  11.7 us
    ppermute x1, waiting for transfers between devices, body(): far_in = lax.ppermute(sends[0], 'dp', Y_SWAP)  10.7 us
    ppermute x1, waiting for transfers between devices, body(): far_across = lax.ppermute(far, 'dp', Y_SWAP)  8.4 us
    ppermute x1, waiting for transfers between devices, body(): below = lax.ppermute(own, 'dp', X_UP)  6.77 us
    ppermute x1, waiting for transfers between devices, body(): half_up = lax.ppermute(sends[1], 'dp', X_UP)  4.92 us
    reduce_scatter x1, waiting for transfers between devices, body(): lax.psum_scatter(rows, 'tensor', scatter_dimension=0, axis_index_groups=Z...  4.61 us
    ppermute x1, waiting for transfers between devices, body(): far_low = lax.ppermute(below[:half], 'dp', X_UP)  3.96 us
  transfers between devices with their start and end apart: 30, of which 19 were waited for; matrix products, arithmetic and copies ran while one was open for 11% of the time, Pallas kernels for 8%

profile of v6, /device:TPU:6, one launch (start us, length us, event | category | flops | bytes accessed | tf_op | source)
XLA Modules:
  0.0 149.8 jit_solution(1306574460958931532)
XLA Ops:
  7.2 1.7 %collective-permute-start.16 = (bf16[16,4096]{1,0:T(8,128)(2,1)}, bf16[16,4096]{1,0:T(8,128)(2,1)S(1)}, u32[]{:S(2)}, u32[]{:S(2)}) collective-permute-start(bf16[16,4096]{1,0:T(8,128)(2,1)} %param.7), channel_id=1, source_target_pairs={{0,8},{1,9},{2,10},{3,11},{4,12},{5,13},{6,14},{7,15},{8,0},{9,1},... | collective-permute-start | bytes 393224 | tf_op jit(solution)/shard_map/ppermute | solution.py:262
  8.9 3.9 %collective-permute-done.16 = bf16[16,4096]{1,0:T(8,128)(2,1)S(1)} collective-permute-done((bf16[16,4096]{1,0:T(8,128)(2,1)}, bf16[16,4096]{1,0:T(8,128)(2,1)S(1)}, u32[]{:S(2)}, u32[]{:S(2)}) %collective-permute-start.16) | collective-permute-done | bytes 131104 | tf_op jit(solution)/shard_map/ppermute | solution.py:262
  12.8 1.6 %pad_maximum_fusion = bf16[2,16,4096]{2,1,0:T(8,128)(2,1)} fusion(bf16[1,16,4096]{2,1,0:T(8,128)(2,1)S(1)} %bitcast.14, bf16[1,16,4096]{2,1,0:T(8,128)(2,1)} %bitcast.13), kind=kLoop, calls=%fused_computation.9 | loop fusion | flops 131072 | bytes 524288 | tf_op jit(solution)/shard_map/stack | solution.py:267
  14.5 2.0 %collective-permute-start = (bf16[8,2,128,128]{3,2,1,0:T(8,128)(2,1)}, bf16[8,2,128,128]{3,2,1,0:T(8,128)(2,1)S(1)}, u32[]{:S(2)}, u32[]{:S(2)}) collective-permute-start(bf16[8,2,128,128]{3,2,1,0:T(8,128)(2,1)} %bitcast.17), channel_id=1, source_target_pairs={{0,64},{16,80},{32,96},{48,112},{64,128},{80,144},{96,160},{112,17... | collective-permute-start | bytes 1572872 | tf_op jit(solution)/shard_map/ppermute | solution.py:264
  16.6 3.2 %collective-permute-start.2 = (bf16[8,2,128,128]{3,2,1,0:T(8,128)(2,1)}, bf16[8,2,128,128]{3,2,1,0:T(8,128)(2,1)S(1)}, u32[]{:S(2)}, u32[]{:S(2)}) collective-permute-start(bf16[8,2,128,128]{3,2,1,0:T(8,128)(2,1)} %bitcast.19), channel_id=1, source_target_pairs={{0,32},{16,48},{32,0},{48,16},{64,96},{80,112},{96,64},{112,80},{1... | collective-permute-start | bytes 1572872 | tf_op jit(solution)/shard_map/ppermute | solution.py:266
  19.8 0.8 copy.13
  20.8 6.8 %collective-permute-done.refs_4_ = bf16[8,2,128,128]{3,2,1,0:T(8,128)(2,1)S(1)} collective-permute-done((bf16[8,2,128,128]{3,2,1,0:T(8,128)(2,1)}, bf16[8,2,128,128]{3,2,1,0:T(8,128)(2,1)S(1)}, u32[]{:S(2)}, u32[]{:S(2)}) %collective-permute-start) | collective-permute-done | bytes 524320 | tf_op jit(solution)/shard_map/ppermute | solution.py:264
  27.6 1.6 %collective-permute-start.3 = (bf16[4,2,128,128]{3,2,1,0:T(8,128)(2,1)S(1)}, bf16[4,2,128,128]{3,2,1,0:T(8,128)(2,1)S(1)}, u32[]{:S(2)}, u32[]{:S(2)}) collective-permute-start(bf16[4,2,128,128]{3,2,1,0:T(8,128)(2,1)S(1)} %slice.94), channel_id=1, source_target_pairs={{0,64},{16,80},{32,96},{48,112},{64,128},{80,144},{96,160},{112,17... | collective-permute-start | bytes 786440 | tf_op jit(solution)/shard_map/ppermute | solution.py:272
  29.4 0.6 collective-permute-start.4
  30.6 2.4 %collective-permute-start.5 = (bf16[8,2,128,128]{3,2,1,0:T(8,128)(2,1)S(1)}, bf16[8,2,128,128]{3,2,1,0:T(8,128)(2,1)}, u32[]{:S(2)}, u32[]{:S(2)}) collective-permute-start(bf16[8,2,128,128]{3,2,1,0:T(8,128)(2,1)S(1)} %collective-permute-done.2.refs_6_), channel_id=1, source_target_pairs={{0,64},{16,80},{32,96},{48,112},{64,128},{80,144},{96,160},{112,17... | collective-permute-start | bytes 1572872 | tf_op jit(solution)/shard_map/ppermute | solution.py:275
  33.0 4.0 %collective-permute-done.3 = bf16[4,2,128,128]{3,2,1,0:T(8,128)(2,1)S(1)} collective-permute-done((bf16[4,2,128,128]{3,2,1,0:T(8,128)(2,1)S(1)}, bf16[4,2,128,128]{3,2,1,0:T(8,128)(2,1)S(1)}, u32[]{:S(2)}, u32[]{:S(2)}) %collective-permute-start.3) | collective-permute-done | bytes 262176 | tf_op jit(solution)/shard_map/ppermute | solution.py:272
  37.0 2.9 %collective-permute-done.4 = bf16[4,2,128,128]{3,2,1,0:T(8,128)(2,1)S(1)} collective-permute-done((bf16[4,2,128,128]{3,2,1,0:T(8,128)(2,1)S(1)}, bf16[4,2,128,128]{3,2,1,0:T(8,128)(2,1)S(1)}, u32[]{:S(2)}, u32[]{:S(2)}) %collective-permute-start.4) | collective-permute-done | bytes 262176 | tf_op jit(solution)/shard_map/ppermute | solution.py:273
  39.9 3.4 %collective-permute-start.7 = (bf16[8,2,128,128]{3,2,1,0:T(8,128)(2,1)S(1)}, bf16[8,2,128,128]{3,2,1,0:T(8,128)(2,1)S(1)}, u32[]{:S(2)}, u32[]{:S(2)}) collective-permute-start(bf16[8,2,128,128]{3,2,1,0:T(8,128)(2,1)S(1)} %constant_dynamic-update-slice_fusion.refs_7_), channel_id=1, source_target_pairs={{0,32},{16,48},{32,0},{48,16},{64,96},{80,112},{96,64},{112,80},{1... | collective-permute-start | bytes 1572872 | tf_op jit(solution)/shard_map/ppermute | solution.py:277
  43.4 0.6 fusion.6
  44.2 0.6 compare_select_fusion.ready
  44.8 0.5 collective-permute-done.5.refs_8_
  45.3 1.7 %collective-permute-done.6.refs_9_ = bf16[8,2,128,128]{3,2,1,0:T(8,128)(2,1)} collective-permute-done((bf16[8,2,128,128]{3,2,1,0:T(8,128)(2,1)S(1)}, bf16[8,2,128,128]{3,2,1,0:T(8,128)(2,1)}, u32[]{:S(2)}, u32[]{:S(2)}) %collective-permute-start.6) | collective-permute-done | bytes 524320 | tf_op jit(solution)/shard_map/ppermute | solution.py:276
  46.9 0.5 collective-permute-start.13
  47.6 8.4 %collective-permute-done.7.refs_10_ = bf16[8,2,128,128]{3,2,1,0:T(8,128)(2,1)S(1)} collective-permute-done((bf16[8,2,128,128]{3,2,1,0:T(8,128)(2,1)S(1)}, bf16[8,2,128,128]{3,2,1,0:T(8,128)(2,1)S(1)}, u32[]{:S(2)}, u32[]{:S(2)}) %collective-permute-start.7) | collective-permute-done | bytes 524320 | tf_op jit(solution)/shard_map/ppermute | solution.py:277
  56.0 0.6 fusion.16.spots
  56.6 0.6 broadcast_add_fusion.1.refs_0_
  57.2 0.5 xor_add_fusion.refs_1_
  58.0 0.8 all-gather.3.cloned.1.call-done
  58.9 16.0 %forward_and_rows.1 = (bf16[256,896]{1,0:T(8,128)(2,1)}, bf16[7,256,256]{2,1,0:T(8,128)(2,1)}, f32[8,2,16,4096]{3,2,1,0:T(8,128)}) custom-call(s32[2,128]{1,0:T(2,128)} %broadcast_add_fusion.1.refs_0_, s32[16]{0:T(128)} %xor_add_fusion.refs_1_, s32[1]{0:T(128)} %bitcast.refs_2_.low, bf16[8,2,128,128]{3,2,1,0:T(8,128)(2,1)} %bitcast.21, ...), custom_call_target="tpu_custom_call" | custom-call | flops 7516192768 | bytes 16777216 | tf_op jit(solution)/shard_map/forward_and_rows/pallas_call | solution.py:128
  74.9 11.7 %tile_sums.1 = (bf16[24,2,128,128]{3,2,1,0:T(8,128)(2,1)}, bf16[40,2,128,128]{3,2,1,0:T(8,128)(2,1)}, bf16[64,2,128,128]{3,2,1,0:T(8,128)(2,1)}) custom-call(s32[2,224]{1,0:T(2,128)} %get-tuple-element.36.target, s32[8]{0:T(128)} %compare_select_fusion.ready, s32[16]{0:T(128)} %fusion.16.spots, s32[1]{0:T(128)} %bitcast.refs_2_.low, ...), custom_call_target="tpu_custom_call" | custom-call | flops 3758096384 | bytes 12582912 | tf_op jit(solution)/shard_map/tile_sums/pallas_call | solution.py:199
  87.0 3.6 %collective-permute-done.18 = bf16[24,2,128,128]{3,2,1,0:T(8,128)(2,1)S(1)} collective-permute-done((bf16[24,2,128,128]{3,2,1,0:T(8,128)(2,1)}, bf16[24,2,128,128]{3,2,1,0:T(8,128)(2,1)S(1)}, u32[]{:S(2)}, u32[]{:S(2)}) %collective-permute-start.18) | collective-permute-done | bytes 1572896 | tf_op jit(solution)/shard_map/ppermute | solution.py:286
  90.6 1.9 %add_convert_fusion.4 = (bf16[8,2,128,128]{3,2,1,0:T(8,128)(2,1)S(1)}, bf16[8,2,128,128]{3,2,1,0:T(8,128)(2,1)S(1)}, bf16[8,2,128,128]{3,2,1,0:T(8,128)(2,1)S(1)}) fusion(bf16[24,2,128,128]{3,2,1,0:T(8,128)(2,1)S(1)} %collective-permute-done.18, bf16[64,2,128,128]{3,2,1,0:T(8,128)(2,1)} %get-tuple-element.40), kind=kLoop, calls=%fused_computation.5 | loop fusion | flops 3145728 | bytes 4718592 | tf_op jit(solution)/shard_map/convert_element_type | solution.py:293
  92.8 3.0 %collective-permute-start.19 = (bf16[8,2,128,128]{3,2,1,0:T(8,128)(2,1)S(1)}, bf16[8,2,128,128]{3,2,1,0:T(8,128)(2,1)S(1)}, u32[]{:S(2)}, u32[]{:S(2)}) collective-permute-start(bf16[8,2,128,128]{3,2,1,0:T(8,128)(2,1)S(1)} %get-tuple-element.43), channel_id=1, source_target_pairs={{0,32},{16,48},{32,0},{48,16},{64,96},{80,112},{96,64},{112,80},{1... | collective-permute-start | bytes 1572872 | tf_op jit(solution)/shard_map/ppermute | solution.py:295
  95.8 0.5 collective-permute-start.20
  96.3 1.5 collective-permute-start.21
  97.8 10.7 %collective-permute-done.19 = bf16[8,2,128,128]{3,2,1,0:T(8,128)(2,1)S(1)} collective-permute-done((bf16[8,2,128,128]{3,2,1,0:T(8,128)(2,1)S(1)}, bf16[8,2,128,128]{3,2,1,0:T(8,128)(2,1)S(1)}, u32[]{:S(2)}, u32[]{:S(2)}) %collective-permute-start.19) | collective-permute-done | bytes 524320 | tf_op jit(solution)/shard_map/ppermute | solution.py:295
  108.5 1.2 collective-permute-done.20
  109.7 1.5 collective-permute-done.21
  111.2 1.8 %add_convert_fusion.2 = (bf16[8,2,128,128]{3,2,1,0:T(8,128)(2,1)S(1)}, bf16[8,2,128,128]{3,2,1,0:T(8,128)(2,1)S(1)}) fusion(bf16[8,2,128,128]{3,2,1,0:T(8,128)(2,1)S(1)} %collective-permute-done.19, bf16[40,2,128,128]{3,2,1,0:T(8,128)(2,1)S(1)} %collective-permute-done.22, bf16[64,2,128,128]{3,2,1,0:T(8,128)(2,1)} %get-tuple-element.40, ...), kind=kLoop, calls=%fused_computation.3 | loop fusion | flops 3670016 | bytes 4718592 | tf_op jit(solution)/shard_map/convert.1
  113.0 0.8 fusion.18
  114.1 1.7 %collective-permute-start.24 = (bf16[4,2,128,128]{3,2,1,0:T(8,128)(2,1)}, bf16[4,2,128,128]{3,2,1,0:T(8,128)(2,1)}, u32[]{:S(2)}, u32[]{:S(2)}) collective-permute-start(bf16[4,2,128,128]{3,2,1,0:T(8,128)(2,1)} %get-tuple-element.52), channel_id=1, source_target_pairs={{0,192},{16,208},{32,224},{48,240},{64,0},{80,16},{96,32},{112,48}... | collective-permute-start | bytes 786440 | tf_op jit(solution)/shard_map/ppermute | solution.py:307
  115.8 0.5 collective-permute-start.27
  116.3 4.9 %collective-permute-done.23 = bf16[4,2,128,128]{3,2,1,0:T(8,128)(2,1)S(1)} collective-permute-done((bf16[4,2,128,128]{3,2,1,0:T(8,128)(2,1)}, bf16[4,2,128,128]{3,2,1,0:T(8,128)(2,1)S(1)}, u32[]{:S(2)}, u32[]{:S(2)}) %collective-permute-start.23) | collective-permute-done | bytes 262176 | tf_op jit(solution)/shard_map/ppermute | solution.py:306
  121.2 1.6 %collective-permute-done.24 = bf16[4,2,128,128]{3,2,1,0:T(8,128)(2,1)} collective-permute-done((bf16[4,2,128,128]{3,2,1,0:T(8,128)(2,1)}, bf16[4,2,128,128]{3,2,1,0:T(8,128)(2,1)}, u32[]{:S(2)}, u32[]{:S(2)}) %collective-permute-start.24) | collective-permute-done | bytes 262176 | tf_op jit(solution)/shard_map/ppermute | solution.py:307
  122.9 2.7 %add_convert_fusion = (bf16[8,2,128,128]{3,2,1,0:T(8,128)(2,1)}, bf16[8,2,128,128]{3,2,1,0:T(8,128)(2,1)}) fusion(bf16[4,2,128,128]{3,2,1,0:T(8,128)(2,1)} %collective-permute-done.24, bf16[40,2,128,128]{3,2,1,0:T(8,128)(2,1)S(1)} %collective-permute-done.22, bf16[64,2,128,128]{3,2,1,0:T(8,128)(2,1)} %get-tuple-element.40, ...), kind=kLoop, calls=%fused_computation.1 | loop fusion | flops 3145728 | bytes 3670016 | tf_op jit(solution)/shard_map/convert_element_type | solution.py:312
  125.8 1.8 %collective-permute-start.26 = (bf16[8,2,128,128]{3,2,1,0:T(8,128)(2,1)}, bf16[8,2,128,128]{3,2,1,0:T(8,128)(2,1)}, u32[]{:S(2)}, u32[]{:S(2)}) collective-permute-start(bf16[8,2,128,128]{3,2,1,0:T(8,128)(2,1)} %get-tuple-element.57), channel_id=1, source_target_pairs={{0,192},{16,208},{32,224},{48,240},{64,0},{80,16},{96,32},{112,48}... | collective-permute-start | bytes 1572872 | tf_op jit(solution)/shard_map/ppermute | solution.py:314
  127.6 4.6 %reduce-scatter.2.cloned.1.call-done = f32[1,2,16,4096]{3,2,1,0:T(8,128)} async-done(((f32[8,2,16,4096]{3,2,1,0:T(8,128)}), f32[1,2,16,4096]{3,2,1,0:T(8,128)}) %reduce-scatter.2.cloned.1.call-update) | async-done | bytes 524304 | tf_op jit(solution)/shard_map/reduce_scatter | solution.py:283
  132.2 1.1 fusion.2
  133.3 1.6 %collective-permute-start.17 = (bf16[16,4096]{1,0:T(8,128)(2,1)S(1)}, bf16[16,4096]{1,0:T(8,128)(2,1)S(1)}, u32[]{:S(2)}, u32[]{:S(2)}) collective-permute-start(bf16[16,4096]{1,0:T(8,128)(2,1)S(1)} %fusion.2), channel_id=1, source_target_pairs={{0,8},{1,9},{2,10},{3,11},{4,12},{5,13},{6,14},{7,15},{8,0},{9,1},... | collective-permute-start | bytes 393224 | tf_op jit(solution)/shard_map/ppermute | solution.py:317
  134.9 2.9 %collective-permute-done.25 = bf16[8,2,128,128]{3,2,1,0:T(8,128)(2,1)} collective-permute-done((bf16[8,2,128,128]{3,2,1,0:T(8,128)(2,1)}, bf16[8,2,128,128]{3,2,1,0:T(8,128)(2,1)}, u32[]{:S(2)}, u32[]{:S(2)}) %collective-permute-start.25) | collective-permute-done | bytes 524320 | tf_op jit(solution)/shard_map/ppermute | solution.py:313
  137.9 1.5 collective-permute-done.26
  139.4 2.9 %multiply_bitcast_fusion = f32[1,8,2,128,128]{4,3,2,1,0:T(8,128)} fusion(bf16[8,2,128,128]{3,2,1,0:T(8,128)(2,1)} %collective-permute-done.26, bf16[8,2,128,128]{3,2,1,0:T(8,128)(2,1)} %collective-permute-done.25, bf16[8,2,128,128]{3,2,1,0:T(8,128)(2,1)} %collective-permute-done.27, bf16[40,2,128,128]{3,2,1,0:T(8,128)(2,1)S(1)} %collective-permute-done.22, ...), kind=kLoop, calls=%fused_computation | loop fusion | flops 2621440 | bytes 3670016 | tf_op jit(solution)/shard_map/broadcast_in_dim | solution.py:323
  142.3 0.7 fusion
  (67 shorter events, 2.9 us)
Async XLA Ops:
  7.2 50.0 %copy-start.4 = (s32[16]{0:T(128)S(1)}, s32[16]{0:T(128)}, u32[]{:S(2)}) copy-start(s32[16]{0:T(128)} %constant.23.clone) | copy-start | bytes 196
  7.2 50.0 %copy-start.5 = (s32[16]{0:T(128)S(1)}, s32[16]{0:T(128)}, u32[]{:S(2)}) copy-start(s32[16]{0:T(128)} %constant.22.clone) | copy-start | bytes 196
  7.2 50.0 %copy-start.6 = (s32[16]{0:T(128)S(1)}, s32[16]{0:T(128)}, u32[]{:S(2)}) copy-start(s32[16]{0:T(128)} %constant.21.clone) | copy-start | bytes 196
  7.2 51.6 %all-gather.3.cloned.1.call-start = ((), (), s32[]{:S(2)}) async-start(), calls=%async_computation.2 | async-start | bytes 2359296 | tf_op jit(solution)/shard_map/all_gather | solution.py:268
  7.2 5.5 %collective-permute-start.16 = (bf16[16,4096]{1,0:T(8,128)(2,1)}, bf16[16,4096]{1,0:T(8,128)(2,1)S(1)}, u32[]{:S(2)}, u32[]{:S(2)}) collective-permute-start(bf16[16,4096]{1,0:T(8,128)(2,1)} %param.7), channel_id=1, source_target_pairs={{0,8},{1,9},{2,10},{3,11},{4,12},{5,13},{6,14},{7,15},{8,0},{9,1},... | collective-permute-start | bytes 393224 | tf_op jit(solution)/shard_map/ppermute | solution.py:262
  14.4 117.8 %reduce-scatter.2.cloned.1.call-start = ((), (), s32[]{:S(2)}) async-start(), calls=%async_computation.1 | async-start | bytes 4718592 | tf_op jit(solution)/shard_map/reduce_scatter | solution.py:283
  14.5 13.1 %collective-permute-start = (bf16[8,2,128,128]{3,2,1,0:T(8,128)(2,1)}, bf16[8,2,128,128]{3,2,1,0:T(8,128)(2,1)S(1)}, u32[]{:S(2)}, u32[]{:S(2)}) collective-permute-start(bf16[8,2,128,128]{3,2,1,0:T(8,128)(2,1)} %bitcast.17), channel_id=1, source_target_pairs={{0,64},{16,80},{32,96},{48,112},{64,128},{80,144},{96,160},{112,17... | collective-permute-start | bytes 1572872 | tf_op jit(solution)/shard_map/ppermute | solution.py:264
  16.5 12.8 %collective-permute-start.1 = (bf16[8,2,128,128]{3,2,1,0:T(8,128)(2,1)}, bf16[8,2,128,128]{3,2,1,0:T(8,128)(2,1)S(1)}, u32[]{:S(2)}, u32[]{:S(2)}) collective-permute-start(bf16[8,2,128,128]{3,2,1,0:T(8,128)(2,1)} %bitcast.18), channel_id=1, source_target_pairs={{0,192},{16,208},{32,224},{48,240},{64,0},{80,16},{96,32},{112,48}... | collective-permute-start | bytes 1572872 | tf_op jit(solution)/shard_map/ppermute | solution.py:265
  16.6 14.0 %collective-permute-start.2 = (bf16[8,2,128,128]{3,2,1,0:T(8,128)(2,1)}, bf16[8,2,128,128]{3,2,1,0:T(8,128)(2,1)S(1)}, u32[]{:S(2)}, u32[]{:S(2)}) collective-permute-start(bf16[8,2,128,128]{3,2,1,0:T(8,128)(2,1)} %bitcast.19), channel_id=1, source_target_pairs={{0,32},{16,48},{32,0},{48,16},{64,96},{80,112},{96,64},{112,80},{1... | collective-permute-start | bytes 1572872 | tf_op jit(solution)/shard_map/ppermute | solution.py:266
  19.8 20.2 %collective-permute-start.8 = (bf16[8,2,128,128]{3,2,1,0:T(8,128)(2,1)}, bf16[8,2,128,128]{3,2,1,0:T(8,128)(2,1)}, u32[]{:S(2)}, u32[]{:S(2)}) collective-permute-start(bf16[8,2,128,128]{3,2,1,0:T(8,128)(2,1)} %bitcast.20), channel_id=1, source_target_pairs={{0,16},{16,0},{32,48},{48,32},{64,80},{80,64},{96,112},{112,96},{1... | collective-permute-start | bytes 1572872 | tf_op jit(solution)/shard_map/ppermute | solution.py:279
  27.6 31.3 %copy-start.1 = (bf16[8,2,128,128]{3,2,1,0:T(8,128)(2,1)}, bf16[8,2,128,128]{3,2,1,0:T(8,128)(2,1)S(1)}, u32[]{:S(2)}) copy-start(bf16[8,2,128,128]{3,2,1,0:T(8,128)(2,1)S(1)} %collective-permute-done.refs_4_) | copy-start | bytes 1572868
  27.6 9.3 %collective-permute-start.3 = (bf16[4,2,128,128]{3,2,1,0:T(8,128)(2,1)S(1)}, bf16[4,2,128,128]{3,2,1,0:T(8,128)(2,1)S(1)}, u32[]{:S(2)}, u32[]{:S(2)}) collective-permute-start(bf16[4,2,128,128]{3,2,1,0:T(8,128)(2,1)S(1)} %slice.94), channel_id=1, source_target_pairs={{0,64},{16,80},{32,96},{48,112},{64,128},{80,144},{96,160},{112,17... | collective-permute-start | bytes 786440 | tf_op jit(solution)/shard_map/ppermute | solution.py:272
  29.3 29.5 %copy-start.2 = (bf16[8,2,128,128]{3,2,1,0:T(8,128)(2,1)}, bf16[8,2,128,128]{3,2,1,0:T(8,128)(2,1)S(1)}, u32[]{:S(2)}) copy-start(bf16[8,2,128,128]{3,2,1,0:T(8,128)(2,1)S(1)} %collective-permute-done.1.refs_5_) | copy-start | bytes 1572868
  29.4 10.5 %collective-permute-start.4 = (bf16[4,2,128,128]{3,2,1,0:T(8,128)(2,1)S(1)}, bf16[4,2,128,128]{3,2,1,0:T(8,128)(2,1)S(1)}, u32[]{:S(2)}, u32[]{:S(2)}) collective-permute-start(bf16[4,2,128,128]{3,2,1,0:T(8,128)(2,1)S(1)} %slice.95), channel_id=1, source_target_pairs={{0,192},{16,208},{32,224},{48,240},{64,0},{80,16},{96,32},{112,48}... | collective-permute-start | bytes 786440 | tf_op jit(solution)/shard_map/ppermute | solution.py:273
  30.6 28.3 %copy-start.8 = (bf16[8,2,128,128]{3,2,1,0:T(8,128)(2,1)}, bf16[8,2,128,128]{3,2,1,0:T(8,128)(2,1)S(1)}, u32[]{:S(2)}) copy-start(bf16[8,2,128,128]{3,2,1,0:T(8,128)(2,1)S(1)} %collective-permute-done.2.refs_6_) | copy-start | bytes 1572868
  30.6 14.7 %collective-permute-start.5 = (bf16[8,2,128,128]{3,2,1,0:T(8,128)(2,1)S(1)}, bf16[8,2,128,128]{3,2,1,0:T(8,128)(2,1)}, u32[]{:S(2)}, u32[]{:S(2)}) collective-permute-start(bf16[8,2,128,128]{3,2,1,0:T(8,128)(2,1)S(1)} %collective-permute-done.2.refs_6_), channel_id=1, source_target_pairs={{0,64},{16,80},{32,96},{48,112},{64,128},{80,144},{96,160},{112,17... | collective-permute-start | bytes 1572872 | tf_op jit(solution)/shard_map/ppermute | solution.py:275
  33.0 14.0 %collective-permute-start.6 = (bf16[8,2,128,128]{3,2,1,0:T(8,128)(2,1)S(1)}, bf16[8,2,128,128]{3,2,1,0:T(8,128)(2,1)}, u32[]{:S(2)}, u32[]{:S(2)}) collective-permute-start(bf16[8,2,128,128]{3,2,1,0:T(8,128)(2,1)S(1)} %collective-permute-done.2.refs_6_), channel_id=1, source_target_pairs={{0,192},{16,208},{32,224},{48,240},{64,0},{80,16},{96,32},{112,48}... | collective-permute-start | bytes 1572872 | tf_op jit(solution)/shard_map/ppermute | solution.py:276
  36.9 10.0 %collective-permute-start.9 = (bf16[8,2,128,128]{3,2,1,0:T(8,128)(2,1)S(1)}, bf16[8,2,128,128]{3,2,1,0:T(8,128)(2,1)S(1)}, u32[]{:S(2)}, u32[]{:S(2)}) collective-permute-start(bf16[8,2,128,128]{3,2,1,0:T(8,128)(2,1)S(1)} %collective-permute-done.refs_4_), channel_id=1, source_target_pairs={{0,16},{16,0},{32,48},{48,32},{64,80},{80,64},{96,112},{112,96},{1... | collective-permute-start | bytes 1572872 | tf_op jit(solution)/shard_map/ppermute | solution.py:279
  39.9 7.6 %collective-permute-start.10 = (bf16[8,2,128,128]{3,2,1,0:T(8,128)(2,1)S(1)}, bf16[8,2,128,128]{3,2,1,0:T(8,128)(2,1)S(1)}, u32[]{:S(2)}, u32[]{:S(2)}) collective-permute-start(bf16[8,2,128,128]{3,2,1,0:T(8,128)(2,1)S(1)} %collective-permute-done.1.refs_5_), channel_id=1, source_target_pairs={{0,16},{16,0},{32,48},{48,32},{64,80},{80,64},{96,112},{112,96},{1... | collective-permute-start | bytes 1572872 | tf_op jit(solution)/shard_map/ppermute | solution.py:279
  39.9 18.9 %copy-start.3 = (bf16[8,2,128,128]{3,2,1,0:T(8,128)(2,1)}, bf16[8,2,128,128]{3,2,1,0:T(8,128)(2,1)S(1)}, u32[]{:S(2)}) copy-start(bf16[8,2,128,128]{3,2,1,0:T(8,128)(2,1)S(1)} %constant_dynamic-update-slice_fusion.refs_7_) | copy-start | bytes 1572868
  39.9 16.0 %collective-permute-start.7 = (bf16[8,2,128,128]{3,2,1,0:T(8,128)(2,1)S(1)}, bf16[8,2,128,128]{3,2,1,0:T(8,128)(2,1)S(1)}, u32[]{:S(2)}, u32[]{:S(2)}) collective-permute-start(bf16[8,2,128,128]{3,2,1,0:T(8,128)(2,1)S(1)} %constant_dynamic-update-slice_fusion.refs_7_), channel_id=1, source_target_pairs={{0,32},{16,48},{32,0},{48,16},{64,96},{80,112},{96,64},{112,80},{1... | collective-permute-start | bytes 1572872 | tf_op jit(solution)/shard_map/ppermute | solution.py:277
  45.3 12.4 %collective-permute-start.11 = (bf16[8,2,128,128]{3,2,1,0:T(8,128)(2,1)S(1)}, bf16[8,2,128,128]{3,2,1,0:T(8,128)(2,1)}, u32[]{:S(2)}, u32[]{:S(2)}) collective-permute-start(bf16[8,2,128,128]{3,2,1,0:T(8,128)(2,1)S(1)} %collective-permute-done.2.refs_6_), channel_id=1, source_target_pairs={{0,16},{16,0},{32,48},{48,32},{64,80},{80,64},{96,112},{112,96},{1... | collective-permute-start | bytes 1572872 | tf_op jit(solution)/shard_map/ppermute | solution.py:279
  46.9 10.8 %collective-permute-start.12 = (bf16[8,2,128,128]{3,2,1,0:T(8,128)(2,1)S(1)}, bf16[8,2,128,128]{3,2,1,0:T(8,128)(2,1)}, u32[]{:S(2)}, u32[]{:S(2)}) collective-permute-start(bf16[8,2,128,128]{3,2,1,0:T(8,128)(2,1)S(1)} %constant_dynamic-update-slice_fusion.refs_7_), channel_id=1, source_target_pairs={{0,16},{16,0},{32,48},{48,32},{64,80},{80,64},{96,112},{112,96},{1... | collective-permute-start | bytes 1572872 | tf_op jit(solution)/shard_map/ppermute | solution.py:279
  46.9 10.2 %copy-start.9 = (bf16[8,2,128,128]{3,2,1,0:T(8,128)(2,1)}, bf16[8,2,128,128]{3,2,1,0:T(8,128)(2,1)S(1)}, u32[]{:S(2)}) copy-start(bf16[8,2,128,128]{3,2,1,0:T(8,128)(2,1)S(1)} %collective-permute-done.9.refs_12_) | copy-start | bytes 1572868
  46.9 10.8 %collective-permute-start.13 = (bf16[8,2,128,128]{3,2,1,0:T(8,128)(2,1)}, bf16[8,2,128,128]{3,2,1,0:T(8,128)(2,1)}, u32[]{:S(2)}, u32[]{:S(2)}) collective-permute-start(bf16[8,2,128,128]{3,2,1,0:T(8,128)(2,1)} %collective-permute-done.5.refs_8_), channel_id=1, source_target_pairs={{0,16},{16,0},{32,48},{48,32},{64,80},{80,64},{96,112},{112,96},{1... | collective-permute-start | bytes 1572872 | tf_op jit(solution)/shard_map/ppermute | solution.py:279
  47.4 11.4 %copy-start.10 = (bf16[8,2,128,128]{3,2,1,0:T(8,128)(2,1)}, bf16[8,2,128,128]{3,2,1,0:T(8,128)(2,1)S(1)}, u32[]{:S(2)}) copy-start(bf16[8,2,128,128]{3,2,1,0:T(8,128)(2,1)S(1)} %collective-permute-done.10.refs_13_) | copy-start | bytes 1572868
  47.5 10.3 %collective-permute-start.14 = (bf16[8,2,128,128]{3,2,1,0:T(8,128)(2,1)}, bf16[8,2,128,128]{3,2,1,0:T(8,128)(2,1)}, u32[]{:S(2)}, u32[]{:S(2)}) collective-permute-start(bf16[8,2,128,128]{3,2,1,0:T(8,128)(2,1)} %collective-permute-done.6.refs_9_), channel_id=1, source_target_pairs={{0,16},{16,0},{32,48},{48,32},{64,80},{80,64},{96,112},{112,96},{1... | collective-permute-start | bytes 1572872 | tf_op jit(solution)/shard_map/ppermute | solution.py:279
  56.0 2.9 %copy-start.11 = (bf16[8,2,128,128]{3,2,1,0:T(8,128)(2,1)}, bf16[8,2,128,128]{3,2,1,0:T(8,128)(2,1)S(1)}, u32[]{:S(2)}) copy-start(bf16[8,2,128,128]{3,2,1,0:T(8,128)(2,1)S(1)} %collective-permute-done.7.refs_10_) | copy-start | bytes 1572868
  56.0 2.0 %collective-permute-start.15 = (bf16[8,2,128,128]{3,2,1,0:T(8,128)(2,1)S(1)}, bf16[8,2,128,128]{3,2,1,0:T(8,128)(2,1)}, u32[]{:S(2)}, u32[]{:S(2)}) collective-permute-start(bf16[8,2,128,128]{3,2,1,0:T(8,128)(2,1)S(1)} %collective-permute-done.7.refs_10_), channel_id=1, source_target_pairs={{0,16},{16,0},{32,48},{48,32},{64,80},{80,64},{96,112},{112,96},{1... | collective-permute-start | bytes 1572872 | tf_op jit(solution)/shard_map/ppermute | solution.py:279
  86.6 5.9 %copy-start.7 = (bf16[40,2,128,128]{3,2,1,0:T(8,128)(2,1)S(1)}, bf16[40,2,128,128]{3,2,1,0:T(8,128)(2,1)}, u32[]{:S(2)}) copy-start(bf16[40,2,128,128]{3,2,1,0:T(8,128)(2,1)} %get-tuple-element.46) | copy-start | bytes 7864324
  86.7 3.9 %collective-permute-start.18 = (bf16[24,2,128,128]{3,2,1,0:T(8,128)(2,1)}, bf16[24,2,128,128]{3,2,1,0:T(8,128)(2,1)S(1)}, u32[]{:S(2)}, u32[]{:S(2)}) collective-permute-start(bf16[24,2,128,128]{3,2,1,0:T(8,128)(2,1)} %get-tuple-element.41), channel_id=1, source_target_pairs={{0,16},{16,0},{32,48},{48,32},{64,80},{80,64},{96,112},{112,96},{1... | collective-permute-start | bytes 4718600 | tf_op jit(solution)/shard_map/ppermute | solution.py:286
  92.5 18.6 %collective-permute-start.22 = (bf16[40,2,128,128]{3,2,1,0:T(8,128)(2,1)S(1)}, bf16[40,2,128,128]{3,2,1,0:T(8,128)(2,1)S(1)}, u32[]{:S(2)}, u32[]{:S(2)}) collective-permute-start(bf16[40,2,128,128]{3,2,1,0:T(8,128)(2,1)S(1)} %copy-done.7), channel_id=1, source_target_pairs={{0,16},{16,0},{32,48},{48,32},{64,80},{80,64},{96,112},{112,96},{1... | collective-permute-start | bytes 7864328 | tf_op jit(solution)/shard_map/ppermute | solution.py:298
  92.8 15.7 %collective-permute-start.19 = (bf16[8,2,128,128]{3,2,1,0:T(8,128)(2,1)S(1)}, bf16[8,2,128,128]{3,2,1,0:T(8,128)(2,1)S(1)}, u32[]{:S(2)}, u32[]{:S(2)}) collective-permute-start(bf16[8,2,128,128]{3,2,1,0:T(8,128)(2,1)S(1)} %get-tuple-element.43), channel_id=1, source_target_pairs={{0,32},{16,48},{32,0},{48,16},{64,96},{80,112},{96,64},{112,80},{1... | collective-permute-start | bytes 1572872 | tf_op jit(solution)/shard_map/ppermute | solution.py:295
  95.8 13.9 %collective-permute-start.20 = (bf16[8,2,128,128]{3,2,1,0:T(8,128)(2,1)S(1)}, bf16[8,2,128,128]{3,2,1,0:T(8,128)(2,1)S(1)}, u32[]{:S(2)}, u32[]{:S(2)}) collective-permute-start(bf16[8,2,128,128]{3,2,1,0:T(8,128)(2,1)S(1)} %get-tuple-element.44), channel_id=1, source_target_pairs={{0,64},{16,80},{32,96},{48,112},{64,128},{80,144},{96,160},{112,17... | collective-permute-start | bytes 1572872 | tf_op jit(solution)/shard_map/ppermute | solution.py:296
  96.3 14.8 %collective-permute-start.21 = (bf16[8,2,128,128]{3,2,1,0:T(8,128)(2,1)S(1)}, bf16[8,2,128,128]{3,2,1,0:T(8,128)(2,1)S(1)}, u32[]{:S(2)}, u32[]{:S(2)}) collective-permute-start(bf16[8,2,128,128]{3,2,1,0:T(8,128)(2,1)S(1)} %get-tuple-element.45), channel_id=1, source_target_pairs={{0,192},{16,208},{32,224},{48,240},{64,0},{80,16},{96,32},{112,48}... | collective-permute-start | bytes 1572872 | tf_op jit(solution)/shard_map/ppermute | solution.py:297
  113.8 7.4 %collective-permute-start.23 = (bf16[4,2,128,128]{3,2,1,0:T(8,128)(2,1)}, bf16[4,2,128,128]{3,2,1,0:T(8,128)(2,1)S(1)}, u32[]{:S(2)}, u32[]{:S(2)}) collective-permute-start(bf16[4,2,128,128]{3,2,1,0:T(8,128)(2,1)} %get-tuple-element.51), channel_id=1, source_target_pairs={{0,64},{16,80},{32,96},{48,112},{64,128},{80,144},{96,160},{112,17... | collective-permute-start | bytes 786440 | tf_op jit(solution)/shard_map/ppermute | solution.py:306
  114.1 8.8 %collective-permute-start.24 = (bf16[4,2,128,128]{3,2,1,0:T(8,128)(2,1)}, bf16[4,2,128,128]{3,2,1,0:T(8,128)(2,1)}, u32[]{:S(2)}, u32[]{:S(2)}) collective-permute-start(bf16[4,2,128,128]{3,2,1,0:T(8,128)(2,1)} %get-tuple-element.52), channel_id=1, source_target_pairs={{0,192},{16,208},{32,224},{48,240},{64,0},{80,16},{96,32},{112,48}... | collective-permute-start | bytes 786440 | tf_op jit(solution)/shard_map/ppermute | solution.py:307
  115.8 19.1 %collective-permute-start.27 = (bf16[8,2,128,128]{3,2,1,0:T(8,128)(2,1)S(1)}, bf16[8,2,128,128]{3,2,1,0:T(8,128)(2,1)}, u32[]{:S(2)}, u32[]{:S(2)}) collective-permute-start(bf16[8,2,128,128]{3,2,1,0:T(8,128)(2,1)S(1)} %get-tuple-element.58), channel_id=1, source_target_pairs={{0,32},{16,48},{32,0},{48,16},{64,96},{80,112},{96,64},{112,80},{1... | collective-permute-start | bytes 1572872 | tf_op jit(solution)/shard_map/ppermute | solution.py:305
  125.6 12.3 %collective-permute-start.25 = (bf16[8,2,128,128]{3,2,1,0:T(8,128)(2,1)}, bf16[8,2,128,128]{3,2,1,0:T(8,128)(2,1)}, u32[]{:S(2)}, u32[]{:S(2)}) collective-permute-start(bf16[8,2,128,128]{3,2,1,0:T(8,128)(2,1)} %get-tuple-element.56), channel_id=1, source_target_pairs={{0,64},{16,80},{32,96},{48,112},{64,128},{80,144},{96,160},{112,17... | collective-permute-start | bytes 1572872 | tf_op jit(solution)/shard_map/ppermute | solution.py:313
  125.8 13.6 %collective-permute-start.26 = (bf16[8,2,128,128]{3,2,1,0:T(8,128)(2,1)}, bf16[8,2,128,128]{3,2,1,0:T(8,128)(2,1)}, u32[]{:S(2)}, u32[]{:S(2)}) collective-permute-start(bf16[8,2,128,128]{3,2,1,0:T(8,128)(2,1)} %get-tuple-element.57), channel_id=1, source_target_pairs={{0,192},{16,208},{32,224},{48,240},{64,0},{80,16},{96,32},{112,48}... | collective-permute-start | bytes 1572872 | tf_op jit(solution)/shard_map/ppermute | solution.py:314
  132.2 10.0 %copy-start = (f32[1,2,16,4096]{3,2,1,0:T(8,128)S(1)}, f32[1,2,16,4096]{3,2,1,0:T(8,128)}, u32[]{:S(2)}) copy-start(f32[1,2,16,4096]{3,2,1,0:T(8,128)} %reduce-scatter.2.cloned.1.call-done) | copy-start | bytes 1572868
  133.3 8.9 %collective-permute-start.17 = (bf16[16,4096]{1,0:T(8,128)(2,1)S(1)}, bf16[16,4096]{1,0:T(8,128)(2,1)S(1)}, u32[]{:S(2)}, u32[]{:S(2)}) collective-permute-start(bf16[16,4096]{1,0:T(8,128)(2,1)S(1)} %fusion.2), channel_id=1, source_target_pairs={{0,8},{1,9},{2,10},{3,11},{4,12},{5,13},{6,14},{7,15},{8,0},{9,1},... | collective-permute-start | bytes 393224 | tf_op jit(solution)/shard_map/ppermute | solution.py:317
Sparse Core Ops, SparseCore 0:
  14.6 44.2 all-gather.2
  75.0 57.1 reduce-scatter.1
